TPU v7x, 32 devices: a whole 2x2x4 slice. The times are simulated.
32 devices in a mesh: cell: 2 (over x), ap: 8 (over z, y), sc: 2 (over core).
Axes of the slice: x: 2, y: 2, z: 4, core: 2. Of those that a mesh axis runs over, the one named last changes fastest.
Arguments:
- unsmoothed_link_guesses: bfloat16 [32, 4, 2, 128, 2048], P(('cell', 'ap'), None, None, None, 'sc'), parts along dimension 0, may hold values from -24 to 24
- received: bfloat16 [32, 4, 2, 4, 2048], P(('cell', 'ap'), None, None, None, 'sc'), parts along dimension 0, may hold values from -6 to 6
- user_power: float32 [256], P('cell'), parts along dimension 0, may hold values from 0.25 to 4
- noise_power: float32 [32], P(('cell', 'ap')), parts along dimension 0, may hold values from 0.1 to 1
- ap_gain: float32 [32, 128], P(('cell', 'ap')), parts along dimension 0, may hold values from 0.5 to 4
- user_cluster: int32 [256], P('cell'), parts along dimension 0, may hold values from 0 to 15, as said below
- serving: int32 [32, 16], P('cell'), parts along dimension 0, may hold values from 0 to 1, as said below
- cluster_owner: int32 [32, 1], P('cell'), parts along dimension 0, may hold values from 0 to 7, as said below
Outputs:
- estimates: float32 [64, 8, 4, 2, 2048], P(('cell', 'ap'), None, None, None, 'sc'), parts along dimension 0
There are 2 independent parts, one for each index of `cell`. A program takes and returns all parts, laid end to end along the dimension named above; each array names one. Nothing has to cross between parts.
Inputs may be any that keep to these rules, and one draw needn't show every extreme that they name: `user_cluster`: each of the 16 clusters holds exactly 8 users. `serving`: column a belongs to index a // 2 of ap. Where a cluster is served by an index of ap, at least one of its access points serves it. Of the clusters that one index of ap serves, at most 2 have the same owner; in every draw some owner has exactly 2 of its clusters served by every index of ap. `cluster_owner`: at most 4 clusters have the same owner, and some owner has exactly 4.
All inputs are finite; a program needn't handle non-finite values.
Results may differ from a plain program's by a relative error of at most 0.017.
Values may be sent and summed in bfloat16 or wider, within the bound.
No kernel may reach another device: no remote copies, remote signals or barrier semaphores. Data moves between devices by JAX's collectives and lax.ppermute only.
A program may use at most 128 MiB of HBM per device.

v0:
```python
import math

import jax
import jax.numpy as jnp
from jax import lax
from jax.sharding import PartitionSpec as P

TONE_NUMBER = 2048
TAPS = 64
CU = 8
OWN_MAX = 4


def complex_times(left_factor, right_factor):
    return (
        left_factor[0] * right_factor[0] - left_factor[1] * right_factor[1],
        left_factor[0] * right_factor[1] + left_factor[1] * right_factor[0],
    )


def times_conj(left_factor, right_factor):
    return (
        left_factor[0] * right_factor[0] + left_factor[1] * right_factor[1],
        left_factor[1] * right_factor[0] - left_factor[0] * right_factor[1],
    )


def hermitian_solve(cov_re, cov_im, right_re, right_im):
    dimension = len(cov_re)
    factor = {}
    pivots = []
    for j in range(dimension):
        pivot_root = cov_re[j][j]
        for k in range(j):
            element = factor[j, k]
            pivot_root = pivot_root - (element[0] * element[0] + element[1] * element[1])
        pivot_root = jnp.sqrt(pivot_root)
        pivots.append(pivot_root)
        for i in range(j + 1, dimension):
            running = (cov_re[i][j], cov_im[i][j])
            for k in range(j):
                product = times_conj(factor[i, k], factor[j, k])
                running = (running[0] - product[0], running[1] - product[1])
            factor[i, j] = (running[0] / pivot_root, running[1] / pivot_root)
    forward = []
    for i in range(dimension):
        running = (right_re[i], right_im[i])
        for k in range(i):
            product = complex_times(factor[i, k], forward[k])
            running = (running[0] - product[0], running[1] - product[1])
        forward.append((running[0] / pivots[i], running[1] / pivots[i]))
    result = [None] * dimension
    for i in range(dimension - 1, -1, -1):
        running = forward[i]
        for k in range(i + 1, dimension):
            product = times_conj(result[k], factor[k, i])
            running = (running[0] - product[0], running[1] - product[1])
        result[i] = (running[0] / pivots[i], running[1] / pivots[i])
    return result


def tone_angles(lowest_tone, tone_quantity, tones_first):
    if tones_first:
        tone_values = lowest_tone + lax.broadcasted_iota(jnp.int32, (tone_quantity, TAPS), 0)
        lag_values = lax.broadcasted_iota(jnp.int32, (tone_quantity, TAPS), 1)
    else:
        tone_values = lowest_tone + lax.broadcasted_iota(jnp.int32, (TAPS, tone_quantity), 1)
        lag_values = lax.broadcasted_iota(jnp.int32, (TAPS, tone_quantity), 0)
    rotation = tone_values * lag_values % TONE_NUMBER
    return rotation.astype(jnp.float32) * (2.0 * math.pi / TONE_NUMBER)


def forward_table(lowest_tone, tone_quantity):
    angles = tone_angles(lowest_tone, tone_quantity, True)
    return jnp.concatenate([jnp.cos(angles), jnp.sin(angles)], axis=1).astype(jnp.bfloat16)


def rebuild_tables(lowest_tone, tone_quantity):
    angles = tone_angles(lowest_tone, tone_quantity, False)
    cosine = jnp.cos(angles).astype(jnp.bfloat16)
    sine = jnp.sin(angles).astype(jnp.bfloat16)
    return (jnp.concatenate([cosine, sine], axis=0), jnp.concatenate([-sine, cosine], axis=0))


def rotate_matrix():
    rows = lax.broadcasted_iota(jnp.int32, (2 * TAPS, 2 * TAPS), 0)
    cols = lax.broadcasted_iota(jnp.int32, (2 * TAPS, 2 * TAPS), 1)
    lower = jnp.where((cols < TAPS) & (rows == cols + TAPS), -1.0, 0.0)
    upper = jnp.where((cols >= TAPS) & (rows == cols - TAPS), 1.0, 0.0)
    return (lower + upper).astype(jnp.float32)


def local_estimates(smooth_re, smooth_im, power_row, noise_level, right_side, weight_row):
    antennas = smooth_re.shape[0]
    user_scale = (power_row / smooth_re.shape[1])[:, None]
    scaled_re = [smooth_re[i] * user_scale for i in range(antennas)]
    scaled_im = [smooth_im[i] * user_scale for i in range(antennas)]
    cov_re = [[None] * antennas for i in range(antennas)]
    cov_im = [[None] * antennas for i in range(antennas)]
    for i in range(antennas):
        for j in range(i + 1):
            cov_re[i][j] = jnp.sum(
                scaled_re[i] * smooth_re[j] + scaled_im[i] * smooth_im[j], axis=0
            )
            if i == j:
                cov_re[i][j] = cov_re[i][j] + noise_level
            else:
                cov_im[i][j] = jnp.sum(
                    scaled_im[i] * smooth_re[j] - scaled_re[i] * smooth_im[j], axis=0
                )
    signal = right_side.astype(jnp.float32)
    solved = hermitian_solve(cov_re, cov_im, signal[:, 0], signal[:, 1])
    est_re = (
        smooth_re[0][:, None, :] * solved[0][0][None]
        + smooth_im[0][:, None, :] * solved[0][1][None]
    )
    est_im = (
        smooth_re[0][:, None, :] * solved[0][1][None]
        - smooth_im[0][:, None, :] * solved[0][0][None]
    )
    for i in range(1, antennas):
        est_re = (
            est_re
            + smooth_re[i][:, None, :] * solved[i][0][None]
            + smooth_im[i][:, None, :] * solved[i][1][None]
        )
        est_im = (
            est_im
            + smooth_re[i][:, None, :] * solved[i][1][None]
            - smooth_im[i][:, None, :] * solved[i][0][None]
        )
    return weight_row[:, None, None, None] * jnp.stack([est_re, est_im], axis=2)


def local(
    unsmoothed_link_guesses,
    received,
    user_power,
    noise_power,
    ap_gain,
    user_cluster,
    serving,
    cluster_owner,
):
    ap_count = unsmoothed_link_guesses.shape[0]
    antennas = unsmoothed_link_guesses.shape[1]
    user_count = unsmoothed_link_guesses.shape[3]
    tone_positions = unsmoothed_link_guesses.shape[4]
    clusters = serving.shape[0]
    devices = lax.axis_size("ap")
    device = lax.axis_index("ap")
    lowest_tone = lax.axis_index("sc") * tone_positions
    products = jnp.dot(
        unsmoothed_link_guesses.reshape(-1, tone_positions),
        forward_table(lowest_tone, tone_positions),
        preferred_element_type=jnp.float32,
    )
    products = products.reshape((ap_count, antennas, 2, user_count, 2 * TAPS))
    rotated = jnp.dot(
        products[:, :, 1].reshape(-1, 2 * TAPS), rotate_matrix(), precision=lax.Precision.HIGHEST
    )
    combined = (
        products[:, :, 0] + rotated.reshape((ap_count, antennas, user_count, 2 * TAPS))
    ) / TONE_NUMBER
    coefficients = lax.psum(combined.astype(jnp.bfloat16), "sc")
    coef_b = coefficients.reshape(-1, 2 * TAPS)
    table_re, table_im = rebuild_tables(lowest_tone, tone_positions)
    smooth_re = jnp.dot(coef_b, table_re, preferred_element_type=jnp.float32).reshape(
        (ap_count, antennas, user_count, tone_positions)
    )
    smooth_im = jnp.dot(coef_b, table_im, preferred_element_type=jnp.float32).reshape(
        (ap_count, antennas, user_count, tone_positions)
    )
    cluster_ids = jnp.arange(clusters, dtype=jnp.int32)
    onehot = (user_cluster[:, None] == cluster_ids[None, :]).astype(jnp.float32)
    own_columns = lax.dynamic_slice_in_dim(serving, device * ap_count, ap_count, 1).astype(
        jnp.float32
    )
    weights = jnp.dot(onehot, own_columns, precision=lax.Precision.HIGHEST).T * ap_gain
    totals = lax.psum(jnp.sum(weights, axis=0), "ap")
    partial_value = local_estimates(
        smooth_re[0], smooth_im[0], user_power, noise_power[0], received[0], weights[0]
    )
    partial_value = partial_value + local_estimates(
        smooth_re[1], smooth_im[1], user_power, noise_power[1], received[1], weights[1]
    )
    partial_value = partial_value.astype(jnp.bfloat16)
    owner_map = cluster_owner[:, 0]
    same_owner = owner_map[:, None] == owner_map[None, :]
    earlier = cluster_ids[None, :] < cluster_ids[:, None]
    cluster_rank = jnp.sum(same_owner & earlier, axis=1)
    user_ids = jnp.arange(user_count, dtype=jnp.int32)
    position = jnp.sum(
        (user_cluster[:, None] == user_cluster[None, :]) & (user_ids[None, :] < user_ids[:, None]),
        axis=1,
    )
    member_hits = (user_cluster[None, None, :] == cluster_ids[:, None, None]) & (
        position[None, None, :] == jnp.arange(CU, dtype=jnp.int32)[None, :, None]
    )
    members = jnp.sum(jnp.where(member_hits, user_ids[None, None, :], 0), axis=2)
    slot_ids = jnp.arange(devices * OWN_MAX, dtype=jnp.int32)
    slot_hits = (owner_map[None, :] == (slot_ids // OWN_MAX)[:, None]) & (
        cluster_rank[None, :] == (slot_ids % OWN_MAX)[:, None]
    )
    hit_table = slot_hits.astype(jnp.int32)
    filled = jnp.sum(hit_table, axis=1)
    member_rows = jnp.sum(hit_table[:, :, None] * members[None], axis=1)
    picked = jnp.take(partial_value, member_rows.reshape(-1), axis=0)
    picked = picked.reshape(member_rows.shape + partial_value.shape[1:])
    owner_sums = lax.psum_scatter(
        picked * filled.astype(jnp.bfloat16)[:, None, None, None, None],
        "ap",
        scatter_dimension=0,
        tiled=True,
    ).astype(jnp.float32)
    my_hits = (
        (owner_map[None, :] == device)
        & (cluster_rank[None, :] == jnp.arange(OWN_MAX, dtype=jnp.int32)[:, None])
    ).astype(jnp.int32)
    my_rows = jnp.sum(my_hits[:, :, None] * members[None], axis=1)
    my_filled = jnp.sum(my_hits, axis=1).astype(jnp.float32)
    denominator = (
        1.0 + jnp.take(totals, my_rows.reshape(-1)).reshape(my_rows.shape) * my_filled[:, None]
    )
    return owner_sums / denominator[:, :, None, None, None]


def solution(mesh):
    placed = (
        P(("cell", "ap"), None, None, None, "sc"),
        P(("cell", "ap"), None, None, None, "sc"),
        P("cell"),
        P(("cell", "ap")),
        P(("cell", "ap"), None),
        P("cell"),
        P("cell", None),
        P("cell", None),
    )
    return jax.shard_map(
        local,
        mesh=mesh,
        in_specs=placed,
        out_specs=P(("cell", "ap"), None, None, None, "sc"),
        check_vma=False,
    )
```

profile of v0, /device:TPU:0, one launch (start us, length us, event | category | flops | bytes accessed | tf_op | source)
XLA Modules:
  0.0 179.4 jit_solution(7883190322390066773)
XLA Ops:
  6.6 2.5 %cosine_convert_fusion = (bf16[1024,64]{1,0:T(8,128)(2,1)S(1)}, bf16[1024,64]{1,0:T(8,128)(2,1)S(1)}) fusion(s32[1024]{0:T(1024)S(1)} %iota_add_fusion), kind=kLoop, calls=%fused_computation.154 | loop fusion | flops 1048576 | bytes 266240 | tf_op jit(solution)/shard_map/convert.2
  9.1 3.9 %convolution_bitcast_fusion = f32[2048,128]{0,1:T(8,128)S(1)} fusion(bf16[2048,1024]{1,0:T(8,128)(2,1)} %bitcast.232, bf16[1024,64]{1,0:T(8,128)(2,1)S(1)} %get-tuple-element.144, bf16[1024,64]{1,0:T(8,128)(2,1)S(1)} %get-tuple-element.143), kind=kOutput, calls=%fused_computation.8 | convolution fusion | flops 537395200 | bytes 5505024 | tf_op jit(solution)/shard_map/dot_general | solution.py:153
  13.0 0.9 reshape.10782
  13.9 0.8 fusion.186
  15.6 1.3 fusion.4
  17.1 1.1 sine_convert_fusion.1
  18.2 1.0 fusion.110
  20.4 0.6 fusion.187
  21.6 16.4 %all-reduce.2.cloned.1.call-done = bf16[1024,128]{1,0:T(8,128)(2,1)} async-done(((bf16[1024,128]{1,0:T(8,128)(2,1)}), bf16[1024,128]{1,0:T(8,128)(2,1)}) %all-reduce.2.cloned.1.call-update) | async-done | bytes 262160 | tf_op jit(solution)/shard_map/psum | solution.py:165
  38.0 1.7 fusion.82
  39.7 0.7 fusion.86
  40.4 1.1 fusion.50
  41.6 0.9 fusion.28
  42.4 0.9 fusion.24
  43.3 0.9 fusion.22
  44.2 1.0 fusion.32
  45.2 0.8 fusion.48
  47.3 0.6 sqrt_multiply_fusion
  48.0 0.7 rsqrt_multiply_fusion.9
  48.7 0.7 rsqrt_multiply_fusion.3
  49.3 0.7 sqrt_multiply_fusion.1
  50.4 4.1 %multiply_add_fusion = (f32[128,4,1,1024]{3,1,2,0:T(4,128)S(1)}, f32[128,4,1,1024]{3,1,2,0:T(4,128)S(1)}) fusion(f32[4,1024]{1,0:T(4,128)S(1)} %get-tuple-element.42, f32[128,1024]{1,0:T(8,128)S(1)} %get-tuple-element.103, f32[4,1024]{1,0:T(4,128)S(1)} %get-tuple-element.41, f32[128,1024]{1,0:T(8,128)S(1)} %get-tuple-element.109, ...), kind=kLoop, calls=%fused_computation.10 | loop fusion | flops 15728640 | bytes 8519680 | tf_op jit(solution)/shard_map/add | solution.py:123
  54.6 4.2 %multiply_add_fusion.1 = (f32[128,4,1,1024]{3,1,2,0:T(4,128)S(1)}, f32[128,4,1,1024]{3,1,2,0:T(4,128)S(1)}) fusion(f32[4,1024]{1,0:T(4,128)S(1)} %get-tuple-element.71, f32[128,1024]{1,0:T(8,128)S(1)} %get-tuple-element.112, f32[4,1024]{1,0:T(4,128)S(1)} %get-tuple-element.70, f32[128,1024]{1,0:T(8,128)S(1)} %get-tuple-element.114, ...), kind=kLoop, calls=%fused_computation.12 | loop fusion | flops 15728640 | bytes 8519680 | tf_op jit(solution)/shard_map/add | solution.py:123
  58.7 2.1 %fusion.1 = bf16[128,4,2,1024]{3,1,2,0:T(4,128)(2,1)S(1)} fusion(f32[128,4,1,1024]{3,1,2,0:T(4,128)S(1)} %get-tuple-element.98, f32[128,4,1,1024]{3,1,2,0:T(4,128)S(1)} %get-tuple-element.97, f32[128,4,1,1024]{3,1,2,0:T(4,128)S(1)} %get-tuple-element.96, f32[128,4,1,1024]{3,1,2,0:T(4,128)S(1)} %get-tuple-element.95, f32[128]{0:T(128)S(1)} %get-tuple-element.146, ...), kind=kLoop, calls=%fused_computation.4 | loop fusion | flops 6291456 | bytes 10486784 | tf_op jit(solution)/shard_map/convert_element_type | solution.py:187
  60.9 9.8 %gather_fusion = bf16[256,4,2,1024]{3,1,2,0:T(4,128)(2,1)} fusion(bf16[128,4,2,1024]{3,1,2,0:T(4,128)(2,1)S(1)} %fusion.1, s32[1024]{0:T(1024)S(1)} %pad_clamp_fusion.1), kind=kCustom, calls=%fused_computation | custom fusion | bytes 8389632 | tf_op jit(solution)/shard_map/jit(_take)/gather | solution.py:208
  70.7 7.1 %fusion.2 = bf16[32,8,4,2,1024]{4,1,0,3,2:T(8,128)(2,1)S(1)} fusion(bf16[256,4,2,1024]{3,1,2,0:T(4,128)(2,1)} %gather_fusion, pred[32,8]{1,0:T(8,128)(4,1)S(1)} %copy.25, bf16[32]{0:T(256)(128)(2,1)S(1)} %convert_element_type.86), kind=kLoop, calls=%fused_computation.7 | loop fusion | flops 4194304 | bytes 8388928 | tf_op jit(solution)/shard_map/mul | solution.py:211
  77.8 2.4 %copy.30 = bf16[32,8,4,2,1024]{4,1,3,2,0:T(8,128)(2,1)} copy(bf16[32,8,4,2,1024]{4,1,0,3,2:T(8,128)(2,1)S(1)} %fusion.2) | data formatting | bytes 8388608 | tf_op jit(solution)/shard_map/mul | solution.py:211
  80.5 22.2 %psum.15 = f32[128]{0:T(128)S(1)} all-reduce(f32[128]{0:T(128)S(1)} %get-tuple-element.149), channel_id=1, replica_groups=mesh['cell'=2,'ap'=8,'sc'=2] {'ap'}, use_global_device_ids=true, to_apply=%region_41.42 | all-reduce | flops 128 | bytes 1024 | tf_op jit(solution)/shard_map/psum | solution.py:180
  102.8 0.7 gather_fusion.1
  103.7 65.8 %reduce-scatter.2.cloned.1.call-done = bf16[4,8,4,2,1024]{4,1,3,2,0:T(8,128)(2,1)} async-done(((bf16[32,8,4,2,1024]{4,1,3,2,0:T(8,128)(2,1)}), bf16[4,8,4,2,1024]{4,1,3,2,0:T(8,128)(2,1)}) %reduce-scatter.2.cloned.1.call-update) | async-done | bytes 524304 | tf_op jit(solution)/shard_map/reduce_scatter | solution.py:210
  169.6 1.2 convert_divide_fusion
  170.8 1.8 copy.32
  (68 shorter events, 5.0 us)
Async XLA Ops:
  6.5 31.5 %all-reduce.2.cloned.1.call-start = ((), (), s32[]{:S(2)}) async-start(), calls=%async_computation.1 | async-start | bytes 524288 | tf_op jit(solution)/shard_map/psum | solution.py:165
  14.7 4.5 %copy-start.4 = (s32[128]{0:T(128)S(1)}, s32[128]{0:T(128)}, u32[]{:S(2)}) copy-start(s32[128]{0:T(128)} %param.13) | copy-start | bytes 1540
  14.7 4.7 %copy-start.2 = (s32[16,1]{0,1:T(1,128)S(1)}, s32[16,1]{0,1:T(1,128)}, u32[]{:S(2)}) copy-start(s32[16,1]{0,1:T(1,128)} %param.15) | copy-start | bytes 196
  14.7 5.6 %copy-start.7 = (f32[128]{0:T(128)S(1)}, f32[128]{0:T(128)}, u32[]{:S(2)}) copy-start(f32[128]{0:T(128)} %param.10) | copy-start | bytes 1540
  14.7 5.6 %copy-start.3 = (f32[2]{0:T(128)S(1)}, f32[2]{0:T(128)}, u32[]{:S(2)}) copy-start(f32[2]{0:T(128)} %param.11) | copy-start | bytes 28
  14.7 6.3 %copy-start.5 = (s32[16,16]{1,0:T(8,128)S(1)}, s32[16,16]{1,0:T(8,128)}, u32[]{:S(2)}) copy-start(s32[16,16]{1,0:T(8,128)} %param.14) | copy-start | bytes 3076
  14.7 6.3 %copy-start.6 = (f32[2,128]{1,0:T(2,128)S(1)}, f32[2,128]{1,0:T(2,128)}, u32[]{:S(2)}) copy-start(f32[2,128]{1,0:T(2,128)} %param.12) | copy-start | bytes 3076
  14.8 6.8 %copy-start.1 = (bf16[2,4,2,4,1024]{4,3,2,1,0:T(4,128)(2,1)S(1)}, bf16[2,4,2,4,1024]{4,3,2,1,0:T(4,128)(2,1)}, u32[]{:S(2)}) copy-start(bf16[2,4,2,4,1024]{4,3,2,1,0:T(4,128)(2,1)} %param.9) | copy-start | bytes 393220
  16.9 152.7 %reduce-scatter.2.cloned.1.call-start = ((), (), s32[]{:S(2)}) async-start(), calls=%async_computation.2 | async-start | bytes 4718592 | tf_op jit(solution)/shard_map/reduce_scatter | solution.py:210
  38.0 1.7 copy-start
Sparse Core Ops, SparseCore 0:
  17.0 20.9 all-reduce.1
  80.3 89.2 reduce-scatter.1
where the time goes:
time: 180 us; the launch traced here: 179 us
  waiting for transfers between devices  82.3 us (46%)
  other arithmetic  34.6 us (19%)
  blocking collectives  22.2 us (12%)
  local copies, waits for them, and re-layouts  18.4 us (10%)
  between operations  13.8 us (8%)
  matrix products  7.86 us (4%)
    reduce_scatter x1, waiting for transfers between devices, local(): lax.psum_scatter(picked * filled.astype(jnp.bfloat16)[:, None, None, None...  65.8 us
    psum x1, blocking collectives, local(): totals = lax.psum(jnp.sum(weights, axis=0), 'ap')  22.2 us
    psum x1, waiting for transfers between devices, local(): coefficients = lax.psum(combined.astype(jnp.bfloat16), 'sc')  16.4 us
    gather x1, local copies, waits for them, and re-layouts, local(): picked = jnp.take(partial_value, member_rows.reshape(-1), axis=0)  9.81 us
    add x2, other arithmetic, local_estimates(): est_re + smooth_re[i][:, None, :] * solved[i][0][None]  8.3 us
    mul x1, other arithmetic, local(): picked * filled.astype(jnp.bfloat16)[:, None, None, None, None]  7.08 us
    dot_general x1, matrix products, local(): jnp.dot(unsmoothed_link_guesses.reshape(-1, tone_positions), forward_tabl...  3.91 us
    another operation x3, other arithmetic  3.78 us
  transfers between devices with their start and end apart: 2, of which 2 were waited for; matrix products, arithmetic and copies ran while one was open for 3% of the time, Pallas kernels for 0%

commit v1 on v0

v1 whole, which is shorter than its diff:
```python
import functools
import math

import jax
import jax.numpy as jnp
import ml_dtypes
import numpy as np
from jax import lax
from jax.experimental import pallas as pl
from jax.experimental.pallas import tpu as pltpu
from jax.sharding import PartitionSpec as P

TONE_NUMBER = 2048
TAPS = 64
CU = 8
OWN_MAX = 4
PEER_MAX = 2
SAMPLES = 2 * TAPS
ROWS = PEER_MAX * CU
F32 = jnp.float32
BF16 = jnp.bfloat16


def np_parts(values, count):
    parts = []
    rest = values.astype(np.float64)
    for _ in range(count):
        part = rest.astype(np.float32).astype(ml_dtypes.bfloat16)
        parts.append(part)
        rest = rest - part.astype(np.float64)
    return parts


def np_angles(tones):
    turns = (tones[:, None] * np.arange(TAPS)[None, :]) % TONE_NUMBER
    return turns.astype(np.float64) * (2.0 * math.pi / TONE_NUMBER)


def forward_tables(shards, width):
    angles = np_angles(np.arange(shards * width))
    cosine = np.cos(angles).astype(np.float32).astype(ml_dtypes.bfloat16)
    sine = np.sin(angles).astype(np.float32).astype(ml_dtypes.bfloat16)
    real = np.concatenate([cosine, sine], axis=1).reshape(shards, width, 2 * TAPS)
    imag = np.concatenate([-sine, cosine], axis=1).reshape(shards, width, 2 * TAPS)
    return np.stack([real, imag], axis=1)


def rebuild_columns(tones):
    angles = np_angles(tones).T
    real = np.concatenate([np.cos(angles), np.sin(angles)], axis=0)
    imag = np.concatenate([-np.sin(angles), np.cos(angles)], axis=0)
    return (
        np.concatenate(np_parts(real, 2), axis=0),
        np.concatenate(np_parts(imag, 2), axis=0),
    )


def rebuild_tables(shards, width, chunk):
    real, imag = rebuild_columns(np.arange(shards * width))
    real = real.reshape(4 * TAPS, shards, width // chunk, 1, chunk)
    imag = imag.reshape(4 * TAPS, shards, width // chunk, 1, chunk)
    both = np.concatenate([real, imag], axis=3).reshape(4 * TAPS, shards, 2 * width)
    return np.ascontiguousarray(both.transpose(1, 0, 2))


def sample_table():
    real, imag = rebuild_columns(np.arange(SAMPLES) * (TONE_NUMBER // SAMPLES))
    return np.concatenate([real, imag], axis=1)


def dirichlet_tables(shards, width):
    step = TONE_NUMBER // SAMPLES
    wave = np.ones((TONE_NUMBER,), np.float64)
    tones = np.arange(TONE_NUMBER)
    for lag in range(1, TAPS):
        wave += 2.0 * np.cos(2.0 * math.pi * ((lag * tones) % TONE_NUMBER) / TONE_NUMBER)
    wave /= SAMPLES
    gap = (np.arange(shards * width)[None, :] - step * np.arange(SAMPLES)[:, None]) % TONE_NUMBER
    kernel = wave[gap]
    parts = np.concatenate(np_parts(kernel, 3), axis=0)
    parts = parts.reshape(3 * SAMPLES, shards, width)
    return np.ascontiguousarray(parts.transpose(1, 0, 2))


def coefficient_kernel(ids, table, guesses, out):
    antennas, _, users, tones = guesses.shape[1:]
    real = guesses[0, :, 0].reshape(antennas * users, tones)
    imag = guesses[0, :, 1].reshape(antennas * users, tones)
    total = jnp.dot(real, table[0, 0], preferred_element_type=F32)
    total = total + jnp.dot(imag, table[0, 1], preferred_element_type=F32)
    out[...] = (total * (1.0 / TONE_NUMBER)).astype(out.dtype)


def delay_coefficients(ids, guesses, shards):
    aps, antennas, _, users, tones = guesses.shape
    group = math.gcd(2, antennas)
    steps = antennas // group
    table = jnp.asarray(forward_tables(shards, tones))
    return pl.pallas_call(
        coefficient_kernel,
        grid_spec=pltpu.PrefetchScalarGridSpec(
            num_scalar_prefetch=1,
            grid=(aps, steps),
            in_specs=[
                pl.BlockSpec((1, 2, tones, 2 * TAPS), lambda a, i, ids: (ids[1], 0, 0, 0)),
                pl.BlockSpec((1, group, 2, users, tones), lambda a, i, ids: (a, i, 0, 0, 0)),
            ],
            out_specs=pl.BlockSpec(
                (group * users, 2 * TAPS), lambda a, i, ids: (a * steps + i, 0)
            ),
        ),
        out_shape=jax.ShapeDtypeStruct((aps * antennas * users, 2 * TAPS), BF16),
        compiler_params=pltpu.CompilerParams(vmem_limit_bytes=32 * 1024 * 1024),
        cost_estimate=pl.CostEstimate(
            flops=4 * guesses.size * 2 * TAPS // 2, bytes_accessed=2 * guesses.size, transcendentals=0
        ),
        name="delay_coefficients",
    )(ids, table, guesses)


def three_parts(values):
    high = values.astype(BF16)
    rest = values - high.astype(F32)
    middle = rest.astype(BF16)
    low = (rest - middle.astype(F32)).astype(BF16)
    return high, middle, low


def iota(shape, axis):
    return lax.broadcasted_iota(jnp.int32, shape, axis)


def column_of(row):
    n = row.shape[1]
    return jnp.sum(jnp.where(iota((n, n), 0) == iota((n, n), 1), row, 0.0), axis=1, keepdims=True)


def row_of(column):
    n = column.shape[0]
    return jnp.sum(
        jnp.where(iota((n, n), 0) == iota((n, n), 1), column, 0.0), axis=0, keepdims=True
    )


def payload_kernel(shape, ids, noise, *refs):
    aps, antennas, users, devices, shards = shape
    per = devices // shards
    parts = refs[:shards]
    power, gain, cluster_row, serving, owner, table = refs[shards : shards + 6]
    outs = refs[shards + 6 : shards + 6 + per]
    slots, coef, smooth, cov = refs[shards + 6 + per :]
    device, core = ids[0], ids[1]
    clusters = serving.shape[0]

    total = parts[0][...].astype(F32)
    for part in parts[1:]:
        total = total + part[...].astype(F32)
    coef_b = total.astype(BF16)
    coef[:, : 2 * TAPS] = coef_b
    coef[:, 2 * TAPS :] = coef_b

    smooth[...] = jnp.dot(coef[...], table[...], preferred_element_type=F32)
    scale = column_of(power[...]) * (1.0 / users)
    for a in range(aps):
        base = a * antennas * users
        sums = {}
        for start in range(0, users, 8):
            re, im = [], []
            for i in range(antennas):
                rows = smooth[pl.ds(base + i * users + start, 8), :]
                re.append(rows[:, :SAMPLES])
                im.append(rows[:, SAMPLES:])
            weight = jnp.broadcast_to(scale[start : start + 8], (8, SAMPLES))
            for i in range(antennas):
                sre, sim = re[i] * weight, im[i] * weight
                for j in range(i + 1):
                    value = sre * re[j] + sim * im[j]
                    sums[i, j, 0] = sums[i, j, 0] + value if start else value
                    if j < i:
                        value = sim * re[j] - sre * im[j]
                        sums[i, j, 1] = sums[i, j, 1] + value if start else value
        field = 0
        for i in range(antennas):
            for j in range(i + 1):
                for c in range(2 if j < i else 1):
                    row = jnp.sum(sums[i, j, c], axis=0, keepdims=True)
                    if i == j:
                        row = row + noise[a]
                    cov[pl.ds(a * antennas * antennas + field, 1), :] = row
                    field += 1

    serving_f = serving[...].astype(F32)
    columns = serving.shape[1]
    pairs = (iota((columns, devices), 0) // aps == iota((columns, devices), 1)).astype(F32)
    served = (jnp.dot(serving_f, pairs, preferred_element_type=F32) > 0.5).astype(F32)
    served_here = jnp.sum(
        jnp.where(iota((clusters, devices), 1) == device, served, 0.0), axis=1, keepdims=True
    )
    owner_col = owner[...]
    owner_f = owner_col.astype(F32)
    square = (clusters, clusters)
    before = iota(square, 1) < iota(square, 0)
    earlier = before & (owner_f == row_of(owner_f))
    turn = jnp.sum(jnp.where(earlier, row_of(served_here), 0.0), axis=1, keepdims=True)
    label = (owner_col ^ device) ^ (core * per)
    valid = (served_here > 0.5) & (label < per)
    base = jnp.where(valid, label.astype(F32) * ROWS + turn * CU, -4.0 * ROWS * devices)
    members = (iota((clusters, users), 0) == cluster_row[...]).astype(F32)
    prefix = (iota((users, users), 0) < iota((users, users), 1)).astype(F32)
    order = jnp.dot(members, prefix, preferred_element_type=F32)
    target = jnp.sum(members * (order + base), axis=0, keepdims=True).astype(jnp.int32)
    pick = (iota((per * ROWS, users), 0) == target).astype(F32).astype(BF16)

    weight_rows = []
    for a in range(aps):
        column = iota((clusters, columns), 1) == device * aps + a
        mine = jnp.sum(jnp.where(column, serving_f, 0.0), axis=1, keepdims=True)
        weight_rows.append(
            jnp.sum(members * mine, axis=0, keepdims=True) * gain[pl.ds(a, 1), :]
        )
    stacked = jnp.concatenate(
        weight_rows + [jnp.zeros((8 - aps, users), F32)], axis=0
    )
    weight_parts = jnp.concatenate(
        [part.astype(F32) for part in three_parts(stacked)]
        + [jnp.zeros((2 * TAPS - 24, users), F32)],
        axis=0,
    ).astype(BF16)
    picked_weights = lax.dot_general(
        pick, weight_parts, (((1,), (1,)), ((), ())), preferred_element_type=F32
    ).astype(BF16)

    cov_parts = three_parts(cov[...])
    cov_rows = cov.shape[0]
    first = aps * antennas * ROWS
    for ai in range(aps * antennas):
        chosen = jnp.dot(
            pick, coef[pl.ds(ai * users, users), : 2 * TAPS], preferred_element_type=F32
        ).astype(BF16)
        for j in range(per):
            outs[j][pl.ds(ai * ROWS, ROWS), :] = chosen[j * ROWS : (j + 1) * ROWS]
    for j in range(per):
        for k in range(3):
            outs[j][pl.ds(first + k * cov_rows, cov_rows), :] = cov_parts[k]
        outs[j][pl.ds(first + 3 * cov_rows, ROWS), :] = picked_weights[j * ROWS : (j + 1) * ROWS]

    mine = (owner_col == device).astype(F32)
    lower = before.astype(F32)
    rank = jnp.sum(jnp.where(before, row_of(mine), 0.0), axis=1, keepdims=True)
    here = mine * served
    turns = jnp.dot(lower, here, preferred_element_type=F32)
    for p in range(PEER_MAX):
        hit = jnp.where(turns == float(p), here, 0.0)
        slots[pl.ds(p, 1), :] = jnp.sum(hit * rank, axis=0, keepdims=True).astype(jnp.int32)


def payload_rows(aps, antennas):
    return aps * antennas * ROWS + 3 * aps * antennas * antennas + ROWS


def owner_payloads(ids, parts, power, noise, gain, cluster, serving, owner, shape):
    aps, antennas, users, devices, shards = shape
    per = devices // shards
    rows = payload_rows(aps, antennas)
    vmem = pl.BlockSpec(memory_space=pltpu.VMEM)
    smem = pl.BlockSpec(memory_space=pltpu.SMEM)
    return pl.pallas_call(
        functools.partial(payload_kernel, shape),
        in_specs=[smem, smem] + [vmem] * (shards + 6),
        out_specs=[vmem] * (per + 1),
        out_shape=[jax.ShapeDtypeStruct((rows, 2 * TAPS), BF16)] * per
        + [jax.ShapeDtypeStruct((PEER_MAX, devices), jnp.int32)],
        scratch_shapes=[
            pltpu.VMEM((aps * antennas * users, 4 * TAPS), BF16),
            pltpu.VMEM((aps * antennas * users, 2 * SAMPLES), F32),
            pltpu.VMEM((aps * antennas * antennas, SAMPLES), F32),
        ],
        compiler_params=pltpu.CompilerParams(vmem_limit_bytes=32 * 1024 * 1024),
        cost_estimate=pl.CostEstimate(
            flops=4 * aps * antennas * users * 4 * TAPS * SAMPLES,
            bytes_accessed=2 * 1024 * 1024,
            transcendentals=0,
        ),
        name="owner_payloads",
    )(
        ids,
        noise,
        *parts,
        power[None, :],
        gain,
        cluster[None, :],
        serving,
        owner,
        jnp.asarray(sample_table()),
    )


def complex_times(left, right):
    return (left[0] * right[0] - left[1] * right[1], left[0] * right[1] + left[1] * right[0])


def times_conj(left, right):
    return (left[0] * right[0] + left[1] * right[1], left[1] * right[0] - left[0] * right[1])


def minus(left, right):
    return (left[0] - right[0], left[1] - right[1])


def factorize(cov, antennas):
    factor, inverse = {}, []
    for j in range(antennas):
        pivot = cov[j, j][0]
        for k in range(j):
            pivot = pivot - (factor[j, k][0] * factor[j, k][0] + factor[j, k][1] * factor[j, k][1])
        root = lax.rsqrt(pivot)
        inverse.append(root)
        for i in range(j + 1, antennas):
            running = cov[i, j]
            for k in range(j):
                running = minus(running, times_conj(factor[i, k], factor[j, k]))
            factor[i, j] = (running[0] * root, running[1] * root)
    return factor, inverse


def substitute(factor, inverse, right):
    antennas = len(inverse)
    forward = []
    for i in range(antennas):
        running = right[i]
        for k in range(i):
            running = minus(running, complex_times(factor[i, k], forward[k]))
        forward.append((running[0] * inverse[i], running[1] * inverse[i]))
    result = [None] * antennas
    for i in range(antennas - 1, -1, -1):
        running = forward[i]
        for k in range(i + 1, antennas):
            running = minus(running, times_conj(result[k], factor[k, i]))
        result[i] = (running[0] * inverse[i], running[1] * inverse[i])
    return result


def estimate_kernel(shape, chunk, ids, slots, *refs):
    aps, antennas, symbols, tones, devices, shards = shape
    per = devices // shards
    pays, signals = refs[:devices], refs[devices : 2 * devices]
    kernel_table, rebuild_table, out = refs[2 * devices : 2 * devices + 3]
    (
        pay, sig, dirichlet, rebuild, left, cov_full, cov_tiles, sig_tiles, solved, smooth, weight,
        acc, denominator, turned, pay_sem, sig_sem, table_sem,
    ) = refs[2 * devices + 3 :]
    device, core = ids[0], ids[1]
    cov_rows = aps * antennas * antennas
    coef_rows = aps * antennas * ROWS
    blocks = tones // 128

    def copies():
        yield pltpu.make_async_copy(kernel_table.at[core], dirichlet, table_sem.at[0])
        for l in range(devices):
            yield pltpu.make_async_copy(pays[l], pay.at[l], pay_sem.at[l])
        yield pltpu.make_async_copy(rebuild_table.at[core], rebuild, table_sem.at[1])
        for v in range(devices):
            yield pltpu.make_async_copy(signals[v], sig.at[v], sig_sem.at[v])

    started = list(copies())
    for copy in started:
        copy.start()
    for copy in started:
        copy.wait()

    def cov_part(k):
        rows = pay[:, pl.ds(coef_rows + k * cov_rows, cov_rows), :]
        return rows.reshape(devices * cov_rows, SAMPLES)

    high, middle, low = cov_part(0), cov_part(1), cov_part(2)
    n = SAMPLES
    cov_full[...] = (
        jnp.dot(low, dirichlet[:n], preferred_element_type=F32)
        + jnp.dot(
            jnp.concatenate([middle, middle], axis=1), dirichlet[: 2 * n], preferred_element_type=F32
        )
        + jnp.dot(
            jnp.concatenate([high, high, high], axis=1), dirichlet[...], preferred_element_type=F32
        )
    )

    for l in range(devices):
        rows = pay[l, pl.ds(0, coef_rows), :]
        left[pl.ds(l * coef_rows, coef_rows), : 2 * TAPS] = rows
        left[pl.ds(l * coef_rows, coef_rows), 2 * TAPS :] = rows
        packed = pay[l, pl.ds(coef_rows + 3 * cov_rows, ROWS), :].astype(F32)
        for a in range(aps):
            value = packed[:, a : a + 1] + packed[:, 8 + a : 9 + a] + packed[:, 16 + a : 17 + a]
            weight[l, a] = jnp.broadcast_to(value, (ROWS, 128))

    acc[...] = jnp.zeros_like(acc)
    denominator[...] = jnp.ones_like(denominator)

    def label_of(l):
        return l ^ (core * per)

    def solve(l, carry):
        v = label_of(l)
        for r in range(0, cov_rows, 8):
            rows = cov_full[pl.ds(pl.multiple_of(l * cov_rows + r, 8), 8), :]
            for b in range(blocks):
                cov_tiles[pl.ds(r * blocks + b, 8, stride=blocks), :] = rows[:, b * 128 : (b + 1) * 128]
        for a in range(aps):
            for i in range(antennas):
                for c in range(2):
                    rows = sig[v, a, i, c].astype(F32)
                    first = ((a * antennas + i) * 2 + c) * symbols * blocks
                    for b in range(blocks):
                        sig_tiles[pl.ds(first + b, symbols, stride=blocks), :] = rows[
                            :, b * 128 : (b + 1) * 128
                        ]
        for a in range(aps):
            cov = {}
            field = a * antennas * antennas
            for i in range(antennas):
                for j in range(i + 1):
                    parts = []
                    for c in range(2 if j < i else 1):
                        parts.append(cov_tiles[pl.ds(field * blocks, blocks), :])
                        field += 1
                    cov[i, j] = parts
            factor, inverse = factorize(cov, antennas)
            for s in range(symbols):
                right = []
                for i in range(antennas):
                    tiles = [
                        (((a * antennas + i) * 2 + c) * symbols + s) * blocks for c in range(2)
                    ]
                    right.append([sig_tiles[pl.ds(t, blocks), :] for t in tiles])
                result = substitute(factor, inverse, right)
                for i in range(antennas):
                    for c in range(2):
                        at = ((a * antennas + i) * symbols + s) * 2 + c
                        solved[l, pl.ds(at * blocks, blocks), :] = result[i][c]
        for p in range(PEER_MAX):
            k = slots[p, v ^ device]
            for a in range(aps):
                denominator[k] = denominator[k] + weight[l, a, pl.ds(p * CU, CU), :]
        return carry

    lax.fori_loop(0, devices, solve, 0)

    def combine(l, q):
        v = label_of(l)
        for h in range(chunk // 128):
            b = q * (chunk // 128) + h
            lanes = pl.ds(pl.multiple_of(b * 128, 128), 128)
            totals = [[None] * (2 * symbols) for p in range(PEER_MAX)]
            for a in range(aps):
                for i in range(antennas):
                    base = pl.multiple_of(l * coef_rows + (a * antennas + i) * ROWS, 8)
                    link = []
                    for p in range(PEER_MAX):
                        scale = weight[l, a, pl.ds(p * CU, CU), :]
                        rows = pl.ds(base + p * CU, CU)
                        link.append(
                            (
                                smooth[rows, h * 128 : (h + 1) * 128] * scale,
                                smooth[rows, chunk + h * 128 : chunk + (h + 1) * 128] * scale,
                            )
                        )
                    for s in range(symbols):
                        at = ((a * antennas + i) * symbols + s) * 2
                        xr = solved[l, pl.ds(at * blocks + b, 1), :]
                        xi = solved[l, pl.ds((at + 1) * blocks + b, 1), :]
                        xr = jnp.broadcast_to(xr, (CU, 128))
                        xi = jnp.broadcast_to(xi, (CU, 128))
                        for p in range(PEER_MAX):
                            gr, gi = link[p]
                            er = gr * xr + gi * xi
                            ei = gr * xi - gi * xr
                            if totals[p][2 * s] is None:
                                totals[p][2 * s], totals[p][2 * s + 1] = er, ei
                            else:
                                totals[p][2 * s] += er
                                totals[p][2 * s + 1] += ei
            for p in range(PEER_MAX):
                k = slots[p, v ^ device]
                for e in range(2 * symbols):
                    acc[k, e, :, lanes] = acc[k, e, :, lanes] + totals[p][e]

    def one_chunk(q, carry):
        columns = pl.ds(pl.multiple_of(q * 2 * chunk, 128), 2 * chunk)
        smooth[...] = jnp.dot(left[...], rebuild[:, columns], preferred_element_type=F32)

        def step(l, inner):
            combine(l, q)
            return inner

        lax.fori_loop(0, devices, step, 0)
        return carry

    lax.fori_loop(0, tones // chunk, one_chunk, 0)

    def finish(k, carry):
        inverse = 1.0 / denominator[k]
        for b in range(blocks):
            for e in range(2 * symbols):
                value = acc[k, e, :, b * 128 : (b + 1) * 128] * inverse
                turned[pl.ds(b * CU * 2 * symbols + e, CU, stride=2 * symbols), :] = value
            for m in range(CU):
                for s in range(symbols):
                    at = ((b * CU + m) * symbols + s) * 2
                    out[k, m, s, :, b * 128 : (b + 1) * 128] = turned[pl.ds(at, 2), :]
        return carry

    lax.fori_loop(0, OWN_MAX, finish, 0)


def owner_estimates(ids, slots, pays, signals, shape):
    aps, antennas, symbols, tones, devices, shards = shape
    chunk = min(256, tones)
    rows = payload_rows(aps, antennas)
    cov_rows = aps * antennas * antennas
    coef_rows = aps * antennas * ROWS
    vmem = pl.BlockSpec(memory_space=pltpu.VMEM)
    smem = pl.BlockSpec(memory_space=pltpu.SMEM)
    anywhere = pl.BlockSpec(memory_space=pl.ANY)
    blocks = tones // 128
    return pl.pallas_call(
        functools.partial(estimate_kernel, shape, chunk),
        in_specs=[smem, smem] + [anywhere] * (2 * devices + 2),
        out_specs=vmem,
        out_shape=jax.ShapeDtypeStruct((OWN_MAX, CU, symbols, 2, tones), F32),
        scratch_shapes=[
            pltpu.VMEM((devices, rows, 2 * TAPS), BF16),
            pltpu.VMEM((devices,) + signals[0].shape, BF16),
            pltpu.VMEM((3 * SAMPLES, tones), BF16),
            pltpu.VMEM((4 * TAPS, 2 * tones), BF16),
            pltpu.VMEM((devices * coef_rows, 4 * TAPS), BF16),
            pltpu.VMEM((devices * cov_rows, tones), F32),
            pltpu.VMEM((cov_rows * blocks, 128), F32),
            pltpu.VMEM((aps * antennas * 2 * symbols * blocks, 128), F32),
            pltpu.VMEM((devices, aps * antennas * 2 * symbols * blocks, 128), F32),
            pltpu.VMEM((devices * coef_rows, 2 * chunk), F32),
            pltpu.VMEM((devices, aps, ROWS, 128), F32),
            pltpu.VMEM((OWN_MAX, 2 * symbols, CU, tones), F32),
            pltpu.VMEM((OWN_MAX, CU, 128), F32),
            pltpu.VMEM((CU * 2 * symbols * blocks, 128), F32),
            pltpu.SemaphoreType.DMA((devices,)),
            pltpu.SemaphoreType.DMA((devices,)),
            pltpu.SemaphoreType.DMA((2,)),
        ],
        compiler_params=pltpu.CompilerParams(vmem_limit_bytes=48 * 1024 * 1024),
        cost_estimate=pl.CostEstimate(
            flops=4 * devices * coef_rows * 4 * TAPS * tones,
            bytes_accessed=8 * 1024 * 1024,
            transcendentals=0,
        ),
        name="owner_estimates",
    )(
        ids,
        slots,
        *pays,
        *signals,
        jnp.asarray(dirichlet_tables(shards, tones)),
        jnp.asarray(rebuild_tables(shards, tones, chunk)),
    )


def local(
    unsmoothed_link_guesses,
    received,
    user_power,
    noise_power,
    ap_gain,
    user_cluster,
    serving,
    cluster_owner,
):
    aps, antennas, _, users, tones = unsmoothed_link_guesses.shape
    symbols = received.shape[3]
    devices, shards = lax.axis_size("ap"), lax.axis_size("sc")
    per = devices // shards
    ids = jnp.stack([lax.axis_index("ap"), lax.axis_index("sc")]).astype(jnp.int32)

    def swap_ap(value, v):
        return lax.ppermute(value, "ap", [(i, i ^ v) for i in range(devices)])

    def swap_sc(value, h):
        return lax.ppermute(value, "sc", [(c, c ^ h) for c in range(shards)])

    signals = [None] * devices
    for v in range(0, devices, 2):
        signals[v] = swap_ap(received, v) if v else received
        signals[v + 1] = swap_ap(signals[v], 1)

    combined = delay_coefficients(ids, unsmoothed_link_guesses, shards)
    parts = [combined] + [swap_sc(combined, h) for h in range(1, shards)]
    *blocks, slots = owner_payloads(
        ids, parts, user_power, noise_power, ap_gain, user_cluster, serving, cluster_owner,
        (aps, antennas, users, devices, shards),
    )

    pairs = lambda j: [
        (i * shards + c, (i ^ (c * per + j)) * shards + c)
        for i in range(devices)
        for c in range(shards)
    ]
    own = [lax.ppermute(blocks[j], ("ap", "sc"), pairs(j)) for j in range(per)]
    pays = own + [swap_sc(own[j], h) for h in range(1, shards) for j in range(per)]
    return owner_estimates(
        ids, slots, pays, signals, (aps, antennas, symbols, tones, devices, shards)
    )


def solution(mesh):
    placed = (
        P(("cell", "ap"), None, None, None, "sc"),
        P(("cell", "ap"), None, None, None, "sc"),
        P("cell"),
        P(("cell", "ap")),
        P(("cell", "ap"), None),
        P("cell"),
        P("cell", None),
        P("cell", None),
    )
    return jax.shard_map(
        local,
        mesh=mesh,
        in_specs=placed,
        out_specs=P(("cell", "ap"), None, None, None, "sc"),
        check_vma=False,
    )
```

time: 180 us -> 57.5 us (0.32)
  waiting for transfers between devices: 82.3 us -> 5.76 us
  other arithmetic: 34.6 us -> 0.07 us
  starting transfers between devices: 0.22 us -> 23.3 us
  blocking collectives: 22.2 us -> 0 us
  Pallas kernels: 0 us -> 17.6 us
  between operations: 13.8 us -> 0.08 us
  local copies, waits for them, and re-layouts: 18.4 us -> 10.4 us
  matrix products: 7.86 us -> 0 us
    reduce_scatter x1 -> x0, waiting for transfers between devices: 65.8 us -> none  [local(): lax.psum_scatter(picked * filled.astype(jnp.bfloat16)[:, None, None, None...]
    ppermute x0 -> x16, starting transfers between devices: none -> 23.3 us  [the longest x7 10.5 us: swap_ap(): return lax.ppermute(value, 'ap', [(i, i ^ v) for i in range(devices)])]
    psum x1 -> x0, blocking collectives: 22.2 us -> none  [local(): totals = lax.psum(jnp.sum(weights, axis=0), 'ap')]
    pallas_call x0 -> x3, Pallas kernels: none -> 17.6 us  [the longest x1 13.7 us: owner_estimates(): pl.pallas_call(functools.partial(estimate_kernel, shape, chunk), in_specs...]
    psum x1 -> x0, waiting for transfers between devices: 16.4 us -> none  [local(): coefficients = lax.psum(combined.astype(jnp.bfloat16), 'sc')]
    gather x3 -> x0, local copies, waits for them, and re-layouts: 10.6 us -> none  [the longest x1 9.81 us: local(): picked = jnp.take(partial_value, member_rows.reshape(-1), axis=0)]
    unnamed x18 -> x29, local copies, waits for them, and re-layouts: 0.83 us -> 10.4 us
    add x4 -> x0, other arithmetic: 8.38 us -> none  [the longest x2 8.3 us: local_estimates(): est_re + smooth_re[i][:, None, :] * solved[i][0][None]]
  transfers between devices with their start and end apart: 2 -> 16, of which waited for: 2 -> 3; matrix products, arithmetic and copies ran while one was open for 3% -> 1% of each run, Pallas kernels for 0% -> 3%
where the time goes in v1:
time: 57.5 us; the launch traced here: 57.2 us
  starting transfers between devices  23.3 us (41%)
  Pallas kernels  17.6 us (31%)
  local copies, waits for them, and re-layouts  10.4 us (18%)
  waiting for transfers between devices  5.76 us (10%)
    pallas_call x1, Pallas kernels, owner_estimates(): pl.pallas_call(functools.partial(estimate_kernel, shape, chunk), in_specs...  13.7 us
    ppermute x7, starting transfers between devices, swap_ap(): return lax.ppermute(value, 'ap', [(i, i ^ v) for i in range(devices)])  10.5 us
    unnamed x29, local copies, waits for them, and re-layouts  10.4 us
    ppermute x5, starting transfers between devices, swap_sc(): return lax.ppermute(value, 'sc', [(c, c ^ h) for c in range(shards)])  8.15 us
    ppermute x7, waiting for transfers between devices, swap_ap(): return lax.ppermute(value, 'ap', [(i, i ^ v) for i in range(devices)])  4.86 us
    ppermute x4, starting transfers between devices, local(): own = [lax.ppermute(blocks[j], ('ap', 'sc'), pairs(j)) for j in range(per)]  4.6 us
    pallas_call x1, Pallas kernels, delay_coefficients(): pl.pallas_call(coefficient_kernel, grid_spec=pltpu.PrefetchScalarGridSpec...  2.3 us
    pallas_call x1, Pallas kernels, owner_payloads(): pl.pallas_call(functools.partial(payload_kernel, shape), in_specs=[smem,...  1.57 us
  transfers between devices with their start and end apart: 16, of which 3 were waited for; matrix products, arithmetic and copies ran while one was open for 1% of the time, Pallas kernels for 3%

profile of v1, /device:TPU:0, one launch (start us, length us, event | category | flops | bytes accessed | tf_op | source)
XLA Modules:
  0.0 57.2 jit_solution(7973807556532337303)
XLA Ops:
  0.1 2.2 %copy-done = bf16[2,4,2,128,1024]{4,3,2,1,0:T(8,128)(2,1)S(1)} copy-done((bf16[2,4,2,128,1024]{4,3,2,1,0:T(8,128)(2,1)S(1)}, bf16[2,4,2,128,1024]{4,3,2,1,0:T(8,128)(2,1)}, u32[]{:S(2)}) %copy-start) | copy-done | bytes 4194328
  2.3 1.2 %copy-done.3 = bf16[2,2,1024,128]{3,2,1,0:T(8,128)(2,1)S(1)} copy-done((bf16[2,2,1024,128]{3,2,1,0:T(8,128)(2,1)S(1)}, bf16[2,2,1024,128]{3,2,1,0:T(8,128)(2,1)}, u32[]{:S(2)}) %copy-start.3) | copy-done | bytes 1048600
  3.5 2.3 %delay_coefficients.1.refs_0_ = bf16[1024,128]{1,0:T(8,128)(2,1)S(1)} custom-call(s32[2]{0:T(128)S(1)} %pad_add_fusion.ids, bf16[2,2,1024,128]{3,2,1,0:T(8,128)(2,1)S(1)} %copy-done.3, bf16[2,4,2,128,1024]{4,3,2,1,0:T(8,128)(2,1)S(1)} %copy-done), custom_call_target="tpu_custom_call" | custom-call | flops 536870912 | bytes 4194304 | tf_op jit(solution)/shard_map/delay_coefficients/pallas_call | solution.py:99
  5.8 0.5 collective-permute-start
  6.3 3.7 %collective-permute-start.12 = (bf16[2,4,2,4,1024]{4,3,2,1,0:T(4,128)(2,1)S(1)}, bf16[2,4,2,4,1024]{4,3,2,1,0:T(4,128)(2,1)S(1)}, u32[]{:S(2)}, u32[]{:S(2)}) collective-permute-start(bf16[2,4,2,4,1024]{4,3,2,1,0:T(4,128)(2,1)S(1)} %copy-done.4), channel_id=1, source_target_pairs={{0,8},{2,10},{4,12},{6,14},{8,0},{10,2},{12,4},{14,6},{1,9},{3,11}... | collective-permute-start | bytes 393224 | tf_op jit(solution)/shard_map/ppermute | solution.py:583
  10.0 1.6 %collective-permute-start.10 = (bf16[2,4,2,4,1024]{4,3,2,1,0:T(4,128)(2,1)S(1)}, bf16[2,4,2,4,1024]{4,3,2,1,0:T(4,128)(2,1)S(1)}, u32[]{:S(2)}, u32[]{:S(2)}) collective-permute-start(bf16[2,4,2,4,1024]{4,3,2,1,0:T(4,128)(2,1)S(1)} %copy-done.4), channel_id=1, source_target_pairs={{0,4},{2,6},{4,0},{6,2},{8,12},{10,14},{12,8},{14,10},{1,5},{3,7},... | collective-permute-start | bytes 393224 | tf_op jit(solution)/shard_map/ppermute | solution.py:583
  11.6 1.7 %collective-permute-start.9 = (bf16[2,4,2,4,1024]{4,3,2,1,0:T(4,128)(2,1)S(1)}, bf16[2,4,2,4,1024]{4,3,2,1,0:T(4,128)(2,1)S(1)}, u32[]{:S(2)}, u32[]{:S(2)}) collective-permute-start(bf16[2,4,2,4,1024]{4,3,2,1,0:T(4,128)(2,1)S(1)} %copy-done.4), channel_id=1, source_target_pairs={{0,2},{2,0},{4,6},{6,4},{8,10},{10,8},{12,14},{14,12},{1,3},{3,1},... | collective-permute-start | bytes 393224 | tf_op jit(solution)/shard_map/ppermute | solution.py:583
  13.3 3.9 %collective-permute-done.12.refs_12_ = bf16[2,4,2,4,1024]{4,3,2,1,0:T(4,128)(2,1)S(1)} collective-permute-done((bf16[2,4,2,4,1024]{4,3,2,1,0:T(4,128)(2,1)S(1)}, bf16[2,4,2,4,1024]{4,3,2,1,0:T(4,128)(2,1)S(1)}, u32[]{:S(2)}, u32[]{:S(2)}) %collective-permute-start.12) | collective-permute-done | bytes 131104 | tf_op jit(solution)/shard_map/ppermute | solution.py:583
  17.2 1.8 %collective-permute-start.13 = (bf16[2,4,2,4,1024]{4,3,2,1,0:T(4,128)(2,1)S(1)}, bf16[2,4,2,4,1024]{4,3,2,1,0:T(4,128)(2,1)S(1)}, u32[]{:S(2)}, u32[]{:S(2)}) collective-permute-start(bf16[2,4,2,4,1024]{4,3,2,1,0:T(4,128)(2,1)S(1)} %collective-permute-done.12.refs_12_), channel_id=1, source_target_pairs={{0,2},{2,0},{4,6},{6,4},{8,10},{10,8},{12,14},{14,12},{1,3},{3,1},... | collective-permute-start | bytes 393224 | tf_op jit(solution)/shard_map/ppermute | solution.py:583
  19.0 0.3 collective-permute-start.11
  19.2 0.7 %copy.13.refs_6_ = s32[16,1]{1,0:T(8,128)S(1)} copy(s32[16,1]{0,1:T(1,128)} %param.19) | data formatting | bytes 128 | tf_op args[7]
  20.0 1.0 %collective-permute-done.14.refs_14_ = bf16[2,4,2,4,1024]{4,3,2,1,0:T(4,128)(2,1)S(1)} collective-permute-done((bf16[2,4,2,4,1024]{4,3,2,1,0:T(4,128)(2,1)S(1)}, bf16[2,4,2,4,1024]{4,3,2,1,0:T(4,128)(2,1)S(1)}, u32[]{:S(2)}, u32[]{:S(2)}) %collective-permute-start.14) | collective-permute-done | bytes 131104 | tf_op jit(solution)/shard_map/ppermute | solution.py:583
  20.9 1.5 %collective-permute-start.15 = (bf16[2,4,2,4,1024]{4,3,2,1,0:T(4,128)(2,1)S(1)}, bf16[2,4,2,4,1024]{4,3,2,1,0:T(4,128)(2,1)S(1)}, u32[]{:S(2)}, u32[]{:S(2)}) collective-permute-start(bf16[2,4,2,4,1024]{4,3,2,1,0:T(4,128)(2,1)S(1)} %collective-permute-done.14.refs_14_), channel_id=1, source_target_pairs={{0,2},{2,0},{4,6},{6,4},{8,10},{10,8},{12,14},{14,12},{1,3},{3,1},... | collective-permute-start | bytes 393224 | tf_op jit(solution)/shard_map/ppermute | solution.py:583
  22.5 0.9 %copy-done.5 = bf16[256,256]{1,0:T(8,128)(2,1)S(1)} copy-done((bf16[256,256]{1,0:T(8,128)(2,1)S(1)}, bf16[256,256]{1,0:T(8,128)(2,1)}, u32[]{:S(2)}) %copy-start.5) | copy-done | bytes 131096
  23.4 0.7 %copy-done.8 = s32[2]{0:T(128)S(1)} copy-done((s32[2]{0:T(128)S(1)}, s32[2]{0:T(128)}, u32[]{:S(2)}) %copy-start.8) | copy-done | bytes 32
  24.0 0.7 %copy-done.10 = f32[2,128]{1,0:T(2,128)S(1)} copy-done((f32[2,128]{1,0:T(2,128)S(1)}, f32[2,128]{1,0:T(2,128)}, u32[]{:S(2)}) %copy-start.10) | copy-done | bytes 1048
  24.7 0.7 %copy-done.11 = f32[2]{0:T(128)S(1)} copy-done((f32[2]{0:T(128)S(1)}, f32[2]{0:T(128)}, u32[]{:S(2)}) %copy-start.11) | copy-done | bytes 32
  25.4 0.7 %copy-done.12 = f32[128]{0:T(128)S(1)} copy-done((f32[128]{0:T(128)S(1)}, f32[128]{0:T(128)}, u32[]{:S(2)}) %copy-start.12) | copy-done | bytes 536
  26.0 0.7 %copy-done.13 = s32[128]{0:T(128)S(1)} copy-done((s32[128]{0:T(128)S(1)}, s32[128]{0:T(128)}, u32[]{:S(2)}) %copy-start.13) | copy-done | bytes 536
  26.7 1.6 %owner_payloads.1 = (bf16[240,128]{1,0:T(8,128)(2,1)S(1)}, bf16[240,128]{1,0:T(8,128)(2,1)S(1)}, bf16[240,128]{1,0:T(8,128)(2,1)S(1)}, bf16[240,128]{1,0:T(8,128)(2,1)S(1)}, s32[2,8]{1,0:T(2,128)S(1)}) custom-call(s32[2]{0:T(128)S(1)} %copy-done.8, f32[2]{0:T(128)S(1)} %copy-done.11, bf16[1024,128]{1,0:T(8,128)(2,1)S(1)} %delay_coefficients.1.refs_0_, ...), custom_call_target="tpu_custom_call" | custom-call | flops 134217728 | bytes 2097152 | tf_op jit(solution)/shard_map/owner_payloads/pallas_call | solution.py:267
  28.3 0.7 %collective-permute-start.1 = (bf16[240,128]{1,0:T(8,128)(2,1)S(1)}, bf16[240,128]{1,0:T(8,128)(2,1)S(1)}, u32[]{:S(2)}, u32[]{:S(2)}) collective-permute-start(bf16[240,128]{1,0:T(8,128)(2,1)S(1)} %get-tuple-element.11), channel_id=1, source_target_pairs={{0,0},{1,9},{2,2},{3,11},{4,4},{5,13},{6,6},{7,15},{8,8},{9,1},{10... | collective-permute-start | bytes 184328 | tf_op jit(solution)/shard_map/ppermute | solution.py:605
  28.9 0.6 %collective-permute-start.2 = (bf16[240,128]{1,0:T(8,128)(2,1)S(1)}, bf16[240,128]{1,0:T(8,128)(2,1)S(1)}, u32[]{:S(2)}, u32[]{:S(2)}) collective-permute-start(bf16[240,128]{1,0:T(8,128)(2,1)S(1)} %get-tuple-element.12), channel_id=1, source_target_pairs={{0,2},{1,11},{2,0},{3,9},{4,6},{5,15},{6,4},{7,13},{8,10},{9,3},{1... | collective-permute-start | bytes 184328 | tf_op jit(solution)/shard_map/ppermute | solution.py:605
  29.5 2.3 %collective-permute-start.3 = (bf16[240,128]{1,0:T(8,128)(2,1)S(1)}, bf16[240,128]{1,0:T(8,128)(2,1)S(1)}, u32[]{:S(2)}, u32[]{:S(2)}) collective-permute-start(bf16[240,128]{1,0:T(8,128)(2,1)S(1)} %get-tuple-element.13), channel_id=1, source_target_pairs={{0,4},{1,13},{2,6},{3,15},{4,0},{5,9},{6,2},{7,11},{8,12},{9,5},{1... | collective-permute-start | bytes 184328 | tf_op jit(solution)/shard_map/ppermute | solution.py:605
  31.9 1.0 %collective-permute-start.4 = (bf16[240,128]{1,0:T(8,128)(2,1)S(1)}, bf16[240,128]{1,0:T(8,128)(2,1)S(1)}, u32[]{:S(2)}, u32[]{:S(2)}) collective-permute-start(bf16[240,128]{1,0:T(8,128)(2,1)S(1)} %get-tuple-element.14), channel_id=1, source_target_pairs={{0,6},{1,15},{2,4},{3,13},{4,2},{5,11},{6,0},{7,9},{8,14},{9,7},{1... | collective-permute-start | bytes 184328 | tf_op jit(solution)/shard_map/ppermute | solution.py:605
  32.9 5.3 %collective-permute-start.5 = (bf16[240,128]{1,0:T(8,128)(2,1)S(1)}, bf16[240,128]{1,0:T(8,128)(2,1)S(1)}, u32[]{:S(2)}, u32[]{:S(2)}) collective-permute-start(bf16[240,128]{1,0:T(8,128)(2,1)S(1)} %collective-permute-done.1.refs_0_), channel_id=1, source_target_pairs={{0,1},{1,0},{2,3},{3,2},{4,5},{5,4},{6,7},{7,6},{8,9},{9,8},{10,11... | collective-permute-start | bytes 184328 | tf_op jit(solution)/shard_map/ppermute | solution.py:586
  38.2 0.7 %collective-permute-start.6 = (bf16[240,128]{1,0:T(8,128)(2,1)S(1)}, bf16[240,128]{1,0:T(8,128)(2,1)S(1)}, u32[]{:S(2)}, u32[]{:S(2)}) collective-permute-start(bf16[240,128]{1,0:T(8,128)(2,1)S(1)} %collective-permute-done.2.refs_1_), channel_id=1, source_target_pairs={{0,1},{1,0},{2,3},{3,2},{4,5},{5,4},{6,7},{7,6},{8,9},{9,8},{10,11... | collective-permute-start | bytes 184328 | tf_op jit(solution)/shard_map/ppermute | solution.py:586
  38.9 0.2 collective-permute-start.7
  39.1 1.5 %collective-permute-start.8 = (bf16[240,128]{1,0:T(8,128)(2,1)S(1)}, bf16[240,128]{1,0:T(8,128)(2,1)S(1)}, u32[]{:S(2)}, u32[]{:S(2)}) collective-permute-start(bf16[240,128]{1,0:T(8,128)(2,1)S(1)} %collective-permute-done.4.refs_3_), channel_id=1, source_target_pairs={{0,1},{1,0},{2,3},{3,2},{4,5},{5,4},{6,7},{7,6},{8,9},{9,8},{10,11... | collective-permute-start | bytes 184328 | tf_op jit(solution)/shard_map/ppermute | solution.py:586
  40.6 0.9 %collective-permute-done.8.refs_7_ = bf16[240,128]{1,0:T(8,128)(2,1)S(1)} collective-permute-done((bf16[240,128]{1,0:T(8,128)(2,1)S(1)}, bf16[240,128]{1,0:T(8,128)(2,1)S(1)}, u32[]{:S(2)}, u32[]{:S(2)}) %collective-permute-start.8) | collective-permute-done | bytes 61472 | tf_op jit(solution)/shard_map/ppermute | solution.py:586
  41.4 1.4 %copy-done.2 = bf16[2,384,1024]{2,1,0:T(8,128)(2,1)S(1)} copy-done((bf16[2,384,1024]{2,1,0:T(8,128)(2,1)S(1)}, bf16[2,384,1024]{2,1,0:T(8,128)(2,1)}, u32[]{:S(2)}) %copy-start.2) | copy-done | bytes 1572888
  42.8 0.7 %copy-done.9 = s32[2]{0:T(128)S(1)} copy-done((s32[2]{0:T(128)S(1)}, s32[2]{0:T(128)}, u32[]{:S(2)}) %copy-start.9) | copy-done | bytes 32
  43.5 13.7 %owner_estimates.1 = f32[4,8,4,2,1024]{4,3,2,1,0:T(2,128)} custom-call(s32[2]{0:T(128)S(1)} %copy-done.9, s32[2,8]{1,0:T(2,128)S(1)} %get-tuple-element.10.slots, bf16[240,128]{1,0:T(8,128)(2,1)S(1)} %collective-permute-done.1.refs_0_, bf16[240,128]{1,0:T(8,128)(2,1)S(1)} %collective-permute-done.2.refs_1_, ...), custom_call_target="tpu_custom_call" | custom-call | flops 1073741824 | bytes 8388608 | tf_op jit(solution)/shard_map/owner_estimates/pallas_call | solution.py:525
  (33 shorter events, 0.1 us)
Async XLA Ops:
  0.1 2.2 %copy-start = (bf16[2,4,2,128,1024]{4,3,2,1,0:T(8,128)(2,1)S(1)}, bf16[2,4,2,128,1024]{4,3,2,1,0:T(8,128)(2,1)}, u32[]{:S(2)}) copy-start(bf16[2,4,2,128,1024]{4,3,2,1,0:T(8,128)(2,1)} %guesses.1) | copy-start | bytes 12582916
  2.3 1.2 %copy-start.3 = (bf16[2,2,1024,128]{3,2,1,0:T(8,128)(2,1)S(1)}, bf16[2,2,1024,128]{3,2,1,0:T(8,128)(2,1)}, u32[]{:S(2)}) copy-start(bf16[2,2,1024,128]{3,2,1,0:T(8,128)(2,1)} %constant.16.clone.table) | copy-start | bytes 3145732
  3.5 2.3 %copy-start.7 = (s32[2]{0:T(128)}, s32[2]{0:T(128)S(1)}, u32[]{:S(2)}) copy-start(s32[2]{0:T(128)S(1)} %pad_add_fusion.ids) | copy-start | bytes 28
  3.5 2.9 %copy-start.4 = (bf16[2,4,2,4,1024]{4,3,2,1,0:T(4,128)(2,1)S(1)}, bf16[2,4,2,4,1024]{4,3,2,1,0:T(4,128)(2,1)}, u32[]{:S(2)}) copy-start(bf16[2,4,2,4,1024]{4,3,2,1,0:T(4,128)(2,1)} %refs_8_.1) | copy-start | bytes 393220
  3.5 19.0 %copy-start.6 = (s32[16,16]{1,0:T(8,128)S(1)}, s32[16,16]{1,0:T(8,128)}, u32[]{:S(2)}) copy-start(s32[16,16]{1,0:T(8,128)} %refs_5_.1) | copy-start | bytes 3076
  3.5 37.9 %copy-start.1 = (bf16[2,256,2048]{2,1,0:T(8,128)(2,1)S(1)}, bf16[2,256,2048]{2,1,0:T(8,128)(2,1)}, u32[]{:S(2)}) copy-start(bf16[2,256,2048]{2,1,0:T(8,128)(2,1)} %constant.19.clone.refs_17_) | copy-start | bytes 6291460
  5.8 16.6 %collective-permute-start = (bf16[1024,128]{1,0:T(8,128)(2,1)S(1)}, bf16[1024,128]{1,0:T(8,128)(2,1)S(1)}, u32[]{:S(2)}, u32[]{:S(2)}) collective-permute-start(bf16[1024,128]{1,0:T(8,128)(2,1)S(1)} %delay_coefficients.1.refs_0_), channel_id=1, source_target_pairs={{0,1},{1,0},{2,3},{3,2},{4,5},{5,4},{6,7},{7,6},{8,9},{9,8},{10,11... | collective-permute-start | bytes 786440 | tf_op jit(solution)/shard_map/ppermute | solution.py:586
  6.3 10.9 %collective-permute-start.12 = (bf16[2,4,2,4,1024]{4,3,2,1,0:T(4,128)(2,1)S(1)}, bf16[2,4,2,4,1024]{4,3,2,1,0:T(4,128)(2,1)S(1)}, u32[]{:S(2)}, u32[]{:S(2)}) collective-permute-start(bf16[2,4,2,4,1024]{4,3,2,1,0:T(4,128)(2,1)S(1)} %copy-done.4), channel_id=1, source_target_pairs={{0,8},{2,10},{4,12},{6,14},{8,0},{10,2},{12,4},{14,6},{1,9},{3,11}... | collective-permute-start | bytes 393224 | tf_op jit(solution)/shard_map/ppermute | solution.py:583
  10.0 8.9 %collective-permute-start.10 = (bf16[2,4,2,4,1024]{4,3,2,1,0:T(4,128)(2,1)S(1)}, bf16[2,4,2,4,1024]{4,3,2,1,0:T(4,128)(2,1)S(1)}, u32[]{:S(2)}, u32[]{:S(2)}) collective-permute-start(bf16[2,4,2,4,1024]{4,3,2,1,0:T(4,128)(2,1)S(1)} %copy-done.4), channel_id=1, source_target_pairs={{0,4},{2,6},{4,0},{6,2},{8,12},{10,14},{12,8},{14,10},{1,5},{3,7},... | collective-permute-start | bytes 393224 | tf_op jit(solution)/shard_map/ppermute | solution.py:583
  11.6 9.4 %collective-permute-start.14 = (bf16[2,4,2,4,1024]{4,3,2,1,0:T(4,128)(2,1)S(1)}, bf16[2,4,2,4,1024]{4,3,2,1,0:T(4,128)(2,1)S(1)}, u32[]{:S(2)}, u32[]{:S(2)}) collective-permute-start(bf16[2,4,2,4,1024]{4,3,2,1,0:T(4,128)(2,1)S(1)} %copy-done.4), channel_id=1, source_target_pairs={{0,12},{2,14},{4,8},{6,10},{8,4},{10,6},{12,0},{14,2},{1,13},{3,15... | collective-permute-start | bytes 393224 | tf_op jit(solution)/shard_map/ppermute | solution.py:583
  11.6 17.3 %collective-permute-start.9 = (bf16[2,4,2,4,1024]{4,3,2,1,0:T(4,128)(2,1)S(1)}, bf16[2,4,2,4,1024]{4,3,2,1,0:T(4,128)(2,1)S(1)}, u32[]{:S(2)}, u32[]{:S(2)}) collective-permute-start(bf16[2,4,2,4,1024]{4,3,2,1,0:T(4,128)(2,1)S(1)} %copy-done.4), channel_id=1, source_target_pairs={{0,2},{2,0},{4,6},{6,4},{8,10},{10,8},{12,14},{14,12},{1,3},{3,1},... | collective-permute-start | bytes 393224 | tf_op jit(solution)/shard_map/ppermute | solution.py:583
  17.2 12.3 %collective-permute-start.13 = (bf16[2,4,2,4,1024]{4,3,2,1,0:T(4,128)(2,1)S(1)}, bf16[2,4,2,4,1024]{4,3,2,1,0:T(4,128)(2,1)S(1)}, u32[]{:S(2)}, u32[]{:S(2)}) collective-permute-start(bf16[2,4,2,4,1024]{4,3,2,1,0:T(4,128)(2,1)S(1)} %collective-permute-done.12.refs_12_), channel_id=1, source_target_pairs={{0,2},{2,0},{4,6},{6,4},{8,10},{10,8},{12,14},{14,12},{1,3},{3,1},... | collective-permute-start | bytes 393224 | tf_op jit(solution)/shard_map/ppermute | solution.py:583
  19.0 12.9 %collective-permute-start.11 = (bf16[2,4,2,4,1024]{4,3,2,1,0:T(4,128)(2,1)S(1)}, bf16[2,4,2,4,1024]{4,3,2,1,0:T(4,128)(2,1)S(1)}, u32[]{:S(2)}, u32[]{:S(2)}) collective-permute-start(bf16[2,4,2,4,1024]{4,3,2,1,0:T(4,128)(2,1)S(1)} %collective-permute-done.10.refs_10_), channel_id=1, source_target_pairs={{0,2},{2,0},{4,6},{6,4},{8,10},{10,8},{12,14},{14,12},{1,3},{3,1},... | collective-permute-start | bytes 393224 | tf_op jit(solution)/shard_map/ppermute | solution.py:583
  20.9 19.6 %collective-permute-start.15 = (bf16[2,4,2,4,1024]{4,3,2,1,0:T(4,128)(2,1)S(1)}, bf16[2,4,2,4,1024]{4,3,2,1,0:T(4,128)(2,1)S(1)}, u32[]{:S(2)}, u32[]{:S(2)}) collective-permute-start(bf16[2,4,2,4,1024]{4,3,2,1,0:T(4,128)(2,1)S(1)} %collective-permute-done.14.refs_14_), channel_id=1, source_target_pairs={{0,2},{2,0},{4,6},{6,4},{8,10},{10,8},{12,14},{14,12},{1,3},{3,1},... | collective-permute-start | bytes 393224 | tf_op jit(solution)/shard_map/ppermute | solution.py:583
  22.5 0.9 %copy-start.5 = (bf16[256,256]{1,0:T(8,128)(2,1)S(1)}, bf16[256,256]{1,0:T(8,128)(2,1)}, u32[]{:S(2)}) copy-start(bf16[256,256]{1,0:T(8,128)(2,1)} %constant.17.clone.refs_7_) | copy-start | bytes 393220
  23.4 0.7 %copy-start.8 = (s32[2]{0:T(128)S(1)}, s32[2]{0:T(128)}, u32[]{:S(2)}) copy-start(s32[2]{0:T(128)} %copy-done.7) | copy-start | bytes 28
  24.0 0.7 %copy-start.10 = (f32[2,128]{1,0:T(2,128)S(1)}, f32[2,128]{1,0:T(2,128)}, u32[]{:S(2)}) copy-start(f32[2,128]{1,0:T(2,128)} %refs_3_.1) | copy-start | bytes 3076
  24.7 0.7 %copy-start.11 = (f32[2]{0:T(128)S(1)}, f32[2]{0:T(128)}, u32[]{:S(2)}) copy-start(f32[2]{0:T(128)} %noise.1) | copy-start | bytes 28
  25.4 0.7 %copy-start.12 = (f32[128]{0:T(128)S(1)}, f32[128]{0:T(128)}, u32[]{:S(2)}) copy-start(f32[128]{0:T(128)} %param.14) | copy-start | bytes 1540
  26.0 0.7 %copy-start.13 = (s32[128]{0:T(128)S(1)}, s32[128]{0:T(128)}, u32[]{:S(2)}) copy-start(s32[128]{0:T(128)} %param.17) | copy-start | bytes 1540
  28.3 4.6 %collective-permute-start.1 = (bf16[240,128]{1,0:T(8,128)(2,1)S(1)}, bf16[240,128]{1,0:T(8,128)(2,1)S(1)}, u32[]{:S(2)}, u32[]{:S(2)}) collective-permute-start(bf16[240,128]{1,0:T(8,128)(2,1)S(1)} %get-tuple-element.11), channel_id=1, source_target_pairs={{0,0},{1,9},{2,2},{3,11},{4,4},{5,13},{6,6},{7,15},{8,8},{9,1},{10... | collective-permute-start | bytes 184328 | tf_op jit(solution)/shard_map/ppermute | solution.py:605
  28.9 9.2 %collective-permute-start.2 = (bf16[240,128]{1,0:T(8,128)(2,1)S(1)}, bf16[240,128]{1,0:T(8,128)(2,1)S(1)}, u32[]{:S(2)}, u32[]{:S(2)}) collective-permute-start(bf16[240,128]{1,0:T(8,128)(2,1)S(1)} %get-tuple-element.12), channel_id=1, source_target_pairs={{0,2},{1,11},{2,0},{3,9},{4,6},{5,15},{6,4},{7,13},{8,10},{9,3},{1... | collective-permute-start | bytes 184328 | tf_op jit(solution)/shard_map/ppermute | solution.py:605
  29.5 9.3 %collective-permute-start.3 = (bf16[240,128]{1,0:T(8,128)(2,1)S(1)}, bf16[240,128]{1,0:T(8,128)(2,1)S(1)}, u32[]{:S(2)}, u32[]{:S(2)}) collective-permute-start(bf16[240,128]{1,0:T(8,128)(2,1)S(1)} %get-tuple-element.13), channel_id=1, source_target_pairs={{0,4},{1,13},{2,6},{3,15},{4,0},{5,9},{6,2},{7,11},{8,12},{9,5},{1... | collective-permute-start | bytes 184328 | tf_op jit(solution)/shard_map/ppermute | solution.py:605
  31.9 7.2 %collective-permute-start.4 = (bf16[240,128]{1,0:T(8,128)(2,1)S(1)}, bf16[240,128]{1,0:T(8,128)(2,1)S(1)}, u32[]{:S(2)}, u32[]{:S(2)}) collective-permute-start(bf16[240,128]{1,0:T(8,128)(2,1)S(1)} %get-tuple-element.14), channel_id=1, source_target_pairs={{0,6},{1,15},{2,4},{3,13},{4,2},{5,11},{6,0},{7,9},{8,14},{9,7},{1... | collective-permute-start | bytes 184328 | tf_op jit(solution)/shard_map/ppermute | solution.py:605
  32.9 7.7 %collective-permute-start.5 = (bf16[240,128]{1,0:T(8,128)(2,1)S(1)}, bf16[240,128]{1,0:T(8,128)(2,1)S(1)}, u32[]{:S(2)}, u32[]{:S(2)}) collective-permute-start(bf16[240,128]{1,0:T(8,128)(2,1)S(1)} %collective-permute-done.1.refs_0_), channel_id=1, source_target_pairs={{0,1},{1,0},{2,3},{3,2},{4,5},{5,4},{6,7},{7,6},{8,9},{9,8},{10,11... | collective-permute-start | bytes 184328 | tf_op jit(solution)/shard_map/ppermute | solution.py:586
  38.2 2.4 %collective-permute-start.6 = (bf16[240,128]{1,0:T(8,128)(2,1)S(1)}, bf16[240,128]{1,0:T(8,128)(2,1)S(1)}, u32[]{:S(2)}, u32[]{:S(2)}) collective-permute-start(bf16[240,128]{1,0:T(8,128)(2,1)S(1)} %collective-permute-done.2.refs_1_), channel_id=1, source_target_pairs={{0,1},{1,0},{2,3},{3,2},{4,5},{5,4},{6,7},{7,6},{8,9},{9,8},{10,11... | collective-permute-start | bytes 184328 | tf_op jit(solution)/shard_map/ppermute | solution.py:586
  38.9 1.7 %collective-permute-start.7 = (bf16[240,128]{1,0:T(8,128)(2,1)S(1)}, bf16[240,128]{1,0:T(8,128)(2,1)S(1)}, u32[]{:S(2)}, u32[]{:S(2)}) collective-permute-start(bf16[240,128]{1,0:T(8,128)(2,1)S(1)} %collective-permute-done.3.refs_2_), channel_id=1, source_target_pairs={{0,1},{1,0},{2,3},{3,2},{4,5},{5,4},{6,7},{7,6},{8,9},{9,8},{10,11... | collective-permute-start | bytes 184328 | tf_op jit(solution)/shard_map/ppermute | solution.py:586
  39.1 2.4 %collective-permute-start.8 = (bf16[240,128]{1,0:T(8,128)(2,1)S(1)}, bf16[240,128]{1,0:T(8,128)(2,1)S(1)}, u32[]{:S(2)}, u32[]{:S(2)}) collective-permute-start(bf16[240,128]{1,0:T(8,128)(2,1)S(1)} %collective-permute-done.4.refs_3_), channel_id=1, source_target_pairs={{0,1},{1,0},{2,3},{3,2},{4,5},{5,4},{6,7},{7,6},{8,9},{9,8},{10,11... | collective-permute-start | bytes 184328 | tf_op jit(solution)/shard_map/ppermute | solution.py:586
  41.4 1.4 %copy-start.2 = (bf16[2,384,1024]{2,1,0:T(8,128)(2,1)S(1)}, bf16[2,384,1024]{2,1,0:T(8,128)(2,1)}, u32[]{:S(2)}) copy-start(bf16[2,384,1024]{2,1,0:T(8,128)(2,1)} %constant.18.clone.refs_16_) | copy-start | bytes 4718596
  42.8 0.7 %copy-start.9 = (s32[2]{0:T(128)S(1)}, s32[2]{0:T(128)}, u32[]{:S(2)}) copy-start(s32[2]{0:T(128)} %copy-done.7) | copy-start | bytes 28

commit v2 on v1

v2 whole, which is shorter than its diff:
```python
import functools
import math

import jax
import jax.numpy as jnp
import ml_dtypes
import numpy as np
from jax import lax
from jax.experimental import pallas as pl
from jax.experimental.pallas import tpu as pltpu
from jax.sharding import PartitionSpec as P

TONE_NUMBER = 2048
TAPS = 64
CU = 8
OWN_MAX = 4
PEER_MAX = 2
SAMPLES = 2 * TAPS
ROWS = PEER_MAX * CU
LARGE_BYTES = 58 * 1024 * 1024
VMEM_BYTES = 36 * 1024 * 1024
F32 = jnp.float32
BF16 = jnp.bfloat16


def np_parts(values, count):
    parts = []
    rest = values.astype(np.float64)
    for _ in range(count):
        part = rest.astype(np.float32).astype(ml_dtypes.bfloat16)
        parts.append(part)
        rest = rest - part.astype(np.float64)
    return parts


def np_angles(tones):
    turns = (tones[:, None] * np.arange(TAPS)[None, :]) % TONE_NUMBER
    return turns.astype(np.float64) * (2.0 * math.pi / TONE_NUMBER)


def forward_tables(shards, width):
    angles = np_angles(np.arange(shards * width))
    cosine = np.cos(angles).astype(np.float32).astype(ml_dtypes.bfloat16)
    sine = np.sin(angles).astype(np.float32).astype(ml_dtypes.bfloat16)
    real = np.concatenate([cosine, sine], axis=1).reshape(shards, width, 2 * TAPS)
    imag = np.concatenate([-sine, cosine], axis=1).reshape(shards, width, 2 * TAPS)
    return np.stack([real, imag], axis=1)


def rebuild_columns(tones):
    angles = np_angles(tones).T
    real = np.concatenate([np.cos(angles), np.sin(angles)], axis=0)
    imag = np.concatenate([-np.sin(angles), np.cos(angles)], axis=0)
    return (
        np.concatenate(np_parts(real, 2), axis=0),
        np.concatenate(np_parts(imag, 2), axis=0),
    )


def rebuild_tables(shards, width, chunk):
    real, imag = rebuild_columns(np.arange(shards * width))
    real = real.reshape(4 * TAPS, shards, width // chunk, 1, chunk)
    imag = imag.reshape(4 * TAPS, shards, width // chunk, 1, chunk)
    both = np.concatenate([real, imag], axis=3).reshape(4 * TAPS, shards, 2 * width)
    return np.ascontiguousarray(both.transpose(1, 0, 2))


def sample_table():
    real, imag = rebuild_columns(np.arange(SAMPLES) * (TONE_NUMBER // SAMPLES))
    return np.concatenate([real, imag], axis=1)


def dirichlet_tables(shards, width):
    step = TONE_NUMBER // SAMPLES
    wave = np.ones((TONE_NUMBER,), np.float64)
    tones = np.arange(TONE_NUMBER)
    for lag in range(1, TAPS):
        wave += 2.0 * np.cos(2.0 * math.pi * ((lag * tones) % TONE_NUMBER) / TONE_NUMBER)
    wave /= SAMPLES
    gap = (np.arange(shards * width)[None, :] - step * np.arange(SAMPLES)[:, None]) % TONE_NUMBER
    kernel = wave[gap]
    parts = np.concatenate(np_parts(kernel, 3), axis=0)
    parts = parts.reshape(3 * SAMPLES, shards, width)
    return np.ascontiguousarray(parts.transpose(1, 0, 2))


def three_parts(values):
    high = values.astype(BF16)
    rest = values - high.astype(F32)
    middle = rest.astype(BF16)
    low = (rest - middle.astype(F32)).astype(BF16)
    return high, middle, low


def iota(shape, axis):
    return lax.broadcasted_iota(jnp.int32, shape, axis)


def column_of(row):
    n = row.shape[1]
    return jnp.sum(jnp.where(iota((n, n), 0) == iota((n, n), 1), row, 0.0), axis=1, keepdims=True)


def row_of(column):
    n = column.shape[0]
    return jnp.sum(
        jnp.where(iota((n, n), 0) == iota((n, n), 1), column, 0.0), axis=0, keepdims=True
    )


def find_routes(shape, power, noise, gain, cluster_row, serving, owner, pick_out, weight_out, slots, extras):
    aps, antennas, users, devices, shards = shape
    per = devices // shards
    device, core = lax.axis_index("ap"), lax.axis_index("sc")
    clusters = serving.shape[0]
    extras[pl.ds(0, users), :] = jnp.broadcast_to(
        column_of(power[...]) * (1.0 / users), (users, SAMPLES)
    )
    for a in range(aps):
        extras[pl.ds(users + a, 1), :] = jnp.broadcast_to(noise[:, a : a + 1], (1, SAMPLES))

    serving_f = serving[...].astype(F32)
    columns = serving.shape[1]
    pairs = (iota((columns, devices), 0) // aps == iota((columns, devices), 1)).astype(F32)
    served = (jnp.dot(serving_f, pairs, preferred_element_type=F32) > 0.5).astype(F32)
    served_here = jnp.sum(
        jnp.where(iota((clusters, devices), 1) == device, served, 0.0), axis=1, keepdims=True
    )
    owner_row = owner[...].astype(F32)
    owner_f = column_of(owner_row)
    owner_col = owner_f.astype(jnp.int32)
    square = (clusters, clusters)
    before = iota(square, 1) < iota(square, 0)
    earlier = before & (owner_f == owner_row)
    turn = jnp.sum(jnp.where(earlier, row_of(served_here), 0.0), axis=1, keepdims=True)
    label = (owner_col ^ device) ^ (core * per)
    valid = (served_here > 0.5) & (label < per)
    base = jnp.where(valid, label.astype(F32) * ROWS + turn * CU, -4.0 * ROWS * devices)
    members = (iota((clusters, users), 0) == cluster_row[...]).astype(F32)
    prefix = (iota((users, users), 0) < iota((users, users), 1)).astype(F32)
    order = jnp.dot(members, prefix, preferred_element_type=F32)
    target = jnp.sum(members * (order + base), axis=0, keepdims=True).astype(jnp.int32)
    pick = (iota((per * ROWS, users), 0) == target).astype(F32).astype(BF16)
    pick_out[...] = pick

    weight_rows = []
    for a in range(aps):
        column = iota((clusters, columns), 1) == device * aps + a
        mine = jnp.sum(jnp.where(column, serving_f, 0.0), axis=1, keepdims=True)
        weight_rows.append(
            jnp.sum(members * mine, axis=0, keepdims=True) * gain[pl.ds(a, 1), :]
        )
    stacked = jnp.concatenate(weight_rows + [jnp.zeros((8 - aps, users), F32)], axis=0)
    weight_parts = jnp.concatenate(
        [part.astype(F32) for part in three_parts(stacked)]
        + [jnp.zeros((2 * TAPS - 24, users), F32)],
        axis=0,
    ).astype(BF16)
    weight_out[...] = lax.dot_general(
        pick, weight_parts, (((1,), (1,)), ((), ())), preferred_element_type=F32
    ).astype(BF16)

    mine = (owner_col == device).astype(F32)
    rank = jnp.sum(jnp.where(before, row_of(mine), 0.0), axis=1, keepdims=True)
    here = mine * served
    turns = jnp.dot(before.astype(F32), here, preferred_element_type=F32)
    for p in range(PEER_MAX):
        hit = jnp.where(turns == float(p), here, 0.0)
        slots[pl.ds(p, 1), :] = jnp.sum(hit * rank, axis=0, keepdims=True).astype(jnp.int32)


def coefficient_kernel(shape, *refs):
    aps, antennas, users, devices, shards = shape
    guesses, table, samples = refs[:3]
    small = refs[3:9]
    out, samples_out, pick, weights, slots, extras = refs[9:15]
    held, tables, *held_small = refs[15:23]
    held_sem, table_sem, small_sem = refs[23:]
    small_copies = [
        pltpu.make_async_copy(src, dst, small_sem.at[k])
        for k, (src, dst) in enumerate(zip(small, held_small))
    ]
    table_copy = pltpu.make_async_copy(table.at[lax.axis_index("sc")], tables, table_sem.at[0])
    sample_copy = pltpu.make_async_copy(samples, samples_out, table_sem.at[1])
    big = [
        pltpu.make_async_copy(guesses.at[a, i], held.at[a * antennas + i], held_sem.at[a * antennas + i])
        for a in range(aps)
        for i in range(antennas)
    ]
    for copy in small_copies + [table_copy] + big + [sample_copy]:
        copy.start()
    for copy in small_copies:
        copy.wait()
    find_routes(shape, *held_small, pick, weights, slots, extras)
    table_copy.wait()
    group = math.gcd(2, antennas)
    tones = held.shape[-1]
    for first in range(0, aps * antennas, group):
        for k in range(group):
            big[first + k].wait()
        real = held[pl.ds(first, group), 0].reshape(group * users, tones)
        imag = held[pl.ds(first, group), 1].reshape(group * users, tones)
        total = jnp.dot(real, tables[0], preferred_element_type=F32)
        total = total + jnp.dot(imag, tables[1], preferred_element_type=F32)
        out[pl.ds(first * users, group * users), :] = (total * (1.0 / TONE_NUMBER)).astype(BF16)
    sample_copy.wait()


def delay_coefficients(guesses, power, noise, gain, cluster, serving, owner, shape):
    aps, antennas, users, devices, shards = shape
    per = devices // shards
    tones = guesses.shape[-1]
    clusters = serving.shape[0]
    table = jnp.asarray(forward_tables(shards, tones))
    samples = jnp.asarray(sample_table())
    small = [
        power.reshape(1, users), noise.reshape(1, aps), gain, cluster.reshape(1, users), serving,
        owner.reshape(1, clusters),
    ]
    hbm = pl.BlockSpec(memory_space=pltpu.HBM)
    vmem = pl.BlockSpec(memory_space=pltpu.VMEM)
    return pl.pallas_call(
        functools.partial(coefficient_kernel, shape),
        in_specs=[hbm] * (3 + len(small)),
        out_specs=[vmem] * 6,
        out_shape=[
            jax.ShapeDtypeStruct((aps * antennas * users, 2 * TAPS), BF16),
            jax.ShapeDtypeStruct(samples.shape, BF16),
            jax.ShapeDtypeStruct((per * ROWS, users), BF16),
            jax.ShapeDtypeStruct((per * ROWS, 2 * TAPS), BF16),
            jax.ShapeDtypeStruct((PEER_MAX, devices), jnp.int32),
            jax.ShapeDtypeStruct((users + 8, SAMPLES), F32),
        ],
        scratch_shapes=[
            pltpu.VMEM((aps * antennas, 2, users, tones), BF16),
            pltpu.VMEM((2, tones, 2 * TAPS), BF16),
        ]
        + [pltpu.VMEM(x.shape, x.dtype) for x in small]
        + [
            pltpu.SemaphoreType.DMA((aps * antennas,)),
            pltpu.SemaphoreType.DMA((2,)),
            pltpu.SemaphoreType.DMA((len(small),)),
        ],
        compiler_params=pltpu.CompilerParams(vmem_limit_bytes=LARGE_BYTES),
        cost_estimate=pl.CostEstimate(
            flops=4 * guesses.size * TAPS, bytes_accessed=2 * guesses.size, transcendentals=0
        ),
        name="delay_coefficients",
    )(guesses, table, samples, *small)


def payload_kernel(shape, *refs):
    aps, antennas, users, devices, shards = shape
    per = devices // shards
    parts = refs[:shards]
    table, pick, weights, extras = refs[shards : shards + 4]
    outs = refs[shards + 4 : shards + 4 + per]
    coef, smooth, cov = refs[shards + 4 + per :]

    total = parts[0][...].astype(F32)
    for part in parts[1:]:
        total = total + part[...].astype(F32)
    coef_b = total.astype(BF16)
    coef[:, : 2 * TAPS] = coef_b
    coef[:, 2 * TAPS :] = coef_b

    smooth[...] = jnp.dot(coef[...], table[...], preferred_element_type=F32)
    for a in range(aps):
        base = a * antennas * users
        sums = {}
        for start in range(0, users, 8):
            re, im = [], []
            for i in range(antennas):
                rows = smooth[pl.ds(base + i * users + start, 8), :]
                re.append(rows[:, :SAMPLES])
                im.append(rows[:, SAMPLES:])
            weight = extras[pl.ds(start, 8), :]
            for i in range(antennas):
                sre, sim = re[i] * weight, im[i] * weight
                for j in range(i + 1):
                    value = sre * re[j] + sim * im[j]
                    sums[i, j, 0] = sums[i, j, 0] + value if start else value
                    if j < i:
                        value = sim * re[j] - sre * im[j]
                        sums[i, j, 1] = sums[i, j, 1] + value if start else value
        field = 0
        for i in range(antennas):
            for j in range(i + 1):
                for c in range(2 if j < i else 1):
                    row = jnp.sum(sums[i, j, c], axis=0, keepdims=True)
                    if i == j:
                        row = row + extras[pl.ds(users + a, 1), :]
                    cov[pl.ds(a * antennas * antennas + field, 1), :] = row
                    field += 1

    cov_parts = three_parts(cov[...])
    cov_rows = cov.shape[0]
    first = aps * antennas * ROWS
    for ai in range(aps * antennas):
        chosen = jnp.dot(
            pick[...], coef[pl.ds(ai * users, users), : 2 * TAPS], preferred_element_type=F32
        ).astype(BF16)
        for j in range(per):
            outs[j][pl.ds(ai * ROWS, ROWS), :] = chosen[j * ROWS : (j + 1) * ROWS]
    for j in range(per):
        for k in range(3):
            outs[j][pl.ds(first + k * cov_rows, cov_rows), :] = cov_parts[k]
        outs[j][pl.ds(first + 3 * cov_rows, ROWS), :] = weights[pl.ds(j * ROWS, ROWS), :]


def payload_rows(aps, antennas):
    return aps * antennas * ROWS + 3 * aps * antennas * antennas + ROWS


def owner_payloads(parts, table, pick, weights, extras, shape):
    aps, antennas, users, devices, shards = shape
    per = devices // shards
    rows = payload_rows(aps, antennas)
    operands = list(parts) + [table, pick, weights, extras]
    whole = lambda dims: pl.BlockSpec(dims, lambda g: (0,) * len(dims))
    return pl.pallas_call(
        functools.partial(payload_kernel, shape),
        grid=(1,),
        in_specs=[whole(x.shape) for x in operands],
        out_specs=[whole((rows, 2 * TAPS))] * per,
        out_shape=[jax.ShapeDtypeStruct((rows, 2 * TAPS), BF16)] * per,
        scratch_shapes=[
            pltpu.VMEM((aps * antennas * users, 4 * TAPS), BF16),
            pltpu.VMEM((aps * antennas * users, 2 * SAMPLES), F32),
            pltpu.VMEM((aps * antennas * antennas, SAMPLES), F32),
        ],
        compiler_params=pltpu.CompilerParams(vmem_limit_bytes=LARGE_BYTES),
        cost_estimate=pl.CostEstimate(
            flops=4 * aps * antennas * users * 4 * TAPS * SAMPLES,
            bytes_accessed=2 * 1024 * 1024,
            transcendentals=0,
        ),
        name="owner_payloads",
    )(*operands)


def complex_times(left, right):
    return (left[0] * right[0] - left[1] * right[1], left[0] * right[1] + left[1] * right[0])


def times_conj(left, right):
    return (left[0] * right[0] + left[1] * right[1], left[1] * right[0] - left[0] * right[1])


def minus(left, right):
    return (left[0] - right[0], left[1] - right[1])


def factorize(cov, antennas):
    factor, inverse = {}, []
    for j in range(antennas):
        pivot = cov[j, j][0]
        for k in range(j):
            pivot = pivot - (factor[j, k][0] * factor[j, k][0] + factor[j, k][1] * factor[j, k][1])
        root = lax.rsqrt(pivot)
        inverse.append(root)
        for i in range(j + 1, antennas):
            running = cov[i, j]
            for k in range(j):
                running = minus(running, times_conj(factor[i, k], factor[j, k]))
            factor[i, j] = (running[0] * root, running[1] * root)
    return factor, inverse


def substitute(factor, inverse, right):
    antennas = len(inverse)
    forward = []
    for i in range(antennas):
        running = right[i]
        for k in range(i):
            running = minus(running, complex_times(factor[i, k], forward[k]))
        forward.append((running[0] * inverse[i], running[1] * inverse[i]))
    result = [None] * antennas
    for i in range(antennas - 1, -1, -1):
        running = forward[i]
        for k in range(i + 1, antennas):
            running = minus(running, times_conj(result[k], factor[k, i]))
        result[i] = (running[0] * inverse[i], running[1] * inverse[i])
    return result


def estimate_kernel(shape, chunk, labels, first_call, last_call, slots, *refs):
    aps, antennas, symbols, tones, devices, shards = shape
    per = devices // shards
    count = len(labels)
    pays, signals = refs[:count], refs[count : 2 * count]
    refs = refs[2 * count :]
    kernel_table, rebuild_table = refs[:2]
    refs = refs[2:]
    if first_call:
        out, denominator_out = refs[:2]
        refs = refs[2:]
    else:
        acc_in, denominator_in, out = refs[:3]
        refs = refs[3:]
    (
        dirichlet, rebuild, left, cov_full, cov_tiles, sig_tiles, solved, smooth, weight,
        acc, denominator, turned, table_sem,
    ) = refs
    if first_call:
        acc, denominator = out, denominator_out
    device, core = lax.axis_index("ap"), lax.axis_index("sc")
    cov_rows = aps * antennas * antennas
    coef_rows = aps * antennas * ROWS
    blocks = tones // 128

    kernel_copy = pltpu.make_async_copy(kernel_table.at[core], dirichlet, table_sem.at[0])
    rebuild_copy = pltpu.make_async_copy(rebuild_table.at[core], rebuild, table_sem.at[1])
    kernel_copy.start()
    rebuild_copy.start()

    def cov_part(k):
        rows = [pay[pl.ds(coef_rows + k * cov_rows, cov_rows), :] for pay in pays]
        return jnp.concatenate(rows, axis=0)

    kernel_copy.wait()
    high, middle, low = cov_part(0), cov_part(1), cov_part(2)
    n = SAMPLES
    cov_full[...] = (
        jnp.dot(low, dirichlet[:n], preferred_element_type=F32)
        + jnp.dot(
            jnp.concatenate([middle, middle], axis=1), dirichlet[: 2 * n], preferred_element_type=F32
        )
        + jnp.dot(
            jnp.concatenate([high, high, high], axis=1), dirichlet[...], preferred_element_type=F32
        )
    )

    for n, pay in enumerate(pays):
        rows = pay[pl.ds(0, coef_rows), :]
        left[pl.ds(n * coef_rows, coef_rows), : 2 * TAPS] = rows
        left[pl.ds(n * coef_rows, coef_rows), 2 * TAPS :] = rows
        packed = pay[pl.ds(coef_rows + 3 * cov_rows, ROWS), :].astype(F32)
        for a in range(aps):
            value = packed[:, a : a + 1] + packed[:, 8 + a : 9 + a] + packed[:, 16 + a : 17 + a]
            weight[n, a] = jnp.broadcast_to(value, (ROWS, 128))

    if first_call:
        acc[...] = jnp.zeros_like(acc)
        denominator[...] = jnp.ones_like(denominator)
    else:
        acc[...] = acc_in[...]
        denominator[...] = denominator_in[...]

    stride = labels[1] - labels[0]

    def partner(n):
        return (labels[0] + n * stride) ^ (core * per)

    for n, label in enumerate(labels):
        place = (label ^ (core * per)) // stride
        for a in range(aps):
            for i in range(antennas):
                for c in range(2):
                    rows = signals[n][a, i, c].astype(F32)
                    first = ((a * antennas + i) * 2 + c) * symbols * blocks
                    for b in range(blocks):
                        sig_tiles[place, pl.ds(first + b, symbols, stride=blocks), :] = rows[
                            :, b * 128 : (b + 1) * 128
                        ]

    def solve(l, carry):
        for r in range(0, cov_rows, 8):
            rows = cov_full[pl.ds(pl.multiple_of(l * cov_rows + r, 8), 8), :]
            for b in range(blocks):
                cov_tiles[pl.ds(r * blocks + b, 8, stride=blocks), :] = rows[:, b * 128 : (b + 1) * 128]
        for a in range(aps):
            cov = {}
            field = a * antennas * antennas
            for i in range(antennas):
                for j in range(i + 1):
                    parts = []
                    for c in range(2 if j < i else 1):
                        parts.append(cov_tiles[pl.ds(field * blocks, blocks), :])
                        field += 1
                    cov[i, j] = parts
            factor, inverse = factorize(cov, antennas)
            for s in range(symbols):
                right = []
                for i in range(antennas):
                    tiles = [
                        (((a * antennas + i) * 2 + c) * symbols + s) * blocks for c in range(2)
                    ]
                    right.append([sig_tiles[l, pl.ds(t, blocks), :] for t in tiles])
                result = substitute(factor, inverse, right)
                for i in range(antennas):
                    for c in range(2):
                        at = ((a * antennas + i) * symbols + s) * 2 + c
                        solved[l, pl.ds(at * blocks, blocks), :] = result[i][c]
        source = partner(l) ^ device
        for p in range(PEER_MAX):
            k = slots[p, source]
            for a in range(aps):
                denominator[k] = denominator[k] + weight[l, a, pl.ds(p * CU, CU), :]
        return carry

    lax.fori_loop(0, count, solve, 0)
    rebuild_copy.wait()

    def combine(l, q):
        source = partner(l) ^ device
        for h in range(chunk // 128):
            b = q * (chunk // 128) + h
            lanes = pl.ds(pl.multiple_of(b * 128, 128), 128)
            totals = [[None] * (2 * symbols) for p in range(PEER_MAX)]
            for a in range(aps):
                for i in range(antennas):
                    base = pl.multiple_of(l * coef_rows + (a * antennas + i) * ROWS, 8)
                    link = []
                    for p in range(PEER_MAX):
                        scale = weight[l, a, pl.ds(p * CU, CU), :]
                        rows = pl.ds(base + p * CU, CU)
                        link.append(
                            (
                                smooth[rows, h * 128 : (h + 1) * 128] * scale,
                                smooth[rows, chunk + h * 128 : chunk + (h + 1) * 128] * scale,
                            )
                        )
                    for s in range(symbols):
                        at = ((a * antennas + i) * symbols + s) * 2
                        xr = solved[l, pl.ds(at * blocks + b, 1), :]
                        xi = solved[l, pl.ds((at + 1) * blocks + b, 1), :]
                        xr = jnp.broadcast_to(xr, (CU, 128))
                        xi = jnp.broadcast_to(xi, (CU, 128))
                        for p in range(PEER_MAX):
                            gr, gi = link[p]
                            er = gr * xr + gi * xi
                            ei = gr * xi - gi * xr
                            if totals[p][2 * s] is None:
                                totals[p][2 * s], totals[p][2 * s + 1] = er, ei
                            else:
                                totals[p][2 * s] += er
                                totals[p][2 * s + 1] += ei
            for p in range(PEER_MAX):
                k = slots[p, source]
                for e in range(2 * symbols):
                    acc[k, e, :, lanes] = acc[k, e, :, lanes] + totals[p][e]

    def one_chunk(q, carry):
        columns = pl.ds(pl.multiple_of(q * 2 * chunk, 128), 2 * chunk)
        smooth[...] = jnp.dot(left[...], rebuild[:, columns], preferred_element_type=F32)

        def step(l, inner):
            combine(l, q)
            return inner

        lax.fori_loop(0, count, step, 0)
        return carry

    lax.fori_loop(0, tones // chunk, one_chunk, 0)

    if not last_call:
        return

    def finish(k, carry):
        inverse = 1.0 / denominator[k]
        for b in range(blocks):
            for e in range(2 * symbols):
                value = acc[k, e, :, b * 128 : (b + 1) * 128] * inverse
                turned[pl.ds(b * CU * 2 * symbols + e, CU, stride=2 * symbols), :] = value
            for m in range(CU):
                for s in range(symbols):
                    at = ((b * CU + m) * symbols + s) * 2
                    out[k, m, s, :, b * 128 : (b + 1) * 128] = turned[pl.ds(at, 2), :]
        return carry

    lax.fori_loop(0, OWN_MAX, finish, 0)


def owner_estimates(slots, pays, signals, labels, before, last_call, shape):
    aps, antennas, symbols, tones, devices, shards = shape
    chunk = min(256, tones)
    count = len(labels)
    cov_rows = aps * antennas * antennas
    coef_rows = aps * antennas * ROWS
    blocks = tones // 128
    hbm = pl.BlockSpec(memory_space=pltpu.HBM)
    vmem = pl.BlockSpec(memory_space=pltpu.VMEM)
    smem = pl.BlockSpec(memory_space=pltpu.SMEM)
    sums = (OWN_MAX, 2 * symbols, CU, tones)
    bottom = (OWN_MAX, CU, 128)
    first_call = not before
    if last_call:
        outs = [jax.ShapeDtypeStruct((OWN_MAX, CU, symbols, 2, tones), F32)]
    else:
        outs = [jax.ShapeDtypeStruct(sums, F32), jax.ShapeDtypeStruct(bottom, F32)]
    return pl.pallas_call(
        functools.partial(estimate_kernel, shape, chunk, labels, first_call, last_call),
        in_specs=[smem] + [vmem] * (2 * count) + [hbm] * 2 + [vmem] * len(before),
        out_specs=[vmem] * len(outs),
        out_shape=outs,
        scratch_shapes=[
            pltpu.VMEM((3 * SAMPLES, tones), BF16),
            pltpu.VMEM((4 * TAPS, 2 * tones), BF16),
            pltpu.VMEM((count * coef_rows, 4 * TAPS), BF16),
            pltpu.VMEM((count * cov_rows, tones), F32),
            pltpu.VMEM((cov_rows * blocks, 128), F32),
            pltpu.VMEM((count, aps * antennas * 2 * symbols * blocks, 128), F32),
            pltpu.VMEM((count, aps * antennas * 2 * symbols * blocks, 128), F32),
            pltpu.VMEM((count * coef_rows, 2 * chunk), F32),
            pltpu.VMEM((count, aps, ROWS, 128), F32),
            pltpu.VMEM(sums, F32),
            pltpu.VMEM(bottom, F32),
            pltpu.VMEM((CU * 2 * symbols * blocks, 128), F32),
            pltpu.SemaphoreType.DMA((2,)),
        ],
        compiler_params=pltpu.CompilerParams(vmem_limit_bytes=VMEM_BYTES),
        cost_estimate=pl.CostEstimate(
            flops=4 * count * coef_rows * 4 * TAPS * tones,
            bytes_accessed=8 * 1024 * 1024,
            transcendentals=0,
        ),
        name="owner_estimates",
    )(
        slots,
        *pays,
        *signals,
        jnp.asarray(dirichlet_tables(shards, tones)),
        jnp.asarray(rebuild_tables(shards, tones, chunk)),
        *before,
    )


def local(
    unsmoothed_link_guesses,
    received,
    user_power,
    noise_power,
    ap_gain,
    user_cluster,
    serving,
    cluster_owner,
):
    aps, antennas, _, users, tones = unsmoothed_link_guesses.shape
    symbols = received.shape[3]
    devices, shards = lax.axis_size("ap"), lax.axis_size("sc")
    per = devices // shards
    def swap_ap(value, v):
        return lax.ppermute(value, "ap", [(i, i ^ v) for i in range(devices)])

    def swap_sc(value, h):
        return lax.ppermute(value, "sc", [(c, c ^ h) for c in range(shards)])

    signals = [None] * devices
    for v in range(0, devices, 2):
        signals[v] = swap_ap(received, v) if v else received
    signals[1] = swap_ap(received, 1)

    combined, samples, pick, weights, slots, extras = delay_coefficients(
        unsmoothed_link_guesses, user_power, noise_power, ap_gain, user_cluster, serving,
        cluster_owner, (aps, antennas, users, devices, shards),
    )
    parts = [combined] + [swap_sc(combined, h) for h in range(1, shards)]
    blocks = owner_payloads(
        parts, samples, pick, weights, extras, (aps, antennas, users, devices, shards)
    )

    pairs = lambda j: [
        (i * shards + c, (i ^ (c * per + j)) * shards + c)
        for i in range(devices)
        for c in range(shards)
    ]
    own = [lax.ppermute(blocks[j], ("ap", "sc"), pairs(j)) for j in range(per)]
    for v in range(2, devices, 2):
        later, _ = lax.optimization_barrier((signals[v], own[0]))
        signals[v + 1] = swap_ap(later, 1)
    pays = own + [swap_sc(own[j], h) for h in range(1, shards) for j in range(per)]
    shape = (aps, antennas, symbols, tones, devices, shards)
    even, odd = list(range(0, devices, 2)), list(range(1, devices, 2))
    sums = owner_estimates(
        slots, [pays[l] for l in even], [signals[v] for v in even], even, [], False, shape
    )
    return owner_estimates(
        slots, [pays[l] for l in odd], [signals[v] for v in odd], odd, sums, True, shape
    )[0]


def solution(mesh):
    placed = (
        P(("cell", "ap"), None, None, None, "sc"),
        P(("cell", "ap"), None, None, None, "sc"),
        P("cell"),
        P(("cell", "ap")),
        P(("cell", "ap"), None),
        P("cell"),
        P("cell", None),
        P("cell", None),
    )
    return jax.shard_map(
        local,
        mesh=mesh,
        in_specs=placed,
        out_specs=P(("cell", "ap"), None, None, None, "sc"),
        check_vma=False,
    )
```

time: 57.5 us -> 45.2 us (0.79)
  local copies, waits for them, and re-layouts: 10.4 us -> 1.38 us
  starting transfers between devices: 23.3 us -> 19.7 us
  Pallas kernels: 17.6 us -> 20.6 us
  waiting for transfers between devices: 5.76 us -> 3.22 us
    unnamed x29 -> x10, local copies, waits for them, and re-layouts: 10.4 us -> 1.38 us
    ppermute x5, starting transfers between devices: 8.15 us -> 3.22 us  [swap_sc(): return lax.ppermute(value, 'sc', [(c, c ^ h) for c in range(shards)])]
    pallas_call x3 -> x4, Pallas kernels: 17.6 us -> 20.6 us  [the longest x2 13.2 us: owner_estimates(): pl.pallas_call(functools.partial(estimate_kernel, shape, chunk, labels, f...]
    ppermute x7, waiting for transfers between devices: 4.86 us -> 2.37 us  [swap_ap(): return lax.ppermute(value, 'ap', [(i, i ^ v) for i in range(devices)])]
    ppermute x4, starting transfers between devices: 4.6 us -> 7.07 us  [local(): own = [lax.ppermute(blocks[j], ('ap', 'sc'), pairs(j)) for j in range(per)]]
    ppermute x7, starting transfers between devices: 10.5 us -> 9.37 us  [swap_ap(): return lax.ppermute(value, 'ap', [(i, i ^ v) for i in range(devices)])]
  transfers between devices with their start and end apart: 16 -> 16, of which waited for: 3 -> 2; matrix products, arithmetic and copies ran while one was open for 1% -> 0% of each run, Pallas kernels for 3% -> 18%
where the time goes in v2:
time: 45.2 us; the launch traced here: 45 us
  Pallas kernels  20.6 us (46%)
  starting transfers between devices  19.7 us (44%)
  waiting for transfers between devices  3.22 us (7%)
  local copies, waits for them, and re-layouts  1.38 us (3%)
    pallas_call x2, Pallas kernels, owner_estimates(): pl.pallas_call(functools.partial(estimate_kernel, shape, chunk, labels, f...  13.2 us
    ppermute x7, starting transfers between devices, swap_ap(): return lax.ppermute(value, 'ap', [(i, i ^ v) for i in range(devices)])  9.37 us
    ppermute x4, starting transfers between devices, local(): own = [lax.ppermute(blocks[j], ('ap', 'sc'), pairs(j)) for j in range(per)]  7.07 us
    pallas_call x1, Pallas kernels, delay_coefficients(): pl.pallas_call(functools.partial(coefficient_kernel, shape), in_specs=[hb...  5.05 us
    ppermute x5, starting transfers between devices, swap_sc(): return lax.ppermute(value, 'sc', [(c, c ^ h) for c in range(shards)])  3.22 us
    pallas_call x1, Pallas kernels, owner_payloads(): pl.pallas_call(functools.partial(payload_kernel, shape), grid=(1,), in_sp...  2.38 us
    ppermute x7, waiting for transfers between devices, swap_ap(): return lax.ppermute(value, 'ap', [(i, i ^ v) for i in range(devices)])  2.37 us
    unnamed x10, local copies, waits for them, and re-layouts  1.38 us
  transfers between devices with their start and end apart: 16, of which 2 were waited for; matrix products, arithmetic and copies ran while one was open for 0% of the time, Pallas kernels for 18%

profile of v2, /device:TPU:0, one launch (start us, length us, event | category | flops | bytes accessed | tf_op | source)
XLA Modules:
  0.0 45.0 jit_solution(18358086697185298916)
XLA Ops:
  0.0 5.1 %delay_coefficients.1 = (bf16[1024,128]{1,0:T(8,128)(2,1)}, bf16[256,256]{1,0:T(8,128)(2,1)}, bf16[64,128]{1,0:T(8,128)(2,1)}, bf16[64,128]{1,0:T(8,128)(2,1)}, s32[2,8]{1,0:T(2,128)}, /*index=5*/f32[136,128]{1,0:T(8,128)}) custom-call(bf16[2,4,2,128,1024]{4,3,2,1,0:T(8,128)(2,1)} %refs_0_.1, bf16[2,2,1024,128]{3,2,1,0:T(8,128)(2,1)} %constant.8.clone.refs_1_, ...), custom_call_target="tpu_custom_call" | custom-call | flops 536870912 | bytes 4194304 | tf_op jit(solution)/shard_map/delay_coefficients/pallas_call | solution.py:222
  5.1 0.5 %collective-permute-start = (bf16[1024,128]{1,0:T(8,128)(2,1)}, bf16[1024,128]{1,0:T(8,128)(2,1)S(1)}, u32[]{:S(2)}, u32[]{:S(2)}) collective-permute-start(bf16[1024,128]{1,0:T(8,128)(2,1)} %get-tuple-element.21.refs_0_), channel_id=1, source_target_pairs={{0,1},{1,0},{2,3},{3,2},{4,5},{5,4},{6,7},{7,6},{8,9},{9,8},{10,11... | collective-permute-start | bytes 786440 | tf_op jit(solution)/shard_map/ppermute | solution.py:647
  5.6 3.7 %collective-permute-start.9 = (bf16[2,4,2,4,1024]{4,3,2,1,0:T(4,128)(2,1)S(1)}, bf16[2,4,2,4,1024]{4,3,2,1,0:T(4,128)(2,1)S(1)}, u32[]{:S(2)}, u32[]{:S(2)}) collective-permute-start(bf16[2,4,2,4,1024]{4,3,2,1,0:T(4,128)(2,1)S(1)} %copy-done.2), channel_id=1, source_target_pairs={{0,8},{2,10},{4,12},{6,14},{8,0},{10,2},{12,4},{14,6},{1,9},{3,11}... | collective-permute-start | bytes 393224 | tf_op jit(solution)/shard_map/ppermute | solution.py:644
  9.3 1.3 %collective-permute-start.11 = (bf16[2,4,2,4,1024]{4,3,2,1,0:T(4,128)(2,1)S(1)}, bf16[2,4,2,4,1024]{4,3,2,1,0:T(4,128)(2,1)S(1)}, u32[]{:S(2)}, u32[]{:S(2)}) collective-permute-start(bf16[2,4,2,4,1024]{4,3,2,1,0:T(4,128)(2,1)S(1)} %copy-done.2), channel_id=1, source_target_pairs={{0,12},{2,14},{4,8},{6,10},{8,4},{10,6},{12,0},{14,2},{1,13},{3,15... | collective-permute-start | bytes 393224 | tf_op jit(solution)/shard_map/ppermute | solution.py:644
  10.6 0.2 collective-permute-start.6
  10.8 1.5 %collective-permute-start.5 = (bf16[2,4,2,4,1024]{4,3,2,1,0:T(4,128)(2,1)S(1)}, bf16[2,4,2,4,1024]{4,3,2,1,0:T(4,128)(2,1)S(1)}, u32[]{:S(2)}, u32[]{:S(2)}) collective-permute-start(bf16[2,4,2,4,1024]{4,3,2,1,0:T(4,128)(2,1)S(1)} %copy-done.2), channel_id=1, source_target_pairs={{0,2},{2,0},{4,6},{6,4},{8,10},{10,8},{12,14},{14,12},{1,3},{3,1},... | collective-permute-start | bytes 393224 | tf_op jit(solution)/shard_map/ppermute | solution.py:644
  12.4 0.0 collective-permute-done.refs_1_
  12.4 0.7 %copy-done.4 = bf16[1024,128]{1,0:T(8,128)(2,1)} copy-done((bf16[1024,128]{1,0:T(8,128)(2,1)}, bf16[1024,128]{1,0:T(8,128)(2,1)S(1)}, u32[]{:S(2)}) %copy-start.4) | copy-done | bytes 262168
  13.1 2.4 %owner_payloads.1 = (bf16[240,128]{1,0:T(8,128)(2,1)}, bf16[240,128]{1,0:T(8,128)(2,1)}, bf16[240,128]{1,0:T(8,128)(2,1)}, bf16[240,128]{1,0:T(8,128)(2,1)}) custom-call(bf16[1024,128]{1,0:T(8,128)(2,1)} %get-tuple-element.21.refs_0_, bf16[1024,128]{1,0:T(8,128)(2,1)} %copy-done.4, bf16[256,256]{1,0:T(8,128)(2,1)} %get-tuple-element.22.refs_2_, ...), custom_call_target="tpu_custom_call" | custom-call | flops 134217728 | bytes 2097152 | tf_op jit(solution)/shard_map/owner_payloads/pallas_call | solution.py:321
  15.4 1.5 %collective-permute-start.7 = (bf16[240,128]{1,0:T(8,128)(2,1)}, bf16[240,128]{1,0:T(8,128)(2,1)S(1)}, u32[]{:S(2)}, u32[]{:S(2)}) collective-permute-start(bf16[240,128]{1,0:T(8,128)(2,1)} %get-tuple-element.28), channel_id=1, source_target_pairs={{0,0},{1,9},{2,2},{3,11},{4,4},{5,13},{6,6},{7,15},{8,8},{9,1},{10... | collective-permute-start | bytes 184328 | tf_op jit(solution)/shard_map/ppermute | solution.py:668
  16.9 2.4 %collective-permute-done.9.refs_6_ = bf16[2,4,2,4,1024]{4,3,2,1,0:T(4,128)(2,1)S(1)} collective-permute-done((bf16[2,4,2,4,1024]{4,3,2,1,0:T(4,128)(2,1)S(1)}, bf16[2,4,2,4,1024]{4,3,2,1,0:T(4,128)(2,1)S(1)}, u32[]{:S(2)}, u32[]{:S(2)}) %collective-permute-start.9) | collective-permute-done | bytes 131104 | tf_op jit(solution)/shard_map/ppermute | solution.py:644
  19.3 1.8 %collective-permute-start.1 = (bf16[240,128]{1,0:T(8,128)(2,1)}, bf16[240,128]{1,0:T(8,128)(2,1)S(1)}, u32[]{:S(2)}, u32[]{:S(2)}) collective-permute-start(bf16[240,128]{1,0:T(8,128)(2,1)} %get-tuple-element.26), channel_id=1, source_target_pairs={{0,2},{1,11},{2,0},{3,9},{4,6},{5,15},{6,4},{7,13},{8,10},{9,3},{1... | collective-permute-start | bytes 184328 | tf_op jit(solution)/shard_map/ppermute | solution.py:668
  21.1 0.0 collective-permute-done.11.refs_7_
  21.1 3.8 %collective-permute-start.2 = (bf16[240,128]{1,0:T(8,128)(2,1)}, bf16[240,128]{1,0:T(8,128)(2,1)S(1)}, u32[]{:S(2)}, u32[]{:S(2)}) collective-permute-start(bf16[240,128]{1,0:T(8,128)(2,1)} %get-tuple-element.27), channel_id=1, source_target_pairs={{0,6},{1,15},{2,4},{3,13},{4,2},{5,11},{6,0},{7,9},{8,14},{9,7},{1... | collective-permute-start | bytes 184328 | tf_op jit(solution)/shard_map/ppermute | solution.py:668
  24.9 0.0 collective-permute-done.7.refs_0_
  24.9 0.0 collective-permute-start.13
  24.9 0.0 collective-permute-done.6.refs_5_
  24.9 0.6 %collective-permute-start.8 = (bf16[2,4,2,4,1024]{4,3,2,1,0:T(4,128)(2,1)S(1)}, bf16[2,4,2,4,1024]{4,3,2,1,0:T(4,128)(2,1)S(1)}, u32[]{:S(2)}, u32[]{:S(2)}) collective-permute-start(bf16[2,4,2,4,1024]{4,3,2,1,0:T(4,128)(2,1)S(1)} %collective-permute-done.6.refs_5_), channel_id=1, source_target_pairs={{0,2},{2,0},{4,6},{6,4},{8,10},{10,8},{12,14},{14,12},{1,3},{3,1},... | collective-permute-start | bytes 393224 | tf_op jit(solution)/shard_map/ppermute | solution.py:644
  25.5 0.0 collective-permute-done.5.refs_4_
  25.5 1.5 %collective-permute-start.10 = (bf16[2,4,2,4,1024]{4,3,2,1,0:T(4,128)(2,1)S(1)}, bf16[2,4,2,4,1024]{4,3,2,1,0:T(4,128)(2,1)S(1)}, u32[]{:S(2)}, u32[]{:S(2)}) collective-permute-start(bf16[2,4,2,4,1024]{4,3,2,1,0:T(4,128)(2,1)S(1)} %collective-permute-done.9.refs_6_), channel_id=1, source_target_pairs={{0,2},{2,0},{4,6},{6,4},{8,10},{10,8},{12,14},{14,12},{1,3},{3,1},... | collective-permute-start | bytes 393224 | tf_op jit(solution)/shard_map/ppermute | solution.py:644
  27.0 0.0 collective-permute-done.1.refs_0_
  27.0 0.5 %collective-permute-start.12 = (bf16[2,4,2,4,1024]{4,3,2,1,0:T(4,128)(2,1)S(1)}, bf16[2,4,2,4,1024]{4,3,2,1,0:T(4,128)(2,1)S(1)}, u32[]{:S(2)}, u32[]{:S(2)}) collective-permute-start(bf16[2,4,2,4,1024]{4,3,2,1,0:T(4,128)(2,1)S(1)} %collective-permute-done.11.refs_7_), channel_id=1, source_target_pairs={{0,2},{2,0},{4,6},{6,4},{8,10},{10,8},{12,14},{14,12},{1,3},{3,1},... | collective-permute-start | bytes 393224 | tf_op jit(solution)/shard_map/ppermute | solution.py:644
  27.5 2.1 %collective-permute-start.14 = (bf16[240,128]{1,0:T(8,128)(2,1)S(1)}, bf16[240,128]{1,0:T(8,128)(2,1)S(1)}, u32[]{:S(2)}, u32[]{:S(2)}) collective-permute-start(bf16[240,128]{1,0:T(8,128)(2,1)S(1)} %collective-permute-done.7.refs_0_), channel_id=1, source_target_pairs={{0,1},{1,0},{2,3},{3,2},{4,5},{5,4},{6,7},{7,6},{8,9},{9,8},{10,11... | collective-permute-start | bytes 184328 | tf_op jit(solution)/shard_map/ppermute | solution.py:647
  29.6 0.1 collective-permute-start.15
  29.7 0.8 %collective-permute-done.14.refs_2_ = bf16[240,128]{1,0:T(8,128)(2,1)S(1)} collective-permute-done((bf16[240,128]{1,0:T(8,128)(2,1)S(1)}, bf16[240,128]{1,0:T(8,128)(2,1)S(1)}, u32[]{:S(2)}, u32[]{:S(2)}) %collective-permute-start.14) | collective-permute-done | bytes 61472 | tf_op jit(solution)/shard_map/ppermute | solution.py:647
  30.5 0.4 collective-permute-start.3
  30.9 0.0 collective-permute-done.15.refs_3_
  30.9 0.2 collective-permute-start.4
  31.0 0.7 %copy-done.3 = s32[2,8]{1,0:T(2,128)S(1)} copy-done((s32[2,8]{1,0:T(2,128)S(1)}, s32[2,8]{1,0:T(2,128)}, u32[]{:S(2)}) %copy-start.3) | copy-done | bytes 88
  31.7 5.9 %owner_estimates.2 = (f32[4,8,8,1024]{3,2,1,0:T(8,128)S(1)}, f32[4,8,128]{2,1,0:T(8,128)S(1)}) custom-call(s32[2,8]{1,0:T(2,128)S(1)} %copy-done.3, bf16[240,128]{1,0:T(8,128)(2,1)S(1)} %collective-permute-done.7.refs_0_, bf16[240,128]{1,0:T(8,128)(2,1)S(1)} %collective-permute-done.13.refs_1_, bf16[240,128]{1,0:T(8,128)(2,1)S(1)} %collective-permute-done.14.refs_2_, ...), custom_call_target="tpu_custom_call" | custom-call | flops 536870912 | bytes 8388608 | tf_op jit(solution)/shard_map/owner_estimates/pallas_call | solution.py:592
  37.6 0.0 collective-permute-done.3.refs_2_
  37.6 7.4 %owner_estimates.3 = f32[4,8,4,2,1024]{4,3,2,1,0:T(2,128)} custom-call(s32[2,8]{1,0:T(2,128)S(1)} %copy-done.3, bf16[240,128]{1,0:T(8,128)(2,1)S(1)} %collective-permute-done.1.refs_0_, bf16[240,128]{1,0:T(8,128)(2,1)S(1)} %collective-permute-done.2.refs_1_, bf16[240,128]{1,0:T(8,128)(2,1)S(1)} %collective-permute-done.3.refs_2_, ...), custom_call_target="tpu_custom_call" | custom-call | flops 536870912 | bytes 8388608 | tf_op jit(solution)/shard_map/owner_estimates/pallas_call | solution.py:592
  (14 shorter events, 0.0 us)
Async XLA Ops:
  0.0 5.6 %copy-start.2 = (bf16[2,4,2,4,1024]{4,3,2,1,0:T(4,128)(2,1)S(1)}, bf16[2,4,2,4,1024]{4,3,2,1,0:T(4,128)(2,1)}, u32[]{:S(2)}) copy-start(bf16[2,4,2,4,1024]{4,3,2,1,0:T(4,128)(2,1)} %refs_4_.1) | copy-start | bytes 393220
  0.0 31.0 %copy-start = (bf16[2,256,2048]{2,1,0:T(8,128)(2,1)S(1)}, bf16[2,256,2048]{2,1,0:T(8,128)(2,1)}, u32[]{:S(2)}) copy-start(bf16[2,256,2048]{2,1,0:T(8,128)(2,1)} %constant.11.clone.refs_9_) | copy-start | bytes 6291460
  0.0 31.0 %copy-start.1 = (bf16[2,384,1024]{2,1,0:T(8,128)(2,1)S(1)}, bf16[2,384,1024]{2,1,0:T(8,128)(2,1)}, u32[]{:S(2)}) copy-start(bf16[2,384,1024]{2,1,0:T(8,128)(2,1)} %constant.10.clone.refs_8_) | copy-start | bytes 4718596
  5.1 7.3 %collective-permute-start = (bf16[1024,128]{1,0:T(8,128)(2,1)}, bf16[1024,128]{1,0:T(8,128)(2,1)S(1)}, u32[]{:S(2)}, u32[]{:S(2)}) collective-permute-start(bf16[1024,128]{1,0:T(8,128)(2,1)} %get-tuple-element.21.refs_0_), channel_id=1, source_target_pairs={{0,1},{1,0},{2,3},{3,2},{4,5},{5,4},{6,7},{7,6},{8,9},{9,8},{10,11... | collective-permute-start | bytes 786440 | tf_op jit(solution)/shard_map/ppermute | solution.py:647
  5.6 13.7 %collective-permute-start.9 = (bf16[2,4,2,4,1024]{4,3,2,1,0:T(4,128)(2,1)S(1)}, bf16[2,4,2,4,1024]{4,3,2,1,0:T(4,128)(2,1)S(1)}, u32[]{:S(2)}, u32[]{:S(2)}) collective-permute-start(bf16[2,4,2,4,1024]{4,3,2,1,0:T(4,128)(2,1)S(1)} %copy-done.2), channel_id=1, source_target_pairs={{0,8},{2,10},{4,12},{6,14},{8,0},{10,2},{12,4},{14,6},{1,9},{3,11}... | collective-permute-start | bytes 393224 | tf_op jit(solution)/shard_map/ppermute | solution.py:644
  9.3 11.8 %collective-permute-start.11 = (bf16[2,4,2,4,1024]{4,3,2,1,0:T(4,128)(2,1)S(1)}, bf16[2,4,2,4,1024]{4,3,2,1,0:T(4,128)(2,1)S(1)}, u32[]{:S(2)}, u32[]{:S(2)}) collective-permute-start(bf16[2,4,2,4,1024]{4,3,2,1,0:T(4,128)(2,1)S(1)} %copy-done.2), channel_id=1, source_target_pairs={{0,12},{2,14},{4,8},{6,10},{8,4},{10,6},{12,0},{14,2},{1,13},{3,15... | collective-permute-start | bytes 393224 | tf_op jit(solution)/shard_map/ppermute | solution.py:644
  10.6 14.3 %collective-permute-start.6 = (bf16[2,4,2,4,1024]{4,3,2,1,0:T(4,128)(2,1)S(1)}, bf16[2,4,2,4,1024]{4,3,2,1,0:T(4,128)(2,1)S(1)}, u32[]{:S(2)}, u32[]{:S(2)}) collective-permute-start(bf16[2,4,2,4,1024]{4,3,2,1,0:T(4,128)(2,1)S(1)} %copy-done.2), channel_id=1, source_target_pairs={{0,4},{2,6},{4,0},{6,2},{8,12},{10,14},{12,8},{14,10},{1,5},{3,7},... | collective-permute-start | bytes 393224 | tf_op jit(solution)/shard_map/ppermute | solution.py:644
  10.8 14.6 %collective-permute-start.5 = (bf16[2,4,2,4,1024]{4,3,2,1,0:T(4,128)(2,1)S(1)}, bf16[2,4,2,4,1024]{4,3,2,1,0:T(4,128)(2,1)S(1)}, u32[]{:S(2)}, u32[]{:S(2)}) collective-permute-start(bf16[2,4,2,4,1024]{4,3,2,1,0:T(4,128)(2,1)S(1)} %copy-done.2), channel_id=1, source_target_pairs={{0,2},{2,0},{4,6},{6,4},{8,10},{10,8},{12,14},{14,12},{1,3},{3,1},... | collective-permute-start | bytes 393224 | tf_op jit(solution)/shard_map/ppermute | solution.py:644
  12.4 0.7 %copy-start.4 = (bf16[1024,128]{1,0:T(8,128)(2,1)}, bf16[1024,128]{1,0:T(8,128)(2,1)S(1)}, u32[]{:S(2)}) copy-start(bf16[1024,128]{1,0:T(8,128)(2,1)S(1)} %collective-permute-done.refs_1_) | copy-start | bytes 786436
  15.4 9.4 %collective-permute-start.7 = (bf16[240,128]{1,0:T(8,128)(2,1)}, bf16[240,128]{1,0:T(8,128)(2,1)S(1)}, u32[]{:S(2)}, u32[]{:S(2)}) collective-permute-start(bf16[240,128]{1,0:T(8,128)(2,1)} %get-tuple-element.28), channel_id=1, source_target_pairs={{0,0},{1,9},{2,2},{3,11},{4,4},{5,13},{6,6},{7,15},{8,8},{9,1},{10... | collective-permute-start | bytes 184328 | tf_op jit(solution)/shard_map/ppermute | solution.py:668
  19.3 7.7 %collective-permute-start.1 = (bf16[240,128]{1,0:T(8,128)(2,1)}, bf16[240,128]{1,0:T(8,128)(2,1)S(1)}, u32[]{:S(2)}, u32[]{:S(2)}) collective-permute-start(bf16[240,128]{1,0:T(8,128)(2,1)} %get-tuple-element.26), channel_id=1, source_target_pairs={{0,2},{1,11},{2,0},{3,9},{4,6},{5,15},{6,4},{7,13},{8,10},{9,3},{1... | collective-permute-start | bytes 184328 | tf_op jit(solution)/shard_map/ppermute | solution.py:668
  21.1 6.4 %collective-permute-start.2 = (bf16[240,128]{1,0:T(8,128)(2,1)}, bf16[240,128]{1,0:T(8,128)(2,1)S(1)}, u32[]{:S(2)}, u32[]{:S(2)}) collective-permute-start(bf16[240,128]{1,0:T(8,128)(2,1)} %get-tuple-element.27), channel_id=1, source_target_pairs={{0,6},{1,15},{2,4},{3,13},{4,2},{5,11},{6,0},{7,9},{8,14},{9,7},{1... | collective-permute-start | bytes 184328 | tf_op jit(solution)/shard_map/ppermute | solution.py:668
  24.9 4.7 %collective-permute-start.13 = (bf16[240,128]{1,0:T(8,128)(2,1)}, bf16[240,128]{1,0:T(8,128)(2,1)S(1)}, u32[]{:S(2)}, u32[]{:S(2)}) collective-permute-start(bf16[240,128]{1,0:T(8,128)(2,1)} %get-tuple-element.32), channel_id=1, source_target_pairs={{0,4},{1,13},{2,6},{3,15},{4,0},{5,9},{6,2},{7,11},{8,12},{9,5},{1... | collective-permute-start | bytes 184328 | tf_op jit(solution)/shard_map/ppermute | solution.py:668
  24.9 12.7 %collective-permute-start.8 = (bf16[2,4,2,4,1024]{4,3,2,1,0:T(4,128)(2,1)S(1)}, bf16[2,4,2,4,1024]{4,3,2,1,0:T(4,128)(2,1)S(1)}, u32[]{:S(2)}, u32[]{:S(2)}) collective-permute-start(bf16[2,4,2,4,1024]{4,3,2,1,0:T(4,128)(2,1)S(1)} %collective-permute-done.6.refs_5_), channel_id=1, source_target_pairs={{0,2},{2,0},{4,6},{6,4},{8,10},{10,8},{12,14},{14,12},{1,3},{3,1},... | collective-permute-start | bytes 393224 | tf_op jit(solution)/shard_map/ppermute | solution.py:644
  25.5 12.1 %collective-permute-start.10 = (bf16[2,4,2,4,1024]{4,3,2,1,0:T(4,128)(2,1)S(1)}, bf16[2,4,2,4,1024]{4,3,2,1,0:T(4,128)(2,1)S(1)}, u32[]{:S(2)}, u32[]{:S(2)}) collective-permute-start(bf16[2,4,2,4,1024]{4,3,2,1,0:T(4,128)(2,1)S(1)} %collective-permute-done.9.refs_6_), channel_id=1, source_target_pairs={{0,2},{2,0},{4,6},{6,4},{8,10},{10,8},{12,14},{14,12},{1,3},{3,1},... | collective-permute-start | bytes 393224 | tf_op jit(solution)/shard_map/ppermute | solution.py:644
  27.0 10.6 %collective-permute-start.12 = (bf16[2,4,2,4,1024]{4,3,2,1,0:T(4,128)(2,1)S(1)}, bf16[2,4,2,4,1024]{4,3,2,1,0:T(4,128)(2,1)S(1)}, u32[]{:S(2)}, u32[]{:S(2)}) collective-permute-start(bf16[2,4,2,4,1024]{4,3,2,1,0:T(4,128)(2,1)S(1)} %collective-permute-done.11.refs_7_), channel_id=1, source_target_pairs={{0,2},{2,0},{4,6},{6,4},{8,10},{10,8},{12,14},{14,12},{1,3},{3,1},... | collective-permute-start | bytes 393224 | tf_op jit(solution)/shard_map/ppermute | solution.py:644
  27.5 3.0 %collective-permute-start.14 = (bf16[240,128]{1,0:T(8,128)(2,1)S(1)}, bf16[240,128]{1,0:T(8,128)(2,1)S(1)}, u32[]{:S(2)}, u32[]{:S(2)}) collective-permute-start(bf16[240,128]{1,0:T(8,128)(2,1)S(1)} %collective-permute-done.7.refs_0_), channel_id=1, source_target_pairs={{0,1},{1,0},{2,3},{3,2},{4,5},{5,4},{6,7},{7,6},{8,9},{9,8},{10,11... | collective-permute-start | bytes 184328 | tf_op jit(solution)/shard_map/ppermute | solution.py:647
  29.6 1.2 %collective-permute-start.15 = (bf16[240,128]{1,0:T(8,128)(2,1)S(1)}, bf16[240,128]{1,0:T(8,128)(2,1)S(1)}, u32[]{:S(2)}, u32[]{:S(2)}) collective-permute-start(bf16[240,128]{1,0:T(8,128)(2,1)S(1)} %collective-permute-done.13.refs_1_), channel_id=1, source_target_pairs={{0,1},{1,0},{2,3},{3,2},{4,5},{5,4},{6,7},{7,6},{8,9},{9,8},{10,11... | collective-permute-start | bytes 184328 | tf_op jit(solution)/shard_map/ppermute | solution.py:647
  30.5 7.1 %collective-permute-start.3 = (bf16[240,128]{1,0:T(8,128)(2,1)S(1)}, bf16[240,128]{1,0:T(8,128)(2,1)S(1)}, u32[]{:S(2)}, u32[]{:S(2)}) collective-permute-start(bf16[240,128]{1,0:T(8,128)(2,1)S(1)} %collective-permute-done.1.refs_0_), channel_id=1, source_target_pairs={{0,1},{1,0},{2,3},{3,2},{4,5},{5,4},{6,7},{7,6},{8,9},{9,8},{10,11... | collective-permute-start | bytes 184328 | tf_op jit(solution)/shard_map/ppermute | solution.py:647
  30.9 6.7 %collective-permute-start.4 = (bf16[240,128]{1,0:T(8,128)(2,1)S(1)}, bf16[240,128]{1,0:T(8,128)(2,1)S(1)}, u32[]{:S(2)}, u32[]{:S(2)}) collective-permute-start(bf16[240,128]{1,0:T(8,128)(2,1)S(1)} %collective-permute-done.2.refs_1_), channel_id=1, source_target_pairs={{0,1},{1,0},{2,3},{3,2},{4,5},{5,4},{6,7},{7,6},{8,9},{9,8},{10,11... | collective-permute-start | bytes 184328 | tf_op jit(solution)/shard_map/ppermute | solution.py:647
  31.0 0.7 %copy-start.3 = (s32[2,8]{1,0:T(2,128)S(1)}, s32[2,8]{1,0:T(2,128)}, u32[]{:S(2)}) copy-start(s32[2,8]{1,0:T(2,128)} %get-tuple-element.20.slots) | copy-start | bytes 196

commit v3 on v2

--- a/solution.py
+++ b/solution.py
@@ -15,6 +15,7 @@
 CU = 8
 OWN_MAX = 4
 PEER_MAX = 2
+EARLY = (1, 4)
 SAMPLES = 2 * TAPS
 ROWS = PEER_MAX * CU
 LARGE_BYTES = 58 * 1024 * 1024
@@ -384,12 +385,12 @@
     return result
 
 
-def estimate_kernel(shape, chunk, labels, first_call, last_call, slots, *refs):
+def estimate_kernel(shape, chunk, group, slots, *refs):
     aps, antennas, symbols, tones, devices, shards = shape
-    per = devices // shards
-    count = len(labels)
-    pays, signals = refs[:count], refs[count : 2 * count]
-    refs = refs[2 * count :]
+    count = devices // shards
+    first_call, last_call = group == 0, group == shards - 1
+    pays, signals = refs[:devices], refs[devices : devices + count]
+    refs = refs[devices + count :]
     kernel_table, rebuild_table = refs[:2]
     refs = refs[2:]
     if first_call:
@@ -399,8 +400,8 @@
         acc_in, denominator_in, out = refs[:3]
         refs = refs[3:]
     (
-        dirichlet, rebuild, left, cov_full, cov_tiles, sig_tiles, solved, smooth, weight,
-        acc, denominator, turned, table_sem,
+        left, cov_full, cov_tiles, sig_tiles, solved, smooth, weight,
+        acc, denominator, turned, staged, out_sem,
     ) = refs
     if first_call:
         acc, denominator = out, denominator_out
@@ -409,16 +410,21 @@
     coef_rows = aps * antennas * ROWS
     blocks = tones // 128
 
-    kernel_copy = pltpu.make_async_copy(kernel_table.at[core], dirichlet, table_sem.at[0])
-    rebuild_copy = pltpu.make_async_copy(rebuild_table.at[core], rebuild, table_sem.at[1])
-    kernel_copy.start()
-    rebuild_copy.start()
+    dirichlet, rebuild = kernel_table.at[core], rebuild_table.at[core]
+
+    def payload(n, start, size):
+        value = pays[n][pl.ds(start, size), :]
+        for h in range(1, shards):
+            value = jnp.where(
+                (core ^ h) == group, pays[h * count + n][pl.ds(start, size), :], value
+            )
+        return value
 
     def cov_part(k):
-        rows = [pay[pl.ds(coef_rows + k * cov_rows, cov_rows), :] for pay in pays]
-        return jnp.concatenate(rows, axis=0)
-
-    kernel_copy.wait()
+        return jnp.concatenate(
+            [payload(n, coef_rows + k * cov_rows, cov_rows) for n in range(count)], axis=0
+        )
+
     high, middle, low = cov_part(0), cov_part(1), cov_part(2)
     n = SAMPLES
     cov_full[...] = (
@@ -431,11 +437,11 @@
         )
     )
 
-    for n, pay in enumerate(pays):
-        rows = pay[pl.ds(0, coef_rows), :]
+    for n in range(count):
+        rows = payload(n, 0, coef_rows)
         left[pl.ds(n * coef_rows, coef_rows), : 2 * TAPS] = rows
         left[pl.ds(n * coef_rows, coef_rows), 2 * TAPS :] = rows
-        packed = pay[pl.ds(coef_rows + 3 * cov_rows, ROWS), :].astype(F32)
+        packed = payload(n, coef_rows + 3 * cov_rows, ROWS).astype(F32)
         for a in range(aps):
             value = packed[:, a : a + 1] + packed[:, 8 + a : 9 + a] + packed[:, 16 + a : 17 + a]
             weight[n, a] = jnp.broadcast_to(value, (ROWS, 128))
@@ -447,20 +453,14 @@
         acc[...] = acc_in[...]
         denominator[...] = denominator_in[...]
 
-    stride = labels[1] - labels[0]
-
-    def partner(n):
-        return (labels[0] + n * stride) ^ (core * per)
-
-    for n, label in enumerate(labels):
-        place = (label ^ (core * per)) // stride
+    for n in range(count):
         for a in range(aps):
             for i in range(antennas):
                 for c in range(2):
                     rows = signals[n][a, i, c].astype(F32)
                     first = ((a * antennas + i) * 2 + c) * symbols * blocks
                     for b in range(blocks):
-                        sig_tiles[place, pl.ds(first + b, symbols, stride=blocks), :] = rows[
+                        sig_tiles[n, pl.ds(first + b, symbols, stride=blocks), :] = rows[
                             :, b * 128 : (b + 1) * 128
                         ]
 
@@ -489,10 +489,11 @@
                     right.append([sig_tiles[l, pl.ds(t, blocks), :] for t in tiles])
                 result = substitute(factor, inverse, right)
                 for i in range(antennas):
-                    for c in range(2):
-                        at = ((a * antennas + i) * symbols + s) * 2 + c
-                        solved[l, pl.ds(at * blocks, blocks), :] = result[i][c]
-        source = partner(l) ^ device
+                    re, im = result[i]
+                    at = ((a * antennas + i) * symbols + s) * 3
+                    for c, tile in enumerate((re, im - re, re + im)):
+                        solved[l, pl.ds((at + c) * blocks, blocks), :] = tile
+        source = (group * count + l) ^ device
         for p in range(PEER_MAX):
             k = slots[p, source]
             for a in range(aps):
@@ -500,14 +501,13 @@
         return carry
 
     lax.fori_loop(0, count, solve, 0)
-    rebuild_copy.wait()
 
     def combine(l, q):
-        source = partner(l) ^ device
+        source = (group * count + l) ^ device
         for h in range(chunk // 128):
             b = q * (chunk // 128) + h
             lanes = pl.ds(pl.multiple_of(b * 128, 128), 128)
-            totals = [[None] * (2 * symbols) for p in range(PEER_MAX)]
+            totals = [[None] * (3 * symbols) for p in range(PEER_MAX)]
             for a in range(aps):
                 for i in range(antennas):
                     base = pl.multiple_of(l * coef_rows + (a * antennas + i) * ROWS, 8)
@@ -515,31 +515,45 @@
                     for p in range(PEER_MAX):
                         scale = weight[l, a, pl.ds(p * CU, CU), :]
                         rows = pl.ds(base + p * CU, CU)
-                        link.append(
-                            (
-                                smooth[rows, h * 128 : (h + 1) * 128] * scale,
-                                smooth[rows, chunk + h * 128 : chunk + (h + 1) * 128] * scale,
-                            )
-                        )
+                        re = smooth[rows, h * 128 : (h + 1) * 128] * scale
+                        im = smooth[rows, chunk + h * 128 : chunk + (h + 1) * 128] * scale
+                        link.append((re - im, re, im))
                     for s in range(symbols):
-                        at = ((a * antennas + i) * symbols + s) * 2
-                        xr = solved[l, pl.ds(at * blocks + b, 1), :]
-                        xi = solved[l, pl.ds((at + 1) * blocks + b, 1), :]
-                        xr = jnp.broadcast_to(xr, (CU, 128))
-                        xi = jnp.broadcast_to(xi, (CU, 128))
-                        for p in range(PEER_MAX):
-                            gr, gi = link[p]
-                            er = gr * xr + gi * xi
-                            ei = gr * xi - gi * xr
-                            if totals[p][2 * s] is None:
-                                totals[p][2 * s], totals[p][2 * s + 1] = er, ei
-                            else:
-                                totals[p][2 * s] += er
-                                totals[p][2 * s + 1] += ei
+                        at = ((a * antennas + i) * symbols + s) * 3
+                        for c in range(3):
+                            x = solved[l, pl.ds((at + c) * blocks + b, 1), :]
+                            x = jnp.broadcast_to(x, (CU, 128))
+                            for p in range(PEER_MAX):
+                                value = link[p][c] * x
+                                old = totals[p][3 * s + c]
+                                totals[p][3 * s + c] = value if old is None else old + value
             for p in range(PEER_MAX):
                 k = slots[p, source]
+                for s in range(symbols):
+                    both, upper, lower = totals[p][3 * s : 3 * s + 3]
+                    acc[k, 2 * s, :, lanes] = acc[k, 2 * s, :, lanes] + (both + lower)
+                    acc[k, 2 * s + 1, :, lanes] = acc[k, 2 * s + 1, :, lanes] + (both + upper)
+
+    chunks = tones // chunk
+
+    def output_copy(q):
+        lanes = pl.ds(pl.multiple_of(q * chunk, 128), chunk)
+        return pltpu.make_async_copy(staged.at[q], out.at[:, :, :, :, lanes], out_sem.at[q])
+
+    def finish(q):
+        for k in range(OWN_MAX):
+            inverse = 1.0 / denominator[k]
+            first = k * CU * 2 * symbols
+            for h in range(chunk // 128):
+                lanes = pl.ds(pl.multiple_of(q * chunk + h * 128, 128), 128)
                 for e in range(2 * symbols):
-                    acc[k, e, :, lanes] = acc[k, e, :, lanes] + totals[p][e]
+                    value = acc[k, e, :, lanes] * inverse
+                    turned[pl.ds(first + e, CU, stride=2 * symbols), :] = value
+                for m in range(CU):
+                    for s in range(symbols):
+                        at = first + (m * symbols + s) * 2
+                        staged[q, k, m, s, :, h * 128 : (h + 1) * 128] = turned[pl.ds(at, 2), :]
+        output_copy(q).start()
 
     def one_chunk(q, carry):
         columns = pl.ds(pl.multiple_of(q * 2 * chunk, 128), 2 * chunk)
@@ -550,32 +564,21 @@
             return inner
 
         lax.fori_loop(0, count, step, 0)
+        if last_call:
+            finish(q)
         return carry
 
-    lax.fori_loop(0, tones // chunk, one_chunk, 0)
-
-    if not last_call:
-        return
-
-    def finish(k, carry):
-        inverse = 1.0 / denominator[k]
-        for b in range(blocks):
-            for e in range(2 * symbols):
-                value = acc[k, e, :, b * 128 : (b + 1) * 128] * inverse
-                turned[pl.ds(b * CU * 2 * symbols + e, CU, stride=2 * symbols), :] = value
-            for m in range(CU):
-                for s in range(symbols):
-                    at = ((b * CU + m) * symbols + s) * 2
-                    out[k, m, s, :, b * 128 : (b + 1) * 128] = turned[pl.ds(at, 2), :]
-        return carry
-
-    lax.fori_loop(0, OWN_MAX, finish, 0)
-
-
-def owner_estimates(slots, pays, signals, labels, before, last_call, shape):
+    lax.fori_loop(0, chunks, one_chunk, 0)
+    if last_call:
+        for q in range(chunks):
+            output_copy(q).wait()
+
+
+def owner_estimates(slots, pays, signals, group, before, shape):
     aps, antennas, symbols, tones, devices, shards = shape
-    chunk = min(256, tones)
-    count = len(labels)
+    chunk = min(512, tones // 2)
+    count = devices // shards
+    last_call = group == shards - 1
     cov_rows = aps * antennas * antennas
     coef_rows = aps * antennas * ROWS
     blocks = tones // 128
@@ -584,30 +587,28 @@
     smem = pl.BlockSpec(memory_space=pltpu.SMEM)
     sums = (OWN_MAX, 2 * symbols, CU, tones)
     bottom = (OWN_MAX, CU, 128)
-    first_call = not before
     if last_call:
         outs = [jax.ShapeDtypeStruct((OWN_MAX, CU, symbols, 2, tones), F32)]
     else:
         outs = [jax.ShapeDtypeStruct(sums, F32), jax.ShapeDtypeStruct(bottom, F32)]
     return pl.pallas_call(
-        functools.partial(estimate_kernel, shape, chunk, labels, first_call, last_call),
-        in_specs=[smem] + [vmem] * (2 * count) + [hbm] * 2 + [vmem] * len(before),
-        out_specs=[vmem] * len(outs),
+        functools.partial(estimate_kernel, shape, chunk, group),
+        in_specs=[smem] + [vmem] * (len(pays) + len(signals) + 2 + len(before)),
+        out_specs=[hbm] if last_call else [vmem] * len(outs),
         out_shape=outs,
         scratch_shapes=[
-            pltpu.VMEM((3 * SAMPLES, tones), BF16),
-            pltpu.VMEM((4 * TAPS, 2 * tones), BF16),
             pltpu.VMEM((count * coef_rows, 4 * TAPS), BF16),
             pltpu.VMEM((count * cov_rows, tones), F32),
             pltpu.VMEM((cov_rows * blocks, 128), F32),
             pltpu.VMEM((count, aps * antennas * 2 * symbols * blocks, 128), F32),
-            pltpu.VMEM((count, aps * antennas * 2 * symbols * blocks, 128), F32),
+            pltpu.VMEM((count, aps * antennas * 3 * symbols * blocks, 128), F32),
             pltpu.VMEM((count * coef_rows, 2 * chunk), F32),
             pltpu.VMEM((count, aps, ROWS, 128), F32),
             pltpu.VMEM(sums, F32),
             pltpu.VMEM(bottom, F32),
-            pltpu.VMEM((CU * 2 * symbols * blocks, 128), F32),
-            pltpu.SemaphoreType.DMA((2,)),
+            pltpu.VMEM((CU * 2 * symbols * OWN_MAX, 128), F32),
+            pltpu.VMEM((tones // chunk, OWN_MAX, CU, symbols, 2, chunk), F32),
+            pltpu.SemaphoreType.DMA((tones // chunk,)),
         ],
         compiler_params=pltpu.CompilerParams(vmem_limit_bytes=VMEM_BYTES),
         cost_estimate=pl.CostEstimate(
@@ -655,6 +656,9 @@
         unsmoothed_link_guesses, user_power, noise_power, ap_gain, user_cluster, serving,
         cluster_owner, (aps, antennas, users, devices, shards),
     )
+    combined, early = lax.optimization_barrier((combined, [signals[v] for v in EARLY]))
+    for v, value in zip(EARLY, early):
+        signals[v] = value
     parts = [combined] + [swap_sc(combined, h) for h in range(1, shards)]
     blocks = owner_payloads(
         parts, samples, pick, weights, extras, (aps, antennas, users, devices, shards)
@@ -666,18 +670,17 @@
         for c in range(shards)
     ]
     own = [lax.ppermute(blocks[j], ("ap", "sc"), pairs(j)) for j in range(per)]
+    pays = own + [swap_sc(own[j], h) for h in range(1, shards) for j in range(per)]
     for v in range(2, devices, 2):
-        later, _ = lax.optimization_barrier((signals[v], own[0]))
-        signals[v + 1] = swap_ap(later, 1)
-    pays = own + [swap_sc(own[j], h) for h in range(1, shards) for j in range(per)]
+        value = signals[v] if v in EARLY else lax.optimization_barrier((signals[v], own[0]))[0]
+        signals[v + 1] = swap_ap(value, 1)
     shape = (aps, antennas, symbols, tones, devices, shards)
-    even, odd = list(range(0, devices, 2)), list(range(1, devices, 2))
-    sums = owner_estimates(
-        slots, [pays[l] for l in even], [signals[v] for v in even], even, [], False, shape
-    )
-    return owner_estimates(
-        slots, [pays[l] for l in odd], [signals[v] for v in odd], odd, sums, True, shape
-    )[0]
+    result = []
+    for group in range(shards):
+        result = owner_estimates(
+            slots, pays, signals[group * per : (group + 1) * per], group, result, shape
+        )
+    return result[0]
 
 
 def solution(mesh):

time: 45.2 us -> 43.7 us (0.967)
  starting transfers between devices: 19.7 us -> 22.3 us
  Pallas kernels: 20.6 us -> 18.5 us
  waiting for transfers between devices: 3.22 us -> 1.21 us
    ppermute x7, starting transfers between devices: 9.37 us -> 12.6 us  [swap_ap(): return lax.ppermute(value, 'ap', [(i, i ^ v) for i in range(devices)])]
    ppermute x7, waiting for transfers between devices: 2.37 us -> 0.02 us  [swap_ap(): return lax.ppermute(value, 'ap', [(i, i ^ v) for i in range(devices)])]
    pallas_call x2, Pallas kernels: 13.2 us -> 11 us  [owner_estimates(): pl.pallas_call(functools.partial(estimate_kernel, shape, chunk, group), i...]
    ppermute x4, starting transfers between devices: 7.07 us -> 4.96 us  [local(): own = [lax.ppermute(blocks[j], ('ap', 'sc'), pairs(j)) for j in range(per)]]
    ppermute x5, starting transfers between devices: 3.22 us -> 4.75 us  [swap_sc(): return lax.ppermute(value, 'sc', [(c, c ^ h) for c in range(shards)])]
  transfers between devices with their start and end apart: 16 -> 16, of which waited for: 2 -> 2; matrix products, arithmetic and copies ran while one was open for 0% -> 0% of each run, Pallas kernels for 18% -> 28%
where the time goes in v3:
time: 43.7 us; the launch traced here: 43.5 us
  starting transfers between devices  22.3 us (51%)
  Pallas kernels  18.5 us (42%)
  local copies, waits for them, and re-layouts  1.37 us (3%)
  waiting for transfers between devices  1.21 us (3%)
    ppermute x7, starting transfers between devices, swap_ap(): return lax.ppermute(value, 'ap', [(i, i ^ v) for i in range(devices)])  12.6 us
    pallas_call x2, Pallas kernels, owner_estimates(): pl.pallas_call(functools.partial(estimate_kernel, shape, chunk, group), i...  11 us
    pallas_call x1, Pallas kernels, delay_coefficients(): pl.pallas_call(functools.partial(coefficient_kernel, shape), in_specs=[hb...  5.05 us
    ppermute x4, starting transfers between devices, local(): own = [lax.ppermute(blocks[j], ('ap', 'sc'), pairs(j)) for j in range(per)]  4.96 us
    ppermute x5, starting transfers between devices, swap_sc(): return lax.ppermute(value, 'sc', [(c, c ^ h) for c in range(shards)])  4.75 us
    pallas_call x1, Pallas kernels, owner_payloads(): pl.pallas_call(functools.partial(payload_kernel, shape), grid=(1,), in_sp...  2.38 us
    unnamed x10, local copies, waits for them, and re-layouts  1.37 us
    ppermute x5, waiting for transfers between devices, swap_sc(): return lax.ppermute(value, 'sc', [(c, c ^ h) for c in range(shards)])  1.19 us
  transfers between devices with their start and end apart: 16, of which 2 were waited for; matrix products, arithmetic and copies ran while one was open for 0% of the time, Pallas kernels for 28%

profile of v3, /device:TPU:0, one launch (start us, length us, event | category | flops | bytes accessed | tf_op | source)
XLA Modules:
  0.0 43.5 jit_solution(7765573778933240499)
XLA Ops:
  0.0 4.0 %collective-permute-start.1 = (bf16[2,4,2,4,1024]{4,3,2,1,0:T(4,128)(2,1)}, bf16[2,4,2,4,1024]{4,3,2,1,0:T(4,128)(2,1)S(1)}, u32[]{:S(2)}, u32[]{:S(2)}) collective-permute-start(bf16[2,4,2,4,1024]{4,3,2,1,0:T(4,128)(2,1)} %refs_8_.1), channel_id=1, source_target_pairs={{0,8},{2,10},{4,12},{6,14},{8,0},{10,2},{12,4},{14,6},{1,9},{3,11}... | collective-permute-start | bytes 393224 | tf_op jit(solution)/shard_map/ppermute | solution.py:645
  4.0 1.5 %collective-permute-start = (bf16[2,4,2,4,1024]{4,3,2,1,0:T(4,128)(2,1)}, bf16[2,4,2,4,1024]{4,3,2,1,0:T(4,128)(2,1)S(1)}, u32[]{:S(2)}, u32[]{:S(2)}) collective-permute-start(bf16[2,4,2,4,1024]{4,3,2,1,0:T(4,128)(2,1)} %refs_8_.1), channel_id=1, source_target_pairs={{0,2},{2,0},{4,6},{6,4},{8,10},{10,8},{12,14},{14,12},{1,3},{3,1},... | collective-permute-start | bytes 393224 | tf_op jit(solution)/shard_map/ppermute | solution.py:645
  5.6 5.1 %delay_coefficients.1 = (bf16[1024,128]{1,0:T(8,128)(2,1)}, bf16[256,256]{1,0:T(8,128)(2,1)}, bf16[64,128]{1,0:T(8,128)(2,1)}, bf16[64,128]{1,0:T(8,128)(2,1)}, s32[2,8]{1,0:T(2,128)}, /*index=5*/f32[136,128]{1,0:T(8,128)}) custom-call(bf16[2,4,2,128,1024]{4,3,2,1,0:T(8,128)(2,1)} %refs_0_.1, bf16[2,2,1024,128]{3,2,1,0:T(8,128)(2,1)} %constant.8.clone.refs_1_, ...), custom_call_target="tpu_custom_call" | custom-call | flops 536870912 | bytes 4194304 | tf_op jit(solution)/shard_map/delay_coefficients/pallas_call | solution.py:223
  10.6 0.0 collective-permute-done.1.refs_8_
  10.6 0.0 collective-permute-done.refs_9_
  10.6 0.1 collective-permute-start.2
  10.7 1.6 %collective-permute-start.14 = (bf16[2,4,2,4,1024]{4,3,2,1,0:T(4,128)(2,1)S(1)}, bf16[2,4,2,4,1024]{4,3,2,1,0:T(4,128)(2,1)S(1)}, u32[]{:S(2)}, u32[]{:S(2)}) collective-permute-start(bf16[2,4,2,4,1024]{4,3,2,1,0:T(4,128)(2,1)S(1)} %copy-done.2), channel_id=1, source_target_pairs={{0,4},{2,6},{4,0},{6,2},{8,12},{10,14},{12,8},{14,10},{1,5},{3,7},... | collective-permute-start | bytes 393224 | tf_op jit(solution)/shard_map/ppermute | solution.py:645
  12.4 1.9 %collective-permute-start.12 = (bf16[2,4,2,4,1024]{4,3,2,1,0:T(4,128)(2,1)S(1)}, bf16[2,4,2,4,1024]{4,3,2,1,0:T(4,128)(2,1)S(1)}, u32[]{:S(2)}, u32[]{:S(2)}) collective-permute-start(bf16[2,4,2,4,1024]{4,3,2,1,0:T(4,128)(2,1)S(1)} %copy-done.2), channel_id=1, source_target_pairs={{0,12},{2,14},{4,8},{6,10},{8,4},{10,6},{12,0},{14,2},{1,13},{3,15... | collective-permute-start | bytes 393224 | tf_op jit(solution)/shard_map/ppermute | solution.py:645
  14.3 0.0 collective-permute-done.2.refs_1_
  14.3 0.7 %copy-done.4 = bf16[1024,128]{1,0:T(8,128)(2,1)} copy-done((bf16[1024,128]{1,0:T(8,128)(2,1)}, bf16[1024,128]{1,0:T(8,128)(2,1)S(1)}, u32[]{:S(2)}) %copy-start.4) | copy-done | bytes 262168
  15.0 2.4 %owner_payloads.1 = (bf16[240,128]{1,0:T(8,128)(2,1)}, bf16[240,128]{1,0:T(8,128)(2,1)}, bf16[240,128]{1,0:T(8,128)(2,1)}, bf16[240,128]{1,0:T(8,128)(2,1)}) custom-call(bf16[1024,128]{1,0:T(8,128)(2,1)} %get-tuple-element.24.refs_0_, bf16[1024,128]{1,0:T(8,128)(2,1)} %copy-done.4, bf16[256,256]{1,0:T(8,128)(2,1)} %get-tuple-element.25.refs_2_, ...), custom_call_target="tpu_custom_call" | custom-call | flops 134217728 | bytes 2097152 | tf_op jit(solution)/shard_map/owner_payloads/pallas_call | solution.py:322
  17.3 1.5 %collective-permute-start.3 = (bf16[240,128]{1,0:T(8,128)(2,1)}, bf16[240,128]{1,0:T(8,128)(2,1)S(1)}, u32[]{:S(2)}, u32[]{:S(2)}) collective-permute-start(bf16[240,128]{1,0:T(8,128)(2,1)} %get-tuple-element.29), channel_id=1, source_target_pairs={{0,0},{1,9},{2,2},{3,11},{4,4},{5,13},{6,6},{7,15},{8,8},{9,1},{10... | collective-permute-start | bytes 184328 | tf_op jit(solution)/shard_map/ppermute | solution.py:672
  18.8 1.5 %collective-permute-start.4 = (bf16[240,128]{1,0:T(8,128)(2,1)}, bf16[240,128]{1,0:T(8,128)(2,1)S(1)}, u32[]{:S(2)}, u32[]{:S(2)}) collective-permute-start(bf16[240,128]{1,0:T(8,128)(2,1)} %get-tuple-element.30), channel_id=1, source_target_pairs={{0,2},{1,11},{2,0},{3,9},{4,6},{5,15},{6,4},{7,13},{8,10},{9,3},{1... | collective-permute-start | bytes 184328 | tf_op jit(solution)/shard_map/ppermute | solution.py:672
  20.3 1.0 %collective-permute-start.5 = (bf16[240,128]{1,0:T(8,128)(2,1)}, bf16[240,128]{1,0:T(8,128)(2,1)S(1)}, u32[]{:S(2)}, u32[]{:S(2)}) collective-permute-start(bf16[240,128]{1,0:T(8,128)(2,1)} %get-tuple-element.31), channel_id=1, source_target_pairs={{0,4},{1,13},{2,6},{3,15},{4,0},{5,9},{6,2},{7,11},{8,12},{9,5},{1... | collective-permute-start | bytes 184328 | tf_op jit(solution)/shard_map/ppermute | solution.py:672
  21.4 0.0 collective-permute-done.14.refs_10_
  21.4 0.9 %collective-permute-start.6 = (bf16[240,128]{1,0:T(8,128)(2,1)}, bf16[240,128]{1,0:T(8,128)(2,1)S(1)}, u32[]{:S(2)}, u32[]{:S(2)}) collective-permute-start(bf16[240,128]{1,0:T(8,128)(2,1)} %get-tuple-element.32), channel_id=1, source_target_pairs={{0,6},{1,15},{2,4},{3,13},{4,2},{5,11},{6,0},{7,9},{8,14},{9,7},{1... | collective-permute-start | bytes 184328 | tf_op jit(solution)/shard_map/ppermute | solution.py:672
  22.3 0.0 collective-permute-done.3.refs_0_
  22.3 1.5 %collective-permute-start.15 = (bf16[2,4,2,4,1024]{4,3,2,1,0:T(4,128)(2,1)S(1)}, bf16[2,4,2,4,1024]{4,3,2,1,0:T(4,128)(2,1)S(1)}, u32[]{:S(2)}, u32[]{:S(2)}) collective-permute-start(bf16[2,4,2,4,1024]{4,3,2,1,0:T(4,128)(2,1)S(1)} %collective-permute-done.14.refs_10_), channel_id=1, source_target_pairs={{0,2},{2,0},{4,6},{6,4},{8,10},{10,8},{12,14},{14,12},{1,3},{3,1},... | collective-permute-start | bytes 393224 | tf_op jit(solution)/shard_map/ppermute | solution.py:645
  23.8 3.3 %collective-permute-start.7 = (bf16[240,128]{1,0:T(8,128)(2,1)S(1)}, bf16[240,128]{1,0:T(8,128)(2,1)S(1)}, u32[]{:S(2)}, u32[]{:S(2)}) collective-permute-start(bf16[240,128]{1,0:T(8,128)(2,1)S(1)} %collective-permute-done.3.refs_0_), channel_id=1, source_target_pairs={{0,1},{1,0},{2,3},{3,2},{4,5},{5,4},{6,7},{7,6},{8,9},{9,8},{10,11... | collective-permute-start | bytes 184328 | tf_op jit(solution)/shard_map/ppermute | solution.py:648
  27.2 0.0 collective-permute-done.4.refs_1_
  27.2 0.1 collective-permute-start.8
  27.2 0.0 collective-permute-done.5.refs_2_
  27.2 0.5 %collective-permute-start.11 = (bf16[2,4,2,4,1024]{4,3,2,1,0:T(4,128)(2,1)S(1)}, bf16[2,4,2,4,1024]{4,3,2,1,0:T(4,128)(2,1)S(1)}, u32[]{:S(2)}, u32[]{:S(2)}) collective-permute-start(bf16[2,4,2,4,1024]{4,3,2,1,0:T(4,128)(2,1)S(1)} %collective-permute-done.1.refs_8_), channel_id=1, source_target_pairs={{0,2},{2,0},{4,6},{6,4},{8,10},{10,8},{12,14},{14,12},{1,3},{3,1},... | collective-permute-start | bytes 393224 | tf_op jit(solution)/shard_map/ppermute | solution.py:645
  27.7 1.5 %collective-permute-start.13 = (bf16[2,4,2,4,1024]{4,3,2,1,0:T(4,128)(2,1)S(1)}, bf16[2,4,2,4,1024]{4,3,2,1,0:T(4,128)(2,1)S(1)}, u32[]{:S(2)}, u32[]{:S(2)}) collective-permute-start(bf16[2,4,2,4,1024]{4,3,2,1,0:T(4,128)(2,1)S(1)} %collective-permute-done.12.refs_10_), channel_id=1, source_target_pairs={{0,2},{2,0},{4,6},{6,4},{8,10},{10,8},{12,14},{14,12},{1,3},{3,1},... | collective-permute-start | bytes 393224 | tf_op jit(solution)/shard_map/ppermute | solution.py:645
  29.3 1.2 %collective-permute-start.9 = (bf16[240,128]{1,0:T(8,128)(2,1)S(1)}, bf16[240,128]{1,0:T(8,128)(2,1)S(1)}, u32[]{:S(2)}, u32[]{:S(2)}) collective-permute-start(bf16[240,128]{1,0:T(8,128)(2,1)S(1)} %collective-permute-done.5.refs_2_), channel_id=1, source_target_pairs={{0,1},{1,0},{2,3},{3,2},{4,5},{5,4},{6,7},{7,6},{8,9},{9,8},{10,11... | collective-permute-start | bytes 184328 | tf_op jit(solution)/shard_map/ppermute | solution.py:648
  30.5 0.1 collective-permute-start.10
  30.6 0.8 %collective-permute-done.9.refs_6_ = bf16[240,128]{1,0:T(8,128)(2,1)S(1)} collective-permute-done((bf16[240,128]{1,0:T(8,128)(2,1)S(1)}, bf16[240,128]{1,0:T(8,128)(2,1)S(1)}, u32[]{:S(2)}, u32[]{:S(2)}) %collective-permute-start.9) | collective-permute-done | bytes 61472 | tf_op jit(solution)/shard_map/ppermute | solution.py:648
  31.4 0.4 collective-permute-done.10.refs_7_
  31.7 0.0 collective-permute-done.15.refs_11_
  31.8 0.7 %copy-done.3 = s32[2,8]{1,0:T(2,128)S(1)} copy-done((s32[2,8]{1,0:T(2,128)S(1)}, s32[2,8]{1,0:T(2,128)}, u32[]{:S(2)}) %copy-start.3) | copy-done | bytes 88
  32.4 4.8 %owner_estimates.2 = (f32[4,8,8,1024]{3,2,1,0:T(8,128)S(1)}, f32[4,8,128]{2,1,0:T(8,128)S(1)}) custom-call(s32[2,8]{1,0:T(2,128)S(1)} %copy-done.3, bf16[240,128]{1,0:T(8,128)(2,1)S(1)} %collective-permute-done.3.refs_0_, bf16[240,128]{1,0:T(8,128)(2,1)S(1)} %collective-permute-done.4.refs_1_, bf16[240,128]{1,0:T(8,128)(2,1)S(1)} %collective-permute-done.5.refs_2_, ...), custom_call_target="tpu_custom_call" | custom-call | flops 536870912 | bytes 8388608 | tf_op jit(solution)/shard_map/owner_estimates/pallas_call | solution.py:594
  37.3 6.2 %owner_estimates.3 = f32[4,8,4,2,1024]{4,3,2,1,0:T(2,128)} custom-call(s32[2,8]{1,0:T(2,128)S(1)} %copy-done.3, bf16[240,128]{1,0:T(8,128)(2,1)S(1)} %collective-permute-done.3.refs_0_, bf16[240,128]{1,0:T(8,128)(2,1)S(1)} %collective-permute-done.4.refs_1_, bf16[240,128]{1,0:T(8,128)(2,1)S(1)} %collective-permute-done.5.refs_2_, ...), custom_call_target="tpu_custom_call" | custom-call | flops 536870912 | bytes 8388608 | tf_op jit(solution)/shard_map/owner_estimates/pallas_call | solution.py:594
  (14 shorter events, 0.0 us)
Async XLA Ops:
  0.0 10.6 %collective-permute-start.1 = (bf16[2,4,2,4,1024]{4,3,2,1,0:T(4,128)(2,1)}, bf16[2,4,2,4,1024]{4,3,2,1,0:T(4,128)(2,1)S(1)}, u32[]{:S(2)}, u32[]{:S(2)}) collective-permute-start(bf16[2,4,2,4,1024]{4,3,2,1,0:T(4,128)(2,1)} %refs_8_.1), channel_id=1, source_target_pairs={{0,8},{2,10},{4,12},{6,14},{8,0},{10,2},{12,4},{14,6},{1,9},{3,11}... | collective-permute-start | bytes 393224 | tf_op jit(solution)/shard_map/ppermute | solution.py:645
  4.0 6.6 %collective-permute-start = (bf16[2,4,2,4,1024]{4,3,2,1,0:T(4,128)(2,1)}, bf16[2,4,2,4,1024]{4,3,2,1,0:T(4,128)(2,1)S(1)}, u32[]{:S(2)}, u32[]{:S(2)}) collective-permute-start(bf16[2,4,2,4,1024]{4,3,2,1,0:T(4,128)(2,1)} %refs_8_.1), channel_id=1, source_target_pairs={{0,2},{2,0},{4,6},{6,4},{8,10},{10,8},{12,14},{14,12},{1,3},{3,1},... | collective-permute-start | bytes 393224 | tf_op jit(solution)/shard_map/ppermute | solution.py:645
  5.6 5.2 %copy-start.2 = (bf16[2,4,2,4,1024]{4,3,2,1,0:T(4,128)(2,1)S(1)}, bf16[2,4,2,4,1024]{4,3,2,1,0:T(4,128)(2,1)}, u32[]{:S(2)}) copy-start(bf16[2,4,2,4,1024]{4,3,2,1,0:T(4,128)(2,1)} %refs_8_.1) | copy-start | bytes 393220
  5.6 26.2 %copy-start = (bf16[2,256,2048]{2,1,0:T(8,128)(2,1)S(1)}, bf16[2,256,2048]{2,1,0:T(8,128)(2,1)}, u32[]{:S(2)}) copy-start(bf16[2,256,2048]{2,1,0:T(8,128)(2,1)} %constant.11.clone.refs_13_) | copy-start | bytes 6291460
  5.6 26.2 %copy-start.1 = (bf16[2,384,1024]{2,1,0:T(8,128)(2,1)S(1)}, bf16[2,384,1024]{2,1,0:T(8,128)(2,1)}, u32[]{:S(2)}) copy-start(bf16[2,384,1024]{2,1,0:T(8,128)(2,1)} %constant.10.clone.refs_12_) | copy-start | bytes 4718596
  10.6 3.6 %collective-permute-start.2 = (bf16[1024,128]{1,0:T(8,128)(2,1)}, bf16[1024,128]{1,0:T(8,128)(2,1)S(1)}, u32[]{:S(2)}, u32[]{:S(2)}) collective-permute-start(bf16[1024,128]{1,0:T(8,128)(2,1)} %get-tuple-element.24.refs_0_), channel_id=1, source_target_pairs={{0,1},{1,0},{2,3},{3,2},{4,5},{5,4},{6,7},{7,6},{8,9},{9,8},{10,11... | collective-permute-start | bytes 786440 | tf_op jit(solution)/shard_map/ppermute | solution.py:648
  10.7 10.6 %collective-permute-start.14 = (bf16[2,4,2,4,1024]{4,3,2,1,0:T(4,128)(2,1)S(1)}, bf16[2,4,2,4,1024]{4,3,2,1,0:T(4,128)(2,1)S(1)}, u32[]{:S(2)}, u32[]{:S(2)}) collective-permute-start(bf16[2,4,2,4,1024]{4,3,2,1,0:T(4,128)(2,1)S(1)} %copy-done.2), channel_id=1, source_target_pairs={{0,4},{2,6},{4,0},{6,2},{8,12},{10,14},{12,8},{14,10},{1,5},{3,7},... | collective-permute-start | bytes 393224 | tf_op jit(solution)/shard_map/ppermute | solution.py:645
  12.4 11.5 %collective-permute-start.12 = (bf16[2,4,2,4,1024]{4,3,2,1,0:T(4,128)(2,1)S(1)}, bf16[2,4,2,4,1024]{4,3,2,1,0:T(4,128)(2,1)S(1)}, u32[]{:S(2)}, u32[]{:S(2)}) collective-permute-start(bf16[2,4,2,4,1024]{4,3,2,1,0:T(4,128)(2,1)S(1)} %copy-done.2), channel_id=1, source_target_pairs={{0,12},{2,14},{4,8},{6,10},{8,4},{10,6},{12,0},{14,2},{1,13},{3,15... | collective-permute-start | bytes 393224 | tf_op jit(solution)/shard_map/ppermute | solution.py:645
  14.3 0.7 %copy-start.4 = (bf16[1024,128]{1,0:T(8,128)(2,1)}, bf16[1024,128]{1,0:T(8,128)(2,1)S(1)}, u32[]{:S(2)}) copy-start(bf16[1024,128]{1,0:T(8,128)(2,1)S(1)} %collective-permute-done.2.refs_1_) | copy-start | bytes 786436
  17.3 5.0 %collective-permute-start.3 = (bf16[240,128]{1,0:T(8,128)(2,1)}, bf16[240,128]{1,0:T(8,128)(2,1)S(1)}, u32[]{:S(2)}, u32[]{:S(2)}) collective-permute-start(bf16[240,128]{1,0:T(8,128)(2,1)} %get-tuple-element.29), channel_id=1, source_target_pairs={{0,0},{1,9},{2,2},{3,11},{4,4},{5,13},{6,6},{7,15},{8,8},{9,1},{10... | collective-permute-start | bytes 184328 | tf_op jit(solution)/shard_map/ppermute | solution.py:672
  18.8 8.3 %collective-permute-start.4 = (bf16[240,128]{1,0:T(8,128)(2,1)}, bf16[240,128]{1,0:T(8,128)(2,1)S(1)}, u32[]{:S(2)}, u32[]{:S(2)}) collective-permute-start(bf16[240,128]{1,0:T(8,128)(2,1)} %get-tuple-element.30), channel_id=1, source_target_pairs={{0,2},{1,11},{2,0},{3,9},{4,6},{5,15},{6,4},{7,13},{8,10},{9,3},{1... | collective-permute-start | bytes 184328 | tf_op jit(solution)/shard_map/ppermute | solution.py:672
  20.3 6.9 %collective-permute-start.5 = (bf16[240,128]{1,0:T(8,128)(2,1)}, bf16[240,128]{1,0:T(8,128)(2,1)S(1)}, u32[]{:S(2)}, u32[]{:S(2)}) collective-permute-start(bf16[240,128]{1,0:T(8,128)(2,1)} %get-tuple-element.31), channel_id=1, source_target_pairs={{0,4},{1,13},{2,6},{3,15},{4,0},{5,9},{6,2},{7,11},{8,12},{9,5},{1... | collective-permute-start | bytes 184328 | tf_op jit(solution)/shard_map/ppermute | solution.py:672
  21.4 6.4 %collective-permute-start.6 = (bf16[240,128]{1,0:T(8,128)(2,1)}, bf16[240,128]{1,0:T(8,128)(2,1)S(1)}, u32[]{:S(2)}, u32[]{:S(2)}) collective-permute-start(bf16[240,128]{1,0:T(8,128)(2,1)} %get-tuple-element.32), channel_id=1, source_target_pairs={{0,6},{1,15},{2,4},{3,13},{4,2},{5,11},{6,0},{7,9},{8,14},{9,7},{1... | collective-permute-start | bytes 184328 | tf_op jit(solution)/shard_map/ppermute | solution.py:672
  22.3 9.4 %collective-permute-start.15 = (bf16[2,4,2,4,1024]{4,3,2,1,0:T(4,128)(2,1)S(1)}, bf16[2,4,2,4,1024]{4,3,2,1,0:T(4,128)(2,1)S(1)}, u32[]{:S(2)}, u32[]{:S(2)}) collective-permute-start(bf16[2,4,2,4,1024]{4,3,2,1,0:T(4,128)(2,1)S(1)} %collective-permute-done.14.refs_10_), channel_id=1, source_target_pairs={{0,2},{2,0},{4,6},{6,4},{8,10},{10,8},{12,14},{14,12},{1,3},{3,1},... | collective-permute-start | bytes 393224 | tf_op jit(solution)/shard_map/ppermute | solution.py:645
  23.8 5.4 %collective-permute-start.7 = (bf16[240,128]{1,0:T(8,128)(2,1)S(1)}, bf16[240,128]{1,0:T(8,128)(2,1)S(1)}, u32[]{:S(2)}, u32[]{:S(2)}) collective-permute-start(bf16[240,128]{1,0:T(8,128)(2,1)S(1)} %collective-permute-done.3.refs_0_), channel_id=1, source_target_pairs={{0,1},{1,0},{2,3},{3,2},{4,5},{5,4},{6,7},{7,6},{8,9},{9,8},{10,11... | collective-permute-start | bytes 184328 | tf_op jit(solution)/shard_map/ppermute | solution.py:648
  27.2 3.3 %collective-permute-start.8 = (bf16[240,128]{1,0:T(8,128)(2,1)S(1)}, bf16[240,128]{1,0:T(8,128)(2,1)S(1)}, u32[]{:S(2)}, u32[]{:S(2)}) collective-permute-start(bf16[240,128]{1,0:T(8,128)(2,1)S(1)} %collective-permute-done.4.refs_1_), channel_id=1, source_target_pairs={{0,1},{1,0},{2,3},{3,2},{4,5},{5,4},{6,7},{7,6},{8,9},{9,8},{10,11... | collective-permute-start | bytes 184328 | tf_op jit(solution)/shard_map/ppermute | solution.py:648
  27.2 10.0 %collective-permute-start.11 = (bf16[2,4,2,4,1024]{4,3,2,1,0:T(4,128)(2,1)S(1)}, bf16[2,4,2,4,1024]{4,3,2,1,0:T(4,128)(2,1)S(1)}, u32[]{:S(2)}, u32[]{:S(2)}) collective-permute-start(bf16[2,4,2,4,1024]{4,3,2,1,0:T(4,128)(2,1)S(1)} %collective-permute-done.1.refs_8_), channel_id=1, source_target_pairs={{0,2},{2,0},{4,6},{6,4},{8,10},{10,8},{12,14},{14,12},{1,3},{3,1},... | collective-permute-start | bytes 393224 | tf_op jit(solution)/shard_map/ppermute | solution.py:645
  27.7 9.5 %collective-permute-start.13 = (bf16[2,4,2,4,1024]{4,3,2,1,0:T(4,128)(2,1)S(1)}, bf16[2,4,2,4,1024]{4,3,2,1,0:T(4,128)(2,1)S(1)}, u32[]{:S(2)}, u32[]{:S(2)}) collective-permute-start(bf16[2,4,2,4,1024]{4,3,2,1,0:T(4,128)(2,1)S(1)} %collective-permute-done.12.refs_10_), channel_id=1, source_target_pairs={{0,2},{2,0},{4,6},{6,4},{8,10},{10,8},{12,14},{14,12},{1,3},{3,1},... | collective-permute-start | bytes 393224 | tf_op jit(solution)/shard_map/ppermute | solution.py:645
  29.3 2.1 %collective-permute-start.9 = (bf16[240,128]{1,0:T(8,128)(2,1)S(1)}, bf16[240,128]{1,0:T(8,128)(2,1)S(1)}, u32[]{:S(2)}, u32[]{:S(2)}) collective-permute-start(bf16[240,128]{1,0:T(8,128)(2,1)S(1)} %collective-permute-done.5.refs_2_), channel_id=1, source_target_pairs={{0,1},{1,0},{2,3},{3,2},{4,5},{5,4},{6,7},{7,6},{8,9},{9,8},{10,11... | collective-permute-start | bytes 184328 | tf_op jit(solution)/shard_map/ppermute | solution.py:648
  30.5 1.2 %collective-permute-start.10 = (bf16[240,128]{1,0:T(8,128)(2,1)S(1)}, bf16[240,128]{1,0:T(8,128)(2,1)S(1)}, u32[]{:S(2)}, u32[]{:S(2)}) collective-permute-start(bf16[240,128]{1,0:T(8,128)(2,1)S(1)} %collective-permute-done.6.refs_3_), channel_id=1, source_target_pairs={{0,1},{1,0},{2,3},{3,2},{4,5},{5,4},{6,7},{7,6},{8,9},{9,8},{10,11... | collective-permute-start | bytes 184328 | tf_op jit(solution)/shard_map/ppermute | solution.py:648
  31.8 0.7 %copy-start.3 = (s32[2,8]{1,0:T(2,128)S(1)}, s32[2,8]{1,0:T(2,128)}, u32[]{:S(2)}) copy-start(s32[2,8]{1,0:T(2,128)} %get-tuple-element.22.slots) | copy-start | bytes 196

commit v4 on v3

--- a/solution.py
+++ b/solution.py
@@ -18,7 +18,9 @@
 EARLY = (1, 4)
 SAMPLES = 2 * TAPS
 ROWS = PEER_MAX * CU
-LARGE_BYTES = 58 * 1024 * 1024
+LARGE_BYTES = 52 * 1024 * 1024
+SMALL_BYTES = 24 * 1024 * 1024
+TABLE_ROWS = 32 * 1024
 VMEM_BYTES = 36 * 1024 * 1024
 F32 = jnp.float32
 BF16 = jnp.bfloat16
@@ -69,6 +71,14 @@
 def sample_table():
     real, imag = rebuild_columns(np.arange(SAMPLES) * (TONE_NUMBER // SAMPLES))
     return np.concatenate([real, imag], axis=1)
+
+
+def first_tables(shards, width):
+    forward = forward_tables(shards, width).reshape(shards * 2 * width, 2 * TAPS)
+    samples = sample_table()
+    rows = np.concatenate([forward, samples[:, :SAMPLES], samples[:, SAMPLES:]], axis=0)
+    filling = max(0, TABLE_ROWS - rows.shape[0])
+    return np.concatenate([rows, np.zeros((filling, 2 * TAPS), ml_dtypes.bfloat16)], axis=0)
 
 
 def dirichlet_tables(shards, width):
@@ -109,25 +119,37 @@
     )
 
 
-def find_routes(shape, power, noise, gain, cluster_row, serving, owner, pick_out, weight_out, slots, extras):
+def pack_rows(power, noise, gain, cluster, serving, owner):
+    width = max(power.shape[0], serving.shape[1], serving.shape[0])
+    rows = [
+        power[None, :], gain, cluster.astype(F32)[None, :], serving.astype(F32),
+        owner.astype(F32).reshape(1, -1), noise[None, :],
+    ]
+    return jnp.concatenate([jnp.pad(x, ((0, 0), (0, width - x.shape[1]))) for x in rows], axis=0)
+
+
+def find_routes(shape, clusters, packed, pick_out, weight_out, slots, extras):
     aps, antennas, users, devices, shards = shape
     per = devices // shards
     device, core = lax.axis_index("ap"), lax.axis_index("sc")
-    clusters = serving.shape[0]
+    power = packed[pl.ds(0, 1), :][:, :users]
+    gain = [packed[pl.ds(1 + a, 1), :][:, :users] for a in range(aps)]
+    cluster_row = packed[pl.ds(1 + aps, 1), :][:, :users]
+    serving_f = packed[pl.ds(2 + aps, clusters), :][:, : aps * devices]
+    owner_row = packed[pl.ds(2 + aps + clusters, 1), :][:, :clusters]
+    noise = packed[pl.ds(3 + aps + clusters, 1), :]
     extras[pl.ds(0, users), :] = jnp.broadcast_to(
-        column_of(power[...]) * (1.0 / users), (users, SAMPLES)
+        column_of(power) * (1.0 / users), (users, SAMPLES)
     )
     for a in range(aps):
         extras[pl.ds(users + a, 1), :] = jnp.broadcast_to(noise[:, a : a + 1], (1, SAMPLES))
 
-    serving_f = serving[...].astype(F32)
-    columns = serving.shape[1]
+    columns = aps * devices
     pairs = (iota((columns, devices), 0) // aps == iota((columns, devices), 1)).astype(F32)
     served = (jnp.dot(serving_f, pairs, preferred_element_type=F32) > 0.5).astype(F32)
     served_here = jnp.sum(
         jnp.where(iota((clusters, devices), 1) == device, served, 0.0), axis=1, keepdims=True
     )
-    owner_row = owner[...].astype(F32)
     owner_f = column_of(owner_row)
     owner_col = owner_f.astype(jnp.int32)
     square = (clusters, clusters)
@@ -137,7 +159,7 @@
     label = (owner_col ^ device) ^ (core * per)
     valid = (served_here > 0.5) & (label < per)
     base = jnp.where(valid, label.astype(F32) * ROWS + turn * CU, -4.0 * ROWS * devices)
-    members = (iota((clusters, users), 0) == cluster_row[...]).astype(F32)
+    members = (iota((clusters, users), 0).astype(F32) == cluster_row).astype(F32)
     prefix = (iota((users, users), 0) < iota((users, users), 1)).astype(F32)
     order = jnp.dot(members, prefix, preferred_element_type=F32)
     target = jnp.sum(members * (order + base), axis=0, keepdims=True).astype(jnp.int32)
@@ -149,7 +171,7 @@
         column = iota((clusters, columns), 1) == device * aps + a
         mine = jnp.sum(jnp.where(column, serving_f, 0.0), axis=1, keepdims=True)
         weight_rows.append(
-            jnp.sum(members * mine, axis=0, keepdims=True) * gain[pl.ds(a, 1), :]
+            jnp.sum(members * mine, axis=0, keepdims=True) * gain[a]
         )
     stacked = jnp.concatenate(weight_rows + [jnp.zeros((8 - aps, users), F32)], axis=0)
     weight_parts = jnp.concatenate(
@@ -170,41 +192,42 @@
         slots[pl.ds(p, 1), :] = jnp.sum(hit * rank, axis=0, keepdims=True).astype(jnp.int32)
 
 
-def coefficient_kernel(shape, *refs):
+def coefficient_kernel(shape, clusters, *refs):
     aps, antennas, users, devices, shards = shape
-    guesses, table, samples = refs[:3]
-    small = refs[3:9]
-    out, samples_out, pick, weights, slots, extras = refs[9:15]
-    held, tables, *held_small = refs[15:23]
-    held_sem, table_sem, small_sem = refs[23:]
-    small_copies = [
-        pltpu.make_async_copy(src, dst, small_sem.at[k])
-        for k, (src, dst) in enumerate(zip(small, held_small))
+    guesses, table, packed = refs[:3]
+    out, samples, pick, weights, slots, extras = refs[3:9]
+    held, tables, held_sem, table_sem = refs[9:]
+    tones = held.shape[-1]
+    first = pl.multiple_of(lax.axis_index("sc") * 2 * tones, 16)
+    table_copy = pltpu.make_async_copy(table.at[pl.ds(first, 2 * tones)], tables, table_sem.at[0])
+    sample_copies = [
+        pltpu.make_async_copy(
+            table.at[pl.ds(shards * 2 * tones + c * 4 * TAPS, 4 * TAPS)],
+            samples.at[:, pl.ds(c * SAMPLES, SAMPLES)],
+            table_sem.at[1 + c],
+        )
+        for c in range(2)
     ]
-    table_copy = pltpu.make_async_copy(table.at[lax.axis_index("sc")], tables, table_sem.at[0])
-    sample_copy = pltpu.make_async_copy(samples, samples_out, table_sem.at[1])
     big = [
         pltpu.make_async_copy(guesses.at[a, i], held.at[a * antennas + i], held_sem.at[a * antennas + i])
         for a in range(aps)
         for i in range(antennas)
     ]
-    for copy in small_copies + [table_copy] + big + [sample_copy]:
+    for copy in [table_copy] + big + sample_copies:
         copy.start()
-    for copy in small_copies:
-        copy.wait()
-    find_routes(shape, *held_small, pick, weights, slots, extras)
+    find_routes(shape, clusters, packed, pick, weights, slots, extras)
     table_copy.wait()
     group = math.gcd(2, antennas)
-    tones = held.shape[-1]
     for first in range(0, aps * antennas, group):
         for k in range(group):
             big[first + k].wait()
         real = held[pl.ds(first, group), 0].reshape(group * users, tones)
         imag = held[pl.ds(first, group), 1].reshape(group * users, tones)
-        total = jnp.dot(real, tables[0], preferred_element_type=F32)
-        total = total + jnp.dot(imag, tables[1], preferred_element_type=F32)
+        total = jnp.dot(real, tables[pl.ds(0, tones), :], preferred_element_type=F32)
+        total = total + jnp.dot(imag, tables[pl.ds(tones, tones), :], preferred_element_type=F32)
         out[pl.ds(first * users, group * users), :] = (total * (1.0 / TONE_NUMBER)).astype(BF16)
-    sample_copy.wait()
+    for copy in sample_copies:
+        copy.wait()
 
 
 def delay_coefficients(guesses, power, noise, gain, cluster, serving, owner, shape):
@@ -212,21 +235,17 @@
     per = devices // shards
     tones = guesses.shape[-1]
     clusters = serving.shape[0]
-    table = jnp.asarray(forward_tables(shards, tones))
-    samples = jnp.asarray(sample_table())
-    small = [
-        power.reshape(1, users), noise.reshape(1, aps), gain, cluster.reshape(1, users), serving,
-        owner.reshape(1, clusters),
-    ]
+    table = jnp.asarray(first_tables(shards, tones))
+    packed = pack_rows(power, noise, gain, cluster, serving, owner)
     hbm = pl.BlockSpec(memory_space=pltpu.HBM)
     vmem = pl.BlockSpec(memory_space=pltpu.VMEM)
     return pl.pallas_call(
-        functools.partial(coefficient_kernel, shape),
-        in_specs=[hbm] * (3 + len(small)),
+        functools.partial(coefficient_kernel, shape, clusters),
+        in_specs=[hbm, hbm, vmem],
         out_specs=[vmem] * 6,
         out_shape=[
             jax.ShapeDtypeStruct((aps * antennas * users, 2 * TAPS), BF16),
-            jax.ShapeDtypeStruct(samples.shape, BF16),
+            jax.ShapeDtypeStruct((4 * TAPS, 2 * SAMPLES), BF16),
             jax.ShapeDtypeStruct((per * ROWS, users), BF16),
             jax.ShapeDtypeStruct((per * ROWS, 2 * TAPS), BF16),
             jax.ShapeDtypeStruct((PEER_MAX, devices), jnp.int32),
@@ -234,20 +253,16 @@
         ],
         scratch_shapes=[
             pltpu.VMEM((aps * antennas, 2, users, tones), BF16),
-            pltpu.VMEM((2, tones, 2 * TAPS), BF16),
-        ]
-        + [pltpu.VMEM(x.shape, x.dtype) for x in small]
-        + [
+            pltpu.VMEM((2 * tones, 2 * TAPS), BF16),
             pltpu.SemaphoreType.DMA((aps * antennas,)),
-            pltpu.SemaphoreType.DMA((2,)),
-            pltpu.SemaphoreType.DMA((len(small),)),
+            pltpu.SemaphoreType.DMA((3,)),
         ],
         compiler_params=pltpu.CompilerParams(vmem_limit_bytes=LARGE_BYTES),
         cost_estimate=pl.CostEstimate(
             flops=4 * guesses.size * TAPS, bytes_accessed=2 * guesses.size, transcendentals=0
         ),
         name="delay_coefficients",
-    )(guesses, table, samples, *small)
+    )(guesses, table, packed)
 
 
 def payload_kernel(shape, *refs):
@@ -318,19 +333,18 @@
     per = devices // shards
     rows = payload_rows(aps, antennas)
     operands = list(parts) + [table, pick, weights, extras]
-    whole = lambda dims: pl.BlockSpec(dims, lambda g: (0,) * len(dims))
+    vmem = pl.BlockSpec(memory_space=pltpu.VMEM)
     return pl.pallas_call(
         functools.partial(payload_kernel, shape),
-        grid=(1,),
-        in_specs=[whole(x.shape) for x in operands],
-        out_specs=[whole((rows, 2 * TAPS))] * per,
+        in_specs=[vmem] * len(operands),
+        out_specs=[vmem] * per,
         out_shape=[jax.ShapeDtypeStruct((rows, 2 * TAPS), BF16)] * per,
         scratch_shapes=[
             pltpu.VMEM((aps * antennas * users, 4 * TAPS), BF16),
             pltpu.VMEM((aps * antennas * users, 2 * SAMPLES), F32),
             pltpu.VMEM((aps * antennas * antennas, SAMPLES), F32),
         ],
-        compiler_params=pltpu.CompilerParams(vmem_limit_bytes=LARGE_BYTES),
+        compiler_params=pltpu.CompilerParams(vmem_limit_bytes=SMALL_BYTES),
         cost_estimate=pl.CostEstimate(
             flops=4 * aps * antennas * users * 4 * TAPS * SAMPLES,
             bytes_accessed=2 * 1024 * 1024,

time: 43.7 us -> 42.4 us (0.970)
  Pallas kernels: 18.5 us -> 15.2 us
  other arithmetic: 0 us -> 2.01 us
  starting transfers between devices: 22.3 us -> 21.4 us
  waiting for transfers between devices: 1.21 us -> 1.87 us
    pallas_call x2, Pallas kernels: 7.43 us -> 4.17 us  [the longest x1 3.63 us: delay_coefficients(): pl.pallas_call(functools.partial(coefficient_kernel, shape, clusters), in...]
    unnamed x10 -> x6, local copies, waits for them, and re-layouts: 1.37 us -> 0.02 us
    ppermute x7, starting transfers between devices: 12.6 us -> 11.7 us  [swap_ap(): return lax.ppermute(value, 'ap', [(i, i ^ v) for i in range(devices)])]
    concatenate x0 -> x1, local copies, waits for them, and re-layouts: none -> 0.8 us  [pack_rows(): jnp.concatenate([jnp.pad(x, ((0, 0), (0, width - x.shape[1]))) for x in r...]
    convert_element_type x0 -> x1, other arithmetic: none -> 0.7 us  [pack_rows(): serving.astype(F32)]
    pad x0 -> x3, local copies, waits for them, and re-layouts: none -> 0.67 us  [pack_rows(): jnp.pad(x, ((0, 0), (0, width - x.shape[1])))]
    broadcast_in_dim x0 -> x1, other arithmetic: none -> 0.66 us  [pack_rows(): cluster.astype(F32)[None, :]]
    reshape x0 -> x1, other arithmetic: none -> 0.66 us  [pack_rows(): owner.astype(F32).reshape(1, -1)]
  transfers between devices with their start and end apart: 16 -> 16, of which waited for: 2 -> 3; matrix products, arithmetic and copies ran while one was open for 0% -> 8% of each run, Pallas kernels for 28% -> 21%
where the time goes in v4:
time: 42.4 us; the launch traced here: 42.1 us
  starting transfers between devices  21.4 us (50%)
  Pallas kernels  15.2 us (36%)
  other arithmetic  2.01 us (5%)
  waiting for transfers between devices  1.87 us (4%)
  local copies, waits for them, and re-layouts  1.49 us (4%)
    ppermute x7, starting transfers between devices, swap_ap(): return lax.ppermute(value, 'ap', [(i, i ^ v) for i in range(devices)])  11.7 us
    pallas_call x2, Pallas kernels, owner_estimates(): pl.pallas_call(functools.partial(estimate_kernel, shape, chunk, group), i...  11.1 us
    ppermute x5, starting transfers between devices, swap_sc(): return lax.ppermute(value, 'sc', [(c, c ^ h) for c in range(shards)])  4.87 us
    ppermute x4, starting transfers between devices, local(): own = [lax.ppermute(blocks[j], ('ap', 'sc'), pairs(j)) for j in range(per)]  4.83 us
    pallas_call x1, Pallas kernels, delay_coefficients(): pl.pallas_call(functools.partial(coefficient_kernel, shape, clusters), in...  3.63 us
    ppermute x5, waiting for transfers between devices, swap_sc(): return lax.ppermute(value, 'sc', [(c, c ^ h) for c in range(shards)])  1.19 us
  transfers between devices with their start and end apart: 16, of which 3 were waited for; matrix products, arithmetic and copies ran while one was open for 8% of the time, Pallas kernels for 21%

profile of v4, /device:TPU:0, one launch (start us, length us, event | category | flops | bytes accessed | tf_op | source)
XLA Modules:
  0.0 42.1 jit_solution(1095615197849969992)
XLA Ops:
  0.0 4.0 %collective-permute-start.1 = (bf16[2,4,2,4,1024]{4,3,2,1,0:T(4,128)(2,1)}, bf16[2,4,2,4,1024]{4,3,2,1,0:T(4,128)(2,1)S(1)}, u32[]{:S(2)}, u32[]{:S(2)}) collective-permute-start(bf16[2,4,2,4,1024]{4,3,2,1,0:T(4,128)(2,1)} %refs_8_.1), channel_id=1, source_target_pairs={{0,8},{2,10},{4,12},{6,14},{8,0},{10,2},{12,4},{14,6},{1,9},{3,11}... | collective-permute-start | bytes 393224 | tf_op jit(solution)/shard_map/ppermute | solution.py:659
  4.0 1.5 %collective-permute-start = (bf16[2,4,2,4,1024]{4,3,2,1,0:T(4,128)(2,1)}, bf16[2,4,2,4,1024]{4,3,2,1,0:T(4,128)(2,1)S(1)}, u32[]{:S(2)}, u32[]{:S(2)}) collective-permute-start(bf16[2,4,2,4,1024]{4,3,2,1,0:T(4,128)(2,1)} %refs_8_.1), channel_id=1, source_target_pairs={{0,2},{2,0},{4,6},{6,4},{8,10},{10,8},{12,14},{14,12},{1,3},{3,1},... | collective-permute-start | bytes 393224 | tf_op jit(solution)/shard_map/ppermute | solution.py:659
  5.6 0.7 %convert_bitcast_fusion.1 = f32[1,128]{1,0:T(1,128)S(1)} fusion(s32[128]{0:T(128)} %param.18), kind=kLoop, calls=%fused_computation.1 | loop fusion | flops 128 | bytes 1024 | tf_op jit(solution)/shard_map/broadcast_in_dim | solution.py:125
  6.2 0.7 %convert_bitcast_fusion = f32[1,16]{1,0:T(1,128)S(1)} fusion(s32[16,1]{0,1:T(1,128)} %param.20), kind=kLoop, calls=%fused_computation | loop fusion | flops 16 | bytes 128 | tf_op jit(solution)/shard_map/reshape | solution.py:126
  6.9 0.7 %pad.14 = f32[1,128]{1,0:T(1,128)S(1)} pad(f32[1,2]{1,0:T(1,128)} %bitcast.7, f32[]{:T(128)} %constant.8.clone.1), padding=0_0x0_126 | pad | bytes 524 | tf_op jit(solution)/shard_map/jit(_pad)/pad | solution.py:128
  7.5 0.7 %convert_element_type.16 = f32[16,16]{1,0:T(8,128)S(1)} convert(s32[16,16]{1,0:T(8,128)} %param.19) | non-fusion elementwise | flops 256 | bytes 2048 | tf_op jit(solution)/shard_map/convert_element_type | solution.py:125
  8.2 0.8 %concatenate.3.refs_2_ = f32[22,128]{1,0:T(8,128)S(1)} concatenate(f32[1,128]{1,0:T(1,128)} %bitcast.6, f32[2,128]{1,0:T(2,128)} %param.17, f32[1,128]{1,0:T(1,128)S(1)} %convert_bitcast_fusion.1, f32[16,128]{1,0:T(8,128)S(1)} %pad.12, f32[1,128]{1,0:T(1,128)S(1)} %pad.13, f32[1,128]{1,0:T(1,128)S(1)} %pad.14), dimensions={0} | concatenate | bytes 22528 | tf_op jit(solution)/shard_map/concatenate | solution.py:128
  9.1 0.0 copy-start
  9.1 0.0 copy-start.1
  9.1 3.6 %delay_coefficients.1 = (bf16[1024,128]{1,0:T(8,128)(2,1)S(1)}, bf16[256,256]{1,0:T(8,128)(2,1)S(1)}, bf16[64,128]{1,0:T(8,128)(2,1)S(1)}, bf16[64,128]{1,0:T(8,...) custom-call(bf16[2,4,2,128,1024]{4,3,2,1,0:T(8,128)(2,1)} %refs_0_.1, ...), custom_call_target="tpu_custom_call" | custom-call | flops 536870912 | bytes 4194304 | tf_op jit(solution)/shard_map/delay_coefficients/pallas_call | solution.py:242
  12.7 0.0 collective-permute-done.1.refs_8_
  12.7 0.1 collective-permute-start.2
  12.8 1.6 %collective-permute-start.14 = (bf16[2,4,2,4,1024]{4,3,2,1,0:T(4,128)(2,1)S(1)}, bf16[2,4,2,4,1024]{4,3,2,1,0:T(4,128)(2,1)S(1)}, u32[]{:S(2)}, u32[]{:S(2)}) collective-permute-start(bf16[2,4,2,4,1024]{4,3,2,1,0:T(4,128)(2,1)S(1)} %copy-done.2), channel_id=1, source_target_pairs={{0,4},{2,6},{4,0},{6,2},{8,12},{10,14},{12,8},{14,10},{1,5},{3,7},... | collective-permute-start | bytes 393224 | tf_op jit(solution)/shard_map/ppermute | solution.py:659
  14.5 0.2 collective-permute-start.12
  14.7 0.5 %owner_payloads.1 = (bf16[240,128]{1,0:T(8,128)(2,1)S(1)}, bf16[240,128]{1,0:T(8,128)(2,1)S(1)}, bf16[240,128]{1,0:T(8,128)(2,1)S(1)}, bf16[240,128]{1,0:T(8,128)(2,1)S(1)}) custom-call(bf16[1024,128]{1,0:T(8,128)(2,1)S(1)} %get-tuple-element.24.refs_0_, bf16[1024,128]{1,0:T(8,128)(2,1)S(1)} %collective-permute-done.2.refs_1_, ...), custom_call_target="tpu_custom_call" | custom-call | flops 134217728 | bytes 2097152 | tf_op jit(solution)/shard_map/owner_payloads/pallas_call | solution.py:337
  15.2 0.7 %collective-permute-start.3 = (bf16[240,128]{1,0:T(8,128)(2,1)S(1)}, bf16[240,128]{1,0:T(8,128)(2,1)S(1)}, u32[]{:S(2)}, u32[]{:S(2)}) collective-permute-start(bf16[240,128]{1,0:T(8,128)(2,1)S(1)} %get-tuple-element.29), channel_id=1, source_target_pairs={{0,0},{1,9},{2,2},{3,11},{4,4},{5,13},{6,6},{7,15},{8,8},{9,1},{10... | collective-permute-start | bytes 184328 | tf_op jit(solution)/shard_map/ppermute | solution.py:686
  15.9 1.2 %collective-permute-start.4 = (bf16[240,128]{1,0:T(8,128)(2,1)S(1)}, bf16[240,128]{1,0:T(8,128)(2,1)S(1)}, u32[]{:S(2)}, u32[]{:S(2)}) collective-permute-start(bf16[240,128]{1,0:T(8,128)(2,1)S(1)} %get-tuple-element.30), channel_id=1, source_target_pairs={{0,2},{1,11},{2,0},{3,9},{4,6},{5,15},{6,4},{7,13},{8,10},{9,3},{1... | collective-permute-start | bytes 184328 | tf_op jit(solution)/shard_map/ppermute | solution.py:686
  17.1 1.0 %collective-permute-start.5 = (bf16[240,128]{1,0:T(8,128)(2,1)S(1)}, bf16[240,128]{1,0:T(8,128)(2,1)S(1)}, u32[]{:S(2)}, u32[]{:S(2)}) collective-permute-start(bf16[240,128]{1,0:T(8,128)(2,1)S(1)} %get-tuple-element.31), channel_id=1, source_target_pairs={{0,4},{1,13},{2,6},{3,15},{4,0},{5,9},{6,2},{7,11},{8,12},{9,5},{1... | collective-permute-start | bytes 184328 | tf_op jit(solution)/shard_map/ppermute | solution.py:686
  18.1 0.6 %collective-permute-done.14.refs_10_ = bf16[2,4,2,4,1024]{4,3,2,1,0:T(4,128)(2,1)S(1)} collective-permute-done((bf16[2,4,2,4,1024]{4,3,2,1,0:T(4,128)(2,1)S(1)}, bf16[2,4,2,4,1024]{4,3,2,1,0:T(4,128)(2,1)S(1)}, u32[]{:S(2)}, u32[]{:S(2)}) %collective-permute-start.14) | collective-permute-done | bytes 131104 | tf_op jit(solution)/shard_map/ppermute | solution.py:659
  18.7 2.0 %collective-permute-start.6 = (bf16[240,128]{1,0:T(8,128)(2,1)S(1)}, bf16[240,128]{1,0:T(8,128)(2,1)S(1)}, u32[]{:S(2)}, u32[]{:S(2)}) collective-permute-start(bf16[240,128]{1,0:T(8,128)(2,1)S(1)} %get-tuple-element.32), channel_id=1, source_target_pairs={{0,6},{1,15},{2,4},{3,13},{4,2},{5,11},{6,0},{7,9},{8,14},{9,7},{1... | collective-permute-start | bytes 184328 | tf_op jit(solution)/shard_map/ppermute | solution.py:686
  20.7 1.5 %collective-permute-start.15 = (bf16[2,4,2,4,1024]{4,3,2,1,0:T(4,128)(2,1)S(1)}, bf16[2,4,2,4,1024]{4,3,2,1,0:T(4,128)(2,1)S(1)}, u32[]{:S(2)}, u32[]{:S(2)}) collective-permute-start(bf16[2,4,2,4,1024]{4,3,2,1,0:T(4,128)(2,1)S(1)} %collective-permute-done.14.refs_10_), channel_id=1, source_target_pairs={{0,2},{2,0},{4,6},{6,4},{8,10},{10,8},{12,14},{14,12},{1,3},{3,1},... | collective-permute-start | bytes 393224 | tf_op jit(solution)/shard_map/ppermute | solution.py:659
  22.2 0.0 collective-permute-done.12.refs_10_
  22.3 2.4 %collective-permute-start.7 = (bf16[240,128]{1,0:T(8,128)(2,1)S(1)}, bf16[240,128]{1,0:T(8,128)(2,1)S(1)}, u32[]{:S(2)}, u32[]{:S(2)}) collective-permute-start(bf16[240,128]{1,0:T(8,128)(2,1)S(1)} %collective-permute-done.3.refs_0_), channel_id=1, source_target_pairs={{0,1},{1,0},{2,3},{3,2},{4,5},{5,4},{6,7},{7,6},{8,9},{9,8},{10,11... | collective-permute-start | bytes 184328 | tf_op jit(solution)/shard_map/ppermute | solution.py:662
  24.6 0.1 collective-permute-start.8
  24.7 2.7 %collective-permute-start.11 = (bf16[2,4,2,4,1024]{4,3,2,1,0:T(4,128)(2,1)S(1)}, bf16[2,4,2,4,1024]{4,3,2,1,0:T(4,128)(2,1)S(1)}, u32[]{:S(2)}, u32[]{:S(2)}) collective-permute-start(bf16[2,4,2,4,1024]{4,3,2,1,0:T(4,128)(2,1)S(1)} %collective-permute-done.1.refs_8_), channel_id=1, source_target_pairs={{0,2},{2,0},{4,6},{6,4},{8,10},{10,8},{12,14},{14,12},{1,3},{3,1},... | collective-permute-start | bytes 393224 | tf_op jit(solution)/shard_map/ppermute | solution.py:659
  27.4 0.1 collective-permute-start.13
  27.5 2.3 %collective-permute-start.9 = (bf16[240,128]{1,0:T(8,128)(2,1)S(1)}, bf16[240,128]{1,0:T(8,128)(2,1)S(1)}, u32[]{:S(2)}, u32[]{:S(2)}) collective-permute-start(bf16[240,128]{1,0:T(8,128)(2,1)S(1)} %collective-permute-done.5.refs_2_), channel_id=1, source_target_pairs={{0,1},{1,0},{2,3},{3,2},{4,5},{5,4},{6,7},{7,6},{8,9},{9,8},{10,11... | collective-permute-start | bytes 184328 | tf_op jit(solution)/shard_map/ppermute | solution.py:662
  29.8 0.1 collective-permute-start.10
  29.8 0.8 %collective-permute-done.9.refs_6_ = bf16[240,128]{1,0:T(8,128)(2,1)S(1)} collective-permute-done((bf16[240,128]{1,0:T(8,128)(2,1)S(1)}, bf16[240,128]{1,0:T(8,128)(2,1)S(1)}, u32[]{:S(2)}, u32[]{:S(2)}) %collective-permute-start.9) | collective-permute-done | bytes 61472 | tf_op jit(solution)/shard_map/ppermute | solution.py:662
  30.7 0.4 collective-permute-done.10.refs_7_
  31.0 4.9 %owner_estimates.2 = (f32[4,8,8,1024]{3,2,1,0:T(8,128)S(1)}, f32[4,8,128]{2,1,0:T(8,128)S(1)}) custom-call(s32[2,8]{1,0:T(2,128)S(1)} %get-tuple-element.22.slots, bf16[240,128]{1,0:T(8,128)(2,1)S(1)} %collective-permute-done.3.refs_0_, bf16[240,128]{1,0:T(8,128)(2,1)S(1)} %collective-permute-done.4.refs_1_, ...), custom_call_target="tpu_custom_call" | custom-call | flops 536870912 | bytes 8388608 | tf_op jit(solution)/shard_map/owner_estimates/pallas_call | solution.py:608
  35.9 6.2 %owner_estimates.3 = f32[4,8,4,2,1024]{4,3,2,1,0:T(2,128)} custom-call(s32[2,8]{1,0:T(2,128)S(1)} %get-tuple-element.22.slots, bf16[240,128]{1,0:T(8,128)(2,1)S(1)} %collective-permute-done.3.refs_0_, bf16[240,128]{1,0:T(8,128)(2,1)S(1)} %collective-permute-done.4.refs_1_, bf16[240,128]{1,0:T(8,128)(2,1)S(1)} %collective-permute-done.5.refs_2_, ...), custom_call_target="tpu_custom_call" | custom-call | flops 536870912 | bytes 8388608 | tf_op jit(solution)/shard_map/owner_estimates/pallas_call | solution.py:608
  (17 shorter events, 0.0 us)
Async XLA Ops:
  0.0 12.7 %collective-permute-start.1 = (bf16[2,4,2,4,1024]{4,3,2,1,0:T(4,128)(2,1)}, bf16[2,4,2,4,1024]{4,3,2,1,0:T(4,128)(2,1)S(1)}, u32[]{:S(2)}, u32[]{:S(2)}) collective-permute-start(bf16[2,4,2,4,1024]{4,3,2,1,0:T(4,128)(2,1)} %refs_8_.1), channel_id=1, source_target_pairs={{0,8},{2,10},{4,12},{6,14},{8,0},{10,2},{12,4},{14,6},{1,9},{3,11}... | collective-permute-start | bytes 393224 | tf_op jit(solution)/shard_map/ppermute | solution.py:659
  4.0 8.7 %collective-permute-start = (bf16[2,4,2,4,1024]{4,3,2,1,0:T(4,128)(2,1)}, bf16[2,4,2,4,1024]{4,3,2,1,0:T(4,128)(2,1)S(1)}, u32[]{:S(2)}, u32[]{:S(2)}) collective-permute-start(bf16[2,4,2,4,1024]{4,3,2,1,0:T(4,128)(2,1)} %refs_8_.1), channel_id=1, source_target_pairs={{0,2},{2,0},{4,6},{6,4},{8,10},{10,8},{12,14},{14,12},{1,3},{3,1},... | collective-permute-start | bytes 393224 | tf_op jit(solution)/shard_map/ppermute | solution.py:659
  9.0 3.8 %copy-start.2 = (bf16[2,4,2,4,1024]{4,3,2,1,0:T(4,128)(2,1)S(1)}, bf16[2,4,2,4,1024]{4,3,2,1,0:T(4,128)(2,1)}, u32[]{:S(2)}) copy-start(bf16[2,4,2,4,1024]{4,3,2,1,0:T(4,128)(2,1)} %refs_8_.1) | copy-start | bytes 393220
  9.1 22.0 %copy-start = (bf16[2,256,2048]{2,1,0:T(8,128)(2,1)S(1)}, bf16[2,256,2048]{2,1,0:T(8,128)(2,1)}, u32[]{:S(2)}) copy-start(bf16[2,256,2048]{2,1,0:T(8,128)(2,1)} %constant.11.clone.refs_13_) | copy-start | bytes 6291460
  9.1 22.0 %copy-start.1 = (bf16[2,384,1024]{2,1,0:T(8,128)(2,1)S(1)}, bf16[2,384,1024]{2,1,0:T(8,128)(2,1)}, u32[]{:S(2)}) copy-start(bf16[2,384,1024]{2,1,0:T(8,128)(2,1)} %constant.10.clone.refs_12_) | copy-start | bytes 4718596
  12.7 2.0 %collective-permute-start.2 = (bf16[1024,128]{1,0:T(8,128)(2,1)S(1)}, bf16[1024,128]{1,0:T(8,128)(2,1)S(1)}, u32[]{:S(2)}, u32[]{:S(2)}) collective-permute-start(bf16[1024,128]{1,0:T(8,128)(2,1)S(1)} %get-tuple-element.24.refs_0_), channel_id=1, source_target_pairs={{0,1},{1,0},{2,3},{3,2},{4,5},{5,4},{6,7},{7,6},{8,9},{9,8},{10,11... | collective-permute-start | bytes 786440 | tf_op jit(solution)/shard_map/ppermute | solution.py:662
  12.8 5.9 %collective-permute-start.14 = (bf16[2,4,2,4,1024]{4,3,2,1,0:T(4,128)(2,1)S(1)}, bf16[2,4,2,4,1024]{4,3,2,1,0:T(4,128)(2,1)S(1)}, u32[]{:S(2)}, u32[]{:S(2)}) collective-permute-start(bf16[2,4,2,4,1024]{4,3,2,1,0:T(4,128)(2,1)S(1)} %copy-done.2), channel_id=1, source_target_pairs={{0,4},{2,6},{4,0},{6,2},{8,12},{10,14},{12,8},{14,10},{1,5},{3,7},... | collective-permute-start | bytes 393224 | tf_op jit(solution)/shard_map/ppermute | solution.py:659
  14.5 7.8 %collective-permute-start.12 = (bf16[2,4,2,4,1024]{4,3,2,1,0:T(4,128)(2,1)S(1)}, bf16[2,4,2,4,1024]{4,3,2,1,0:T(4,128)(2,1)S(1)}, u32[]{:S(2)}, u32[]{:S(2)}) collective-permute-start(bf16[2,4,2,4,1024]{4,3,2,1,0:T(4,128)(2,1)S(1)} %copy-done.2), channel_id=1, source_target_pairs={{0,12},{2,14},{4,8},{6,10},{8,4},{10,6},{12,0},{14,2},{1,13},{3,15... | collective-permute-start | bytes 393224 | tf_op jit(solution)/shard_map/ppermute | solution.py:659
  15.2 5.5 %collective-permute-start.3 = (bf16[240,128]{1,0:T(8,128)(2,1)S(1)}, bf16[240,128]{1,0:T(8,128)(2,1)S(1)}, u32[]{:S(2)}, u32[]{:S(2)}) collective-permute-start(bf16[240,128]{1,0:T(8,128)(2,1)S(1)} %get-tuple-element.29), channel_id=1, source_target_pairs={{0,0},{1,9},{2,2},{3,11},{4,4},{5,13},{6,6},{7,15},{8,8},{9,1},{10... | collective-permute-start | bytes 184328 | tf_op jit(solution)/shard_map/ppermute | solution.py:686
  15.9 8.7 %collective-permute-start.4 = (bf16[240,128]{1,0:T(8,128)(2,1)S(1)}, bf16[240,128]{1,0:T(8,128)(2,1)S(1)}, u32[]{:S(2)}, u32[]{:S(2)}) collective-permute-start(bf16[240,128]{1,0:T(8,128)(2,1)S(1)} %get-tuple-element.30), channel_id=1, source_target_pairs={{0,2},{1,11},{2,0},{3,9},{4,6},{5,15},{6,4},{7,13},{8,10},{9,3},{1... | collective-permute-start | bytes 184328 | tf_op jit(solution)/shard_map/ppermute | solution.py:686
  17.1 7.7 %collective-permute-start.5 = (bf16[240,128]{1,0:T(8,128)(2,1)S(1)}, bf16[240,128]{1,0:T(8,128)(2,1)S(1)}, u32[]{:S(2)}, u32[]{:S(2)}) collective-permute-start(bf16[240,128]{1,0:T(8,128)(2,1)S(1)} %get-tuple-element.31), channel_id=1, source_target_pairs={{0,4},{1,13},{2,6},{3,15},{4,0},{5,9},{6,2},{7,11},{8,12},{9,5},{1... | collective-permute-start | bytes 184328 | tf_op jit(solution)/shard_map/ppermute | solution.py:686
  18.7 8.7 %collective-permute-start.6 = (bf16[240,128]{1,0:T(8,128)(2,1)S(1)}, bf16[240,128]{1,0:T(8,128)(2,1)S(1)}, u32[]{:S(2)}, u32[]{:S(2)}) collective-permute-start(bf16[240,128]{1,0:T(8,128)(2,1)S(1)} %get-tuple-element.32), channel_id=1, source_target_pairs={{0,6},{1,15},{2,4},{3,13},{4,2},{5,11},{6,0},{7,9},{8,14},{9,7},{1... | collective-permute-start | bytes 184328 | tf_op jit(solution)/shard_map/ppermute | solution.py:686
  20.7 10.3 %collective-permute-start.15 = (bf16[2,4,2,4,1024]{4,3,2,1,0:T(4,128)(2,1)S(1)}, bf16[2,4,2,4,1024]{4,3,2,1,0:T(4,128)(2,1)S(1)}, u32[]{:S(2)}, u32[]{:S(2)}) collective-permute-start(bf16[2,4,2,4,1024]{4,3,2,1,0:T(4,128)(2,1)S(1)} %collective-permute-done.14.refs_10_), channel_id=1, source_target_pairs={{0,2},{2,0},{4,6},{6,4},{8,10},{10,8},{12,14},{14,12},{1,3},{3,1},... | collective-permute-start | bytes 393224 | tf_op jit(solution)/shard_map/ppermute | solution.py:659
  22.3 5.2 %collective-permute-start.7 = (bf16[240,128]{1,0:T(8,128)(2,1)S(1)}, bf16[240,128]{1,0:T(8,128)(2,1)S(1)}, u32[]{:S(2)}, u32[]{:S(2)}) collective-permute-start(bf16[240,128]{1,0:T(8,128)(2,1)S(1)} %collective-permute-done.3.refs_0_), channel_id=1, source_target_pairs={{0,1},{1,0},{2,3},{3,2},{4,5},{5,4},{6,7},{7,6},{8,9},{9,8},{10,11... | collective-permute-start | bytes 184328 | tf_op jit(solution)/shard_map/ppermute | solution.py:662
  24.6 5.1 %collective-permute-start.8 = (bf16[240,128]{1,0:T(8,128)(2,1)S(1)}, bf16[240,128]{1,0:T(8,128)(2,1)S(1)}, u32[]{:S(2)}, u32[]{:S(2)}) collective-permute-start(bf16[240,128]{1,0:T(8,128)(2,1)S(1)} %collective-permute-done.4.refs_1_), channel_id=1, source_target_pairs={{0,1},{1,0},{2,3},{3,2},{4,5},{5,4},{6,7},{7,6},{8,9},{9,8},{10,11... | collective-permute-start | bytes 184328 | tf_op jit(solution)/shard_map/ppermute | solution.py:662
  24.7 11.2 %collective-permute-start.11 = (bf16[2,4,2,4,1024]{4,3,2,1,0:T(4,128)(2,1)S(1)}, bf16[2,4,2,4,1024]{4,3,2,1,0:T(4,128)(2,1)S(1)}, u32[]{:S(2)}, u32[]{:S(2)}) collective-permute-start(bf16[2,4,2,4,1024]{4,3,2,1,0:T(4,128)(2,1)S(1)} %collective-permute-done.1.refs_8_), channel_id=1, source_target_pairs={{0,2},{2,0},{4,6},{6,4},{8,10},{10,8},{12,14},{14,12},{1,3},{3,1},... | collective-permute-start | bytes 393224 | tf_op jit(solution)/shard_map/ppermute | solution.py:659
  27.4 8.5 %collective-permute-start.13 = (bf16[2,4,2,4,1024]{4,3,2,1,0:T(4,128)(2,1)S(1)}, bf16[2,4,2,4,1024]{4,3,2,1,0:T(4,128)(2,1)S(1)}, u32[]{:S(2)}, u32[]{:S(2)}) collective-permute-start(bf16[2,4,2,4,1024]{4,3,2,1,0:T(4,128)(2,1)S(1)} %collective-permute-done.12.refs_10_), channel_id=1, source_target_pairs={{0,2},{2,0},{4,6},{6,4},{8,10},{10,8},{12,14},{14,12},{1,3},{3,1},... | collective-permute-start | bytes 393224 | tf_op jit(solution)/shard_map/ppermute | solution.py:659
  27.5 3.2 %collective-permute-start.9 = (bf16[240,128]{1,0:T(8,128)(2,1)S(1)}, bf16[240,128]{1,0:T(8,128)(2,1)S(1)}, u32[]{:S(2)}, u32[]{:S(2)}) collective-permute-start(bf16[240,128]{1,0:T(8,128)(2,1)S(1)} %collective-permute-done.5.refs_2_), channel_id=1, source_target_pairs={{0,1},{1,0},{2,3},{3,2},{4,5},{5,4},{6,7},{7,6},{8,9},{9,8},{10,11... | collective-permute-start | bytes 184328 | tf_op jit(solution)/shard_map/ppermute | solution.py:662
  29.8 1.2 %collective-permute-start.10 = (bf16[240,128]{1,0:T(8,128)(2,1)S(1)}, bf16[240,128]{1,0:T(8,128)(2,1)S(1)}, u32[]{:S(2)}, u32[]{:S(2)}) collective-permute-start(bf16[240,128]{1,0:T(8,128)(2,1)S(1)} %collective-permute-done.6.refs_3_), channel_id=1, source_target_pairs={{0,1},{1,0},{2,3},{3,2},{4,5},{5,4},{6,7},{7,6},{8,9},{9,8},{10,11... | collective-permute-start | bytes 184328 | tf_op jit(solution)/shard_map/ppermute | solution.py:662

commit v5 on v4

--- a/solution.py
+++ b/solution.py
@@ -614,7 +614,7 @@
             pltpu.VMEM((count * coef_rows, 4 * TAPS), BF16),
             pltpu.VMEM((count * cov_rows, tones), F32),
             pltpu.VMEM((cov_rows * blocks, 128), F32),
-            pltpu.VMEM((count, aps * antennas * 2 * symbols * blocks, 128), F32),
+            pltpu.VMEM((count, (aps * antennas * 2 * symbols + CU) * blocks, 128), F32),
             pltpu.VMEM((count, aps * antennas * 3 * symbols * blocks, 128), F32),
             pltpu.VMEM((count * coef_rows, 2 * chunk), F32),
             pltpu.VMEM((count, aps, ROWS, 128), F32),

time: 42.4 us -> 42.4 us (level)
  no operation moved by 1% of the time
where the time goes in v5:
time: 42.4 us; the launch traced here: 42.1 us
  starting transfers between devices  21.4 us (50%)
  Pallas kernels  15.2 us (36%)
  other arithmetic  2.01 us (5%)
  waiting for transfers between devices  1.87 us (4%)
  local copies, waits for them, and re-layouts  1.49 us (4%)
    ppermute x7, starting transfers between devices, swap_ap(): return lax.ppermute(value, 'ap', [(i, i ^ v) for i in range(devices)])  11.7 us
    pallas_call x2, Pallas kernels, owner_estimates(): pl.pallas_call(functools.partial(estimate_kernel, shape, chunk, group), i...  11 us
    ppermute x5, starting transfers between devices, swap_sc(): return lax.ppermute(value, 'sc', [(c, c ^ h) for c in range(shards)])  4.87 us
    ppermute x4, starting transfers between devices, local(): own = [lax.ppermute(blocks[j], ('ap', 'sc'), pairs(j)) for j in range(per)]  4.83 us
    pallas_call x1, Pallas kernels, delay_coefficients(): pl.pallas_call(functools.partial(coefficient_kernel, shape, clusters), in...  3.63 us
    ppermute x5, waiting for transfers between devices, swap_sc(): return lax.ppermute(value, 'sc', [(c, c ^ h) for c in range(shards)])  1.19 us
  transfers between devices with their start and end apart: 16, of which 3 were waited for; matrix products, arithmetic and copies ran while one was open for 8% of the time, Pallas kernels for 21%

profile of v5, /device:TPU:0, one launch (start us, length us, event | category | flops | bytes accessed | tf_op | source)
XLA Modules:
  0.0 42.1 jit_solution(3533643373757074312)
XLA Ops:
  0.0 4.0 %collective-permute-start.1 = (bf16[2,4,2,4,1024]{4,3,2,1,0:T(4,128)(2,1)}, bf16[2,4,2,4,1024]{4,3,2,1,0:T(4,128)(2,1)S(1)}, u32[]{:S(2)}, u32[]{:S(2)}) collective-permute-start(bf16[2,4,2,4,1024]{4,3,2,1,0:T(4,128)(2,1)} %refs_8_.1), channel_id=1, source_target_pairs={{0,8},{2,10},{4,12},{6,14},{8,0},{10,2},{12,4},{14,6},{1,9},{3,11}... | collective-permute-start | bytes 393224 | tf_op jit(solution)/shard_map/ppermute | solution.py:659
  4.0 1.5 %collective-permute-start = (bf16[2,4,2,4,1024]{4,3,2,1,0:T(4,128)(2,1)}, bf16[2,4,2,4,1024]{4,3,2,1,0:T(4,128)(2,1)S(1)}, u32[]{:S(2)}, u32[]{:S(2)}) collective-permute-start(bf16[2,4,2,4,1024]{4,3,2,1,0:T(4,128)(2,1)} %refs_8_.1), channel_id=1, source_target_pairs={{0,2},{2,0},{4,6},{6,4},{8,10},{10,8},{12,14},{14,12},{1,3},{3,1},... | collective-permute-start | bytes 393224 | tf_op jit(solution)/shard_map/ppermute | solution.py:659
  5.6 0.7 %convert_bitcast_fusion.1 = f32[1,128]{1,0:T(1,128)S(1)} fusion(s32[128]{0:T(128)} %param.18), kind=kLoop, calls=%fused_computation.1 | loop fusion | flops 128 | bytes 1024 | tf_op jit(solution)/shard_map/broadcast_in_dim | solution.py:125
  6.2 0.7 %convert_bitcast_fusion = f32[1,16]{1,0:T(1,128)S(1)} fusion(s32[16,1]{0,1:T(1,128)} %param.20), kind=kLoop, calls=%fused_computation | loop fusion | flops 16 | bytes 128 | tf_op jit(solution)/shard_map/reshape | solution.py:126
  6.9 0.7 %pad.14 = f32[1,128]{1,0:T(1,128)S(1)} pad(f32[1,2]{1,0:T(1,128)} %bitcast.7, f32[]{:T(128)} %constant.8.clone.1), padding=0_0x0_126 | pad | bytes 524 | tf_op jit(solution)/shard_map/jit(_pad)/pad | solution.py:128
  7.5 0.7 %convert_element_type.16 = f32[16,16]{1,0:T(8,128)S(1)} convert(s32[16,16]{1,0:T(8,128)} %param.19) | non-fusion elementwise | flops 256 | bytes 2048 | tf_op jit(solution)/shard_map/convert_element_type | solution.py:125
  8.2 0.8 %concatenate.3.refs_2_ = f32[22,128]{1,0:T(8,128)S(1)} concatenate(f32[1,128]{1,0:T(1,128)} %bitcast.6, f32[2,128]{1,0:T(2,128)} %param.17, f32[1,128]{1,0:T(1,128)S(1)} %convert_bitcast_fusion.1, f32[16,128]{1,0:T(8,128)S(1)} %pad.12, f32[1,128]{1,0:T(1,128)S(1)} %pad.13, f32[1,128]{1,0:T(1,128)S(1)} %pad.14), dimensions={0} | concatenate | bytes 22528 | tf_op jit(solution)/shard_map/concatenate | solution.py:128
  9.1 0.0 copy-start
  9.1 0.0 copy-start.1
  9.1 3.6 %delay_coefficients.1 = (bf16[1024,128]{1,0:T(8,128)(2,1)S(1)}, bf16[256,256]{1,0:T(8,128)(2,1)S(1)}, bf16[64,128]{1,0:T(8,128)(2,1)S(1)}, bf16[64,128]{1,0:T(8,...) custom-call(bf16[2,4,2,128,1024]{4,3,2,1,0:T(8,128)(2,1)} %refs_0_.1, ...), custom_call_target="tpu_custom_call" | custom-call | flops 536870912 | bytes 4194304 | tf_op jit(solution)/shard_map/delay_coefficients/pallas_call | solution.py:242
  12.7 0.0 collective-permute-done.1.refs_8_
  12.7 0.1 collective-permute-start.2
  12.8 1.6 %collective-permute-start.14 = (bf16[2,4,2,4,1024]{4,3,2,1,0:T(4,128)(2,1)S(1)}, bf16[2,4,2,4,1024]{4,3,2,1,0:T(4,128)(2,1)S(1)}, u32[]{:S(2)}, u32[]{:S(2)}) collective-permute-start(bf16[2,4,2,4,1024]{4,3,2,1,0:T(4,128)(2,1)S(1)} %copy-done.2), channel_id=1, source_target_pairs={{0,4},{2,6},{4,0},{6,2},{8,12},{10,14},{12,8},{14,10},{1,5},{3,7},... | collective-permute-start | bytes 393224 | tf_op jit(solution)/shard_map/ppermute | solution.py:659
  14.5 0.2 collective-permute-start.12
  14.7 0.5 %owner_payloads.1 = (bf16[240,128]{1,0:T(8,128)(2,1)S(1)}, bf16[240,128]{1,0:T(8,128)(2,1)S(1)}, bf16[240,128]{1,0:T(8,128)(2,1)S(1)}, bf16[240,128]{1,0:T(8,128)(2,1)S(1)}) custom-call(bf16[1024,128]{1,0:T(8,128)(2,1)S(1)} %get-tuple-element.24.refs_0_, bf16[1024,128]{1,0:T(8,128)(2,1)S(1)} %collective-permute-done.2.refs_1_, ...), custom_call_target="tpu_custom_call" | custom-call | flops 134217728 | bytes 2097152 | tf_op jit(solution)/shard_map/owner_payloads/pallas_call | solution.py:337
  15.2 0.7 %collective-permute-start.3 = (bf16[240,128]{1,0:T(8,128)(2,1)S(1)}, bf16[240,128]{1,0:T(8,128)(2,1)S(1)}, u32[]{:S(2)}, u32[]{:S(2)}) collective-permute-start(bf16[240,128]{1,0:T(8,128)(2,1)S(1)} %get-tuple-element.29), channel_id=1, source_target_pairs={{0,0},{1,9},{2,2},{3,11},{4,4},{5,13},{6,6},{7,15},{8,8},{9,1},{10... | collective-permute-start | bytes 184328 | tf_op jit(solution)/shard_map/ppermute | solution.py:686
  15.9 1.2 %collective-permute-start.4 = (bf16[240,128]{1,0:T(8,128)(2,1)S(1)}, bf16[240,128]{1,0:T(8,128)(2,1)S(1)}, u32[]{:S(2)}, u32[]{:S(2)}) collective-permute-start(bf16[240,128]{1,0:T(8,128)(2,1)S(1)} %get-tuple-element.30), channel_id=1, source_target_pairs={{0,2},{1,11},{2,0},{3,9},{4,6},{5,15},{6,4},{7,13},{8,10},{9,3},{1... | collective-permute-start | bytes 184328 | tf_op jit(solution)/shard_map/ppermute | solution.py:686
  17.1 1.0 %collective-permute-start.5 = (bf16[240,128]{1,0:T(8,128)(2,1)S(1)}, bf16[240,128]{1,0:T(8,128)(2,1)S(1)}, u32[]{:S(2)}, u32[]{:S(2)}) collective-permute-start(bf16[240,128]{1,0:T(8,128)(2,1)S(1)} %get-tuple-element.31), channel_id=1, source_target_pairs={{0,4},{1,13},{2,6},{3,15},{4,0},{5,9},{6,2},{7,11},{8,12},{9,5},{1... | collective-permute-start | bytes 184328 | tf_op jit(solution)/shard_map/ppermute | solution.py:686
  18.1 0.6 %collective-permute-done.14.refs_10_ = bf16[2,4,2,4,1024]{4,3,2,1,0:T(4,128)(2,1)S(1)} collective-permute-done((bf16[2,4,2,4,1024]{4,3,2,1,0:T(4,128)(2,1)S(1)}, bf16[2,4,2,4,1024]{4,3,2,1,0:T(4,128)(2,1)S(1)}, u32[]{:S(2)}, u32[]{:S(2)}) %collective-permute-start.14) | collective-permute-done | bytes 131104 | tf_op jit(solution)/shard_map/ppermute | solution.py:659
  18.7 2.0 %collective-permute-start.6 = (bf16[240,128]{1,0:T(8,128)(2,1)S(1)}, bf16[240,128]{1,0:T(8,128)(2,1)S(1)}, u32[]{:S(2)}, u32[]{:S(2)}) collective-permute-start(bf16[240,128]{1,0:T(8,128)(2,1)S(1)} %get-tuple-element.32), channel_id=1, source_target_pairs={{0,6},{1,15},{2,4},{3,13},{4,2},{5,11},{6,0},{7,9},{8,14},{9,7},{1... | collective-permute-start | bytes 184328 | tf_op jit(solution)/shard_map/ppermute | solution.py:686
  20.7 1.5 %collective-permute-start.15 = (bf16[2,4,2,4,1024]{4,3,2,1,0:T(4,128)(2,1)S(1)}, bf16[2,4,2,4,1024]{4,3,2,1,0:T(4,128)(2,1)S(1)}, u32[]{:S(2)}, u32[]{:S(2)}) collective-permute-start(bf16[2,4,2,4,1024]{4,3,2,1,0:T(4,128)(2,1)S(1)} %collective-permute-done.14.refs_10_), channel_id=1, source_target_pairs={{0,2},{2,0},{4,6},{6,4},{8,10},{10,8},{12,14},{14,12},{1,3},{3,1},... | collective-permute-start | bytes 393224 | tf_op jit(solution)/shard_map/ppermute | solution.py:659
  22.2 0.0 collective-permute-done.12.refs_10_
  22.3 2.4 %collective-permute-start.7 = (bf16[240,128]{1,0:T(8,128)(2,1)S(1)}, bf16[240,128]{1,0:T(8,128)(2,1)S(1)}, u32[]{:S(2)}, u32[]{:S(2)}) collective-permute-start(bf16[240,128]{1,0:T(8,128)(2,1)S(1)} %collective-permute-done.3.refs_0_), channel_id=1, source_target_pairs={{0,1},{1,0},{2,3},{3,2},{4,5},{5,4},{6,7},{7,6},{8,9},{9,8},{10,11... | collective-permute-start | bytes 184328 | tf_op jit(solution)/shard_map/ppermute | solution.py:662
  24.6 0.1 collective-permute-start.8
  24.7 2.7 %collective-permute-start.11 = (bf16[2,4,2,4,1024]{4,3,2,1,0:T(4,128)(2,1)S(1)}, bf16[2,4,2,4,1024]{4,3,2,1,0:T(4,128)(2,1)S(1)}, u32[]{:S(2)}, u32[]{:S(2)}) collective-permute-start(bf16[2,4,2,4,1024]{4,3,2,1,0:T(4,128)(2,1)S(1)} %collective-permute-done.1.refs_8_), channel_id=1, source_target_pairs={{0,2},{2,0},{4,6},{6,4},{8,10},{10,8},{12,14},{14,12},{1,3},{3,1},... | collective-permute-start | bytes 393224 | tf_op jit(solution)/shard_map/ppermute | solution.py:659
  27.4 0.1 collective-permute-start.13
  27.5 2.3 %collective-permute-start.9 = (bf16[240,128]{1,0:T(8,128)(2,1)S(1)}, bf16[240,128]{1,0:T(8,128)(2,1)S(1)}, u32[]{:S(2)}, u32[]{:S(2)}) collective-permute-start(bf16[240,128]{1,0:T(8,128)(2,1)S(1)} %collective-permute-done.5.refs_2_), channel_id=1, source_target_pairs={{0,1},{1,0},{2,3},{3,2},{4,5},{5,4},{6,7},{7,6},{8,9},{9,8},{10,11... | collective-permute-start | bytes 184328 | tf_op jit(solution)/shard_map/ppermute | solution.py:662
  29.8 0.1 collective-permute-start.10
  29.8 0.8 %collective-permute-done.9.refs_6_ = bf16[240,128]{1,0:T(8,128)(2,1)S(1)} collective-permute-done((bf16[240,128]{1,0:T(8,128)(2,1)S(1)}, bf16[240,128]{1,0:T(8,128)(2,1)S(1)}, u32[]{:S(2)}, u32[]{:S(2)}) %collective-permute-start.9) | collective-permute-done | bytes 61472 | tf_op jit(solution)/shard_map/ppermute | solution.py:662
  30.7 0.4 collective-permute-done.10.refs_7_
  31.0 4.9 %owner_estimates.2 = (f32[4,8,8,1024]{3,2,1,0:T(8,128)S(1)}, f32[4,8,128]{2,1,0:T(8,128)S(1)}) custom-call(s32[2,8]{1,0:T(2,128)S(1)} %get-tuple-element.22.slots, bf16[240,128]{1,0:T(8,128)(2,1)S(1)} %collective-permute-done.3.refs_0_, bf16[240,128]{1,0:T(8,128)(2,1)S(1)} %collective-permute-done.4.refs_1_, ...), custom_call_target="tpu_custom_call" | custom-call | flops 536870912 | bytes 8388608 | tf_op jit(solution)/shard_map/owner_estimates/pallas_call | solution.py:608
  35.9 6.2 %owner_estimates.3 = f32[4,8,4,2,1024]{4,3,2,1,0:T(2,128)} custom-call(s32[2,8]{1,0:T(2,128)S(1)} %get-tuple-element.22.slots, bf16[240,128]{1,0:T(8,128)(2,1)S(1)} %collective-permute-done.3.refs_0_, bf16[240,128]{1,0:T(8,128)(2,1)S(1)} %collective-permute-done.4.refs_1_, bf16[240,128]{1,0:T(8,128)(2,1)S(1)} %collective-permute-done.5.refs_2_, ...), custom_call_target="tpu_custom_call" | custom-call | flops 536870912 | bytes 8388608 | tf_op jit(solution)/shard_map/owner_estimates/pallas_call | solution.py:608
  (17 shorter events, 0.0 us)
Async XLA Ops:
  0.0 12.7 %collective-permute-start.1 = (bf16[2,4,2,4,1024]{4,3,2,1,0:T(4,128)(2,1)}, bf16[2,4,2,4,1024]{4,3,2,1,0:T(4,128)(2,1)S(1)}, u32[]{:S(2)}, u32[]{:S(2)}) collective-permute-start(bf16[2,4,2,4,1024]{4,3,2,1,0:T(4,128)(2,1)} %refs_8_.1), channel_id=1, source_target_pairs={{0,8},{2,10},{4,12},{6,14},{8,0},{10,2},{12,4},{14,6},{1,9},{3,11}... | collective-permute-start | bytes 393224 | tf_op jit(solution)/shard_map/ppermute | solution.py:659
  4.0 8.7 %collective-permute-start = (bf16[2,4,2,4,1024]{4,3,2,1,0:T(4,128)(2,1)}, bf16[2,4,2,4,1024]{4,3,2,1,0:T(4,128)(2,1)S(1)}, u32[]{:S(2)}, u32[]{:S(2)}) collective-permute-start(bf16[2,4,2,4,1024]{4,3,2,1,0:T(4,128)(2,1)} %refs_8_.1), channel_id=1, source_target_pairs={{0,2},{2,0},{4,6},{6,4},{8,10},{10,8},{12,14},{14,12},{1,3},{3,1},... | collective-permute-start | bytes 393224 | tf_op jit(solution)/shard_map/ppermute | solution.py:659
  9.0 3.8 %copy-start.2 = (bf16[2,4,2,4,1024]{4,3,2,1,0:T(4,128)(2,1)S(1)}, bf16[2,4,2,4,1024]{4,3,2,1,0:T(4,128)(2,1)}, u32[]{:S(2)}) copy-start(bf16[2,4,2,4,1024]{4,3,2,1,0:T(4,128)(2,1)} %refs_8_.1) | copy-start | bytes 393220
  9.1 22.0 %copy-start = (bf16[2,256,2048]{2,1,0:T(8,128)(2,1)S(1)}, bf16[2,256,2048]{2,1,0:T(8,128)(2,1)}, u32[]{:S(2)}) copy-start(bf16[2,256,2048]{2,1,0:T(8,128)(2,1)} %constant.11.clone.refs_13_) | copy-start | bytes 6291460
  9.1 22.0 %copy-start.1 = (bf16[2,384,1024]{2,1,0:T(8,128)(2,1)S(1)}, bf16[2,384,1024]{2,1,0:T(8,128)(2,1)}, u32[]{:S(2)}) copy-start(bf16[2,384,1024]{2,1,0:T(8,128)(2,1)} %constant.10.clone.refs_12_) | copy-start | bytes 4718596
  12.7 2.0 %collective-permute-start.2 = (bf16[1024,128]{1,0:T(8,128)(2,1)S(1)}, bf16[1024,128]{1,0:T(8,128)(2,1)S(1)}, u32[]{:S(2)}, u32[]{:S(2)}) collective-permute-start(bf16[1024,128]{1,0:T(8,128)(2,1)S(1)} %get-tuple-element.24.refs_0_), channel_id=1, source_target_pairs={{0,1},{1,0},{2,3},{3,2},{4,5},{5,4},{6,7},{7,6},{8,9},{9,8},{10,11... | collective-permute-start | bytes 786440 | tf_op jit(solution)/shard_map/ppermute | solution.py:662
  12.8 5.9 %collective-permute-start.14 = (bf16[2,4,2,4,1024]{4,3,2,1,0:T(4,128)(2,1)S(1)}, bf16[2,4,2,4,1024]{4,3,2,1,0:T(4,128)(2,1)S(1)}, u32[]{:S(2)}, u32[]{:S(2)}) collective-permute-start(bf16[2,4,2,4,1024]{4,3,2,1,0:T(4,128)(2,1)S(1)} %copy-done.2), channel_id=1, source_target_pairs={{0,4},{2,6},{4,0},{6,2},{8,12},{10,14},{12,8},{14,10},{1,5},{3,7},... | collective-permute-start | bytes 393224 | tf_op jit(solution)/shard_map/ppermute | solution.py:659
  14.5 7.8 %collective-permute-start.12 = (bf16[2,4,2,4,1024]{4,3,2,1,0:T(4,128)(2,1)S(1)}, bf16[2,4,2,4,1024]{4,3,2,1,0:T(4,128)(2,1)S(1)}, u32[]{:S(2)}, u32[]{:S(2)}) collective-permute-start(bf16[2,4,2,4,1024]{4,3,2,1,0:T(4,128)(2,1)S(1)} %copy-done.2), channel_id=1, source_target_pairs={{0,12},{2,14},{4,8},{6,10},{8,4},{10,6},{12,0},{14,2},{1,13},{3,15... | collective-permute-start | bytes 393224 | tf_op jit(solution)/shard_map/ppermute | solution.py:659
  15.2 5.5 %collective-permute-start.3 = (bf16[240,128]{1,0:T(8,128)(2,1)S(1)}, bf16[240,128]{1,0:T(8,128)(2,1)S(1)}, u32[]{:S(2)}, u32[]{:S(2)}) collective-permute-start(bf16[240,128]{1,0:T(8,128)(2,1)S(1)} %get-tuple-element.29), channel_id=1, source_target_pairs={{0,0},{1,9},{2,2},{3,11},{4,4},{5,13},{6,6},{7,15},{8,8},{9,1},{10... | collective-permute-start | bytes 184328 | tf_op jit(solution)/shard_map/ppermute | solution.py:686
  15.9 8.7 %collective-permute-start.4 = (bf16[240,128]{1,0:T(8,128)(2,1)S(1)}, bf16[240,128]{1,0:T(8,128)(2,1)S(1)}, u32[]{:S(2)}, u32[]{:S(2)}) collective-permute-start(bf16[240,128]{1,0:T(8,128)(2,1)S(1)} %get-tuple-element.30), channel_id=1, source_target_pairs={{0,2},{1,11},{2,0},{3,9},{4,6},{5,15},{6,4},{7,13},{8,10},{9,3},{1... | collective-permute-start | bytes 184328 | tf_op jit(solution)/shard_map/ppermute | solution.py:686
  17.1 7.7 %collective-permute-start.5 = (bf16[240,128]{1,0:T(8,128)(2,1)S(1)}, bf16[240,128]{1,0:T(8,128)(2,1)S(1)}, u32[]{:S(2)}, u32[]{:S(2)}) collective-permute-start(bf16[240,128]{1,0:T(8,128)(2,1)S(1)} %get-tuple-element.31), channel_id=1, source_target_pairs={{0,4},{1,13},{2,6},{3,15},{4,0},{5,9},{6,2},{7,11},{8,12},{9,5},{1... | collective-permute-start | bytes 184328 | tf_op jit(solution)/shard_map/ppermute | solution.py:686
  18.7 8.7 %collective-permute-start.6 = (bf16[240,128]{1,0:T(8,128)(2,1)S(1)}, bf16[240,128]{1,0:T(8,128)(2,1)S(1)}, u32[]{:S(2)}, u32[]{:S(2)}) collective-permute-start(bf16[240,128]{1,0:T(8,128)(2,1)S(1)} %get-tuple-element.32), channel_id=1, source_target_pairs={{0,6},{1,15},{2,4},{3,13},{4,2},{5,11},{6,0},{7,9},{8,14},{9,7},{1... | collective-permute-start | bytes 184328 | tf_op jit(solution)/shard_map/ppermute | solution.py:686
  20.7 10.3 %collective-permute-start.15 = (bf16[2,4,2,4,1024]{4,3,2,1,0:T(4,128)(2,1)S(1)}, bf16[2,4,2,4,1024]{4,3,2,1,0:T(4,128)(2,1)S(1)}, u32[]{:S(2)}, u32[]{:S(2)}) collective-permute-start(bf16[2,4,2,4,1024]{4,3,2,1,0:T(4,128)(2,1)S(1)} %collective-permute-done.14.refs_10_), channel_id=1, source_target_pairs={{0,2},{2,0},{4,6},{6,4},{8,10},{10,8},{12,14},{14,12},{1,3},{3,1},... | collective-permute-start | bytes 393224 | tf_op jit(solution)/shard_map/ppermute | solution.py:659
  22.3 5.2 %collective-permute-start.7 = (bf16[240,128]{1,0:T(8,128)(2,1)S(1)}, bf16[240,128]{1,0:T(8,128)(2,1)S(1)}, u32[]{:S(2)}, u32[]{:S(2)}) collective-permute-start(bf16[240,128]{1,0:T(8,128)(2,1)S(1)} %collective-permute-done.3.refs_0_), channel_id=1, source_target_pairs={{0,1},{1,0},{2,3},{3,2},{4,5},{5,4},{6,7},{7,6},{8,9},{9,8},{10,11... | collective-permute-start | bytes 184328 | tf_op jit(solution)/shard_map/ppermute | solution.py:662
  24.6 5.1 %collective-permute-start.8 = (bf16[240,128]{1,0:T(8,128)(2,1)S(1)}, bf16[240,128]{1,0:T(8,128)(2,1)S(1)}, u32[]{:S(2)}, u32[]{:S(2)}) collective-permute-start(bf16[240,128]{1,0:T(8,128)(2,1)S(1)} %collective-permute-done.4.refs_1_), channel_id=1, source_target_pairs={{0,1},{1,0},{2,3},{3,2},{4,5},{5,4},{6,7},{7,6},{8,9},{9,8},{10,11... | collective-permute-start | bytes 184328 | tf_op jit(solution)/shard_map/ppermute | solution.py:662
  24.7 11.2 %collective-permute-start.11 = (bf16[2,4,2,4,1024]{4,3,2,1,0:T(4,128)(2,1)S(1)}, bf16[2,4,2,4,1024]{4,3,2,1,0:T(4,128)(2,1)S(1)}, u32[]{:S(2)}, u32[]{:S(2)}) collective-permute-start(bf16[2,4,2,4,1024]{4,3,2,1,0:T(4,128)(2,1)S(1)} %collective-permute-done.1.refs_8_), channel_id=1, source_target_pairs={{0,2},{2,0},{4,6},{6,4},{8,10},{10,8},{12,14},{14,12},{1,3},{3,1},... | collective-permute-start | bytes 393224 | tf_op jit(solution)/shard_map/ppermute | solution.py:659
  27.4 8.5 %collective-permute-start.13 = (bf16[2,4,2,4,1024]{4,3,2,1,0:T(4,128)(2,1)S(1)}, bf16[2,4,2,4,1024]{4,3,2,1,0:T(4,128)(2,1)S(1)}, u32[]{:S(2)}, u32[]{:S(2)}) collective-permute-start(bf16[2,4,2,4,1024]{4,3,2,1,0:T(4,128)(2,1)S(1)} %collective-permute-done.12.refs_10_), channel_id=1, source_target_pairs={{0,2},{2,0},{4,6},{6,4},{8,10},{10,8},{12,14},{14,12},{1,3},{3,1},... | collective-permute-start | bytes 393224 | tf_op jit(solution)/shard_map/ppermute | solution.py:659
  27.5 3.2 %collective-permute-start.9 = (bf16[240,128]{1,0:T(8,128)(2,1)S(1)}, bf16[240,128]{1,0:T(8,128)(2,1)S(1)}, u32[]{:S(2)}, u32[]{:S(2)}) collective-permute-start(bf16[240,128]{1,0:T(8,128)(2,1)S(1)} %collective-permute-done.5.refs_2_), channel_id=1, source_target_pairs={{0,1},{1,0},{2,3},{3,2},{4,5},{5,4},{6,7},{7,6},{8,9},{9,8},{10,11... | collective-permute-start | bytes 184328 | tf_op jit(solution)/shard_map/ppermute | solution.py:662
  29.8 1.2 %collective-permute-start.10 = (bf16[240,128]{1,0:T(8,128)(2,1)S(1)}, bf16[240,128]{1,0:T(8,128)(2,1)S(1)}, u32[]{:S(2)}, u32[]{:S(2)}) collective-permute-start(bf16[240,128]{1,0:T(8,128)(2,1)S(1)} %collective-permute-done.6.refs_3_), channel_id=1, source_target_pairs={{0,1},{1,0},{2,3},{3,2},{4,5},{5,4},{6,7},{7,6},{8,9},{9,8},{10,11... | collective-permute-start | bytes 184328 | tf_op jit(solution)/shard_map/ppermute | solution.py:662
